TPU v7x, 32 devices: a whole 2x2x4 slice. The times are simulated.
32 devices in a mesh: groups: 2 (over x), ctx: 16 (over z, y, core).
Axes of the slice: x: 2, y: 2, z: 4, core: 2. Of those that a mesh axis runs over, the one named last changes fastest.
Arguments:
- queries: bfloat16 [2048, 2048], P('ctx', 'groups'), parts along dimension 1, may hold values from -25 to 25
- keys: bfloat16 [2048, 256], P('ctx', 'groups'), parts along dimension 1, may hold values from -6 to 6
- values: bfloat16 [2048, 256], P('ctx', 'groups'), parts along dimension 1, may hold values from -6 to 6
- d_out: bfloat16 [2048, 2048], P('ctx', 'groups'), parts along dimension 1, may hold values from -96 to 96
- mixer_input: bfloat16 [2048, 4096], P('ctx', 'groups'), parts along dimension 1, may hold values from -54 to 54
- gate_input: bfloat16 [2048, 4096], P('ctx', 'groups'), parts along dimension 1, may hold values from -6 to 6
- state_write: bfloat16 [2048, 512], P('ctx', 'groups'), parts along dimension 1, may hold values from -0.375 to 0.375
- state_read: bfloat16 [2048, 512], P('ctx', 'groups'), parts along dimension 1, may hold values from -0.375 to 0.375
- log_decay: float32 [2048, 64], P('ctx', 'groups'), parts along dimension 1, may hold values from -1 to 0
- norm_gain: float32 [4096], P('groups'), parts along dimension 0, may hold values from 0.25 to 1.75
- project_weight: bfloat16 [2048, 2560], P(None, 'groups'), parts along dimension 1, may hold values from -0.125 to 0.125
Outputs:
- input_gradient: float32 [2048, 4096], P('ctx', 'groups'), parts along dimension 1
- gate_gradient: float32 [2048, 4096], P('ctx', 'groups'), parts along dimension 1
- write_gradient: float32 [2048, 512], P('ctx', 'groups'), parts along dimension 1
- read_gradient: float32 [2048, 512], P('ctx', 'groups'), parts along dimension 1
There are 2 independent parts, one for each index of `groups`. A program takes and returns all parts, laid end to end along the dimension named above; each array names one. Nothing has to cross between parts.
All inputs are finite; a program needn't handle non-finite values.
Results may differ from a plain program's by a relative error of at most 0.011.
Values may be sent and summed in bfloat16 or wider, within the bound.
No kernel may reach another device: no remote copies, remote signals or barrier semaphores. Data moves between devices by JAX's collectives and lax.ppermute only.
A program may use at most 192 MiB of HBM per device.

v0:
```python
import functools
import math

import jax
import jax.numpy as jnp
from jax import lax
from jax.experimental import pallas as pl
from jax.experimental.pallas import tpu as pltpu
from jax.sharding import PartitionSpec as P

EPSILON = 1e-05
HIGHEST = lax.Precision.HIGHEST
F32 = jnp.float32
BF16 = jnp.bfloat16
EXTRA = 16
MIB = 1024 * 1024


def nn(a, b, **kw):
    return lax.dot_general(a, b, (((1,), (0,)), ((), ())), preferred_element_type=F32, **kw)


def nt(a, b, **kw):
    return lax.dot_general(a, b, (((1,), (1,)), ((), ())), preferred_element_type=F32, **kw)


def tn(a, b, **kw):
    return lax.dot_general(a, b, (((0,), (0,)), ((), ())), preferred_element_type=F32, **kw)


def iota(shape, dim):
    return lax.broadcasted_iota(jnp.int32, shape, dim)


def call(kernel, outs, args, flops, smem=(), scratch=(), spare=4 * MIB):
    specs = [
        pl.BlockSpec(memory_space=pltpu.SMEM if i in smem else pltpu.VMEM) for i in range(len(args))
    ]
    moved = sum(a.size * a.dtype.itemsize for a in args) + sum(
        math.prod(o.shape) * o.dtype.itemsize for o in outs
    )
    held = moved + sum(
        math.prod(s.shape) * jnp.dtype(s.dtype).itemsize for s in scratch
    )
    return pl.pallas_call(
        kernel,
        out_shape=tuple(outs),
        in_specs=specs,
        out_specs=tuple(pl.BlockSpec(memory_space=pltpu.VMEM) for _ in outs),
        scratch_shapes=list(scratch),
        compiler_params=pltpu.CompilerParams(vmem_limit_bytes=held + spare),
        cost_estimate=pl.CostEstimate(flops=flops, bytes_accessed=moved, transcendentals=0),
    )(*args)


def struct(shape, dtype):
    return jax.ShapeDtypeStruct(shape, dtype)


def running_sums(log_decay):
    rows = log_decay.shape[1]
    lower = (iota((rows, rows), 0) >= iota((rows, rows), 1)).astype(F32)
    upper = (iota((rows, rows), 0) <= iota((rows, rows), 1)).astype(F32)
    return nt(lower, log_decay, precision=HIGHEST), nn(log_decay, upper, precision=HIGHEST)


def spread_heads(per_head, mdim):
    rows, heads = per_head.shape
    first = iota((rows, 2 * mdim), 1) < mdim
    pairs = [
        jnp.where(first, per_head[:, h : h + 1], per_head[:, h + 1 : h + 2])
        for h in range(0, heads, 2)
    ]
    return jnp.concatenate(pairs, axis=1)


def split_pair(block, mdim):
    first = iota(block.shape, 1) < mdim
    zero = jnp.zeros_like(block)
    return jnp.concatenate([jnp.where(first, block, zero), jnp.where(first, zero, block)], axis=0)


def plane_kernel(*refs):
    *piece_refs, out_ref = refs
    for i, piece_ref in enumerate(piece_refs):
        out_ref[i] = piece_ref[...]


def tile_of(rows):
    return min(32, rows)


def stack_kernel(*refs):
    count = len(refs) // 2
    for ref, out_ref in zip(refs[:count], refs[count:]):
        tiles, wide, head_dim = out_ref.shape
        tile = ref.shape[0] // tiles
        for t in range(tiles):
            for h in range(wide // tile):
                out_ref[t, h * tile : (h + 1) * tile, :] = ref[
                    t * tile : (t + 1) * tile, h * head_dim : (h + 1) * head_dim
                ]


def put_logs(ref, logs):
    heads = logs.shape[1]
    high = logs.astype(BF16).astype(F32)
    middle = (logs - high).astype(BF16).astype(F32)
    low = (logs - high - middle).astype(BF16).astype(F32)
    place = iota((EXTRA, heads), 0)
    split = jnp.where(place == 0, high, jnp.where(place == 1, middle, low))
    wide = jnp.concatenate([split, jnp.zeros((EXTRA, ref.shape[1] - heads), F32)], axis=1)
    ref[ref.shape[0] - EXTRA :, :] = wide.astype(BF16)


def get_logs(ref, heads):
    parts = ref[ref.shape[0] - EXTRA :, 0:heads].astype(F32)
    return parts[0:1, :] + parts[1:2, :] + parts[2:3, :]


def times(logs, start, mdim, state):
    head = iota(logs.shape, 1)
    blocks = []
    for i in range(state.shape[0] // mdim):
        log = jnp.sum(jnp.where(head == start + i, logs, 0.0), axis=1, keepdims=True)
        blocks.append(jnp.exp(log) * state[i * mdim : (i + 1) * mdim, :])
    return jnp.concatenate(blocks, axis=0)


def write_halves(core, logs, scaled_ref, other_ref, keep_ref, give_ref):
    half = keep_ref.shape[0]
    for out_ref, which in ((keep_ref, core), (give_ref, 1 - core)):
        lanes = pl.ds(pl.multiple_of(which * half, half), half)
        out_ref[0:half, :] = tn(scaled_ref[:, lanes], other_ref[...]).astype(BF16)
    put_logs(give_ref, logs)


def state_kernel(
    me_ref,
    input_ref,
    write_ref,
    decay_ref,
    keep_ref,
    give_ref,
    scaled_ref,
    remain_ref,
    grow_ref,
    sum_ref,
    turned_ref,
):
    cumulated, turned = running_sums(decay_ref[...])
    sum_ref[...], turned_ref[...] = cumulated, turned
    mdim = input_ref.shape[1] // cumulated.shape[1]
    last = cumulated[-1:, :]
    remain_ref[...] = spread_heads(jnp.exp(last - cumulated), mdim)
    grow_ref[...] = spread_heads(jnp.exp(cumulated), mdim)
    scaled_ref[...] = (input_ref[...].astype(F32) * remain_ref[...]).astype(BF16)
    write_halves(me_ref[0] % 2, last, scaled_ref, write_ref, keep_ref, give_ref)


def chip_kernel(reverse, me_ref, sum_ref, keep_ref, got_ref, *rest):
    *out_refs, total_ref = rest
    heads = sum_ref.shape[1]
    half = keep_ref.shape[0]
    mdim = 2 * half // heads
    core = me_ref[0] % 2
    chip = me_ref[0] // 2 % len(out_refs)
    slice_rows = out_refs[0].shape[0] - EXTRA
    own_logs = sum_ref[sum_ref.shape[0] - 1 :, :]
    got_logs = get_logs(got_ref, heads)
    keep, got = keep_ref[...].astype(F32), got_ref[0:half, :].astype(F32)
    first = core == (1 if reverse else 0)
    decayed = times(jnp.where(first, got_logs, own_logs), core * heads // 2, mdim, jnp.where(first, keep, got))
    total_ref[...] = decayed + jnp.where(first, got, keep)
    for k, out_ref in enumerate(out_refs):
        start = pl.multiple_of((chip ^ k) * slice_rows, slice_rows)
        out_ref[0:slice_rows, :] = total_ref[pl.ds(start, slice_rows), :].astype(BF16)
        put_logs(out_ref, own_logs + got_logs)


def steps(count, reverse):
    return range(count - 1, -1, -1) if reverse else range(count)


def ordered(chip, part_refs, order_ref):
    for k, part_ref in enumerate(part_refs):
        order_ref[chip ^ k] = part_ref[...]


def advance(order_ref, source, start, heads, mdim, state):
    part_ref = order_ref.at[source]
    rows = state.shape[0]
    return times(get_logs(part_ref, heads), start, mdim, state) + part_ref[0:rows, :].astype(F32)


def total_kernel(reverse, heads, mdim, me_ref, *rest):
    *part_refs, out_ref, order_ref = rest
    count = len(part_refs)
    chip = me_ref[0] // 2 % count
    ordered(chip, part_refs, order_ref)
    start = me_ref[0] % 2 * (heads // 2) + chip * (heads // 2 // count)
    state = jnp.zeros(out_ref.shape, F32)
    for source in steps(count, reverse):
        state = advance(order_ref, source, start, heads, mdim, state)
    out_ref[...] = state.astype(BF16)


def scan_kernel(reverse, heads, mdim, me_ref, carry_ref, *rest):
    *refs, order_ref, result_ref = rest
    count = len(refs) // 2
    chip = me_ref[0] // 2 % count
    ordered(chip, refs[:count], order_ref)
    start = me_ref[0] % 2 * (heads // 2) + chip * (heads // 2 // count)
    state = carry_ref[...].astype(F32)
    for source in steps(count, reverse):
        result_ref[source] = state.astype(BF16)
        state = advance(order_ref, source, start, heads, mdim, state)
    for k, out_ref in enumerate(refs[count:]):
        out_ref[...] = result_ref[chip ^ k]


def core_kernel(reverse, me_ref, sum_ref, keep_ref, got_ref, *rest):
    *part_refs, mine_ref, send_ref, order_ref = rest
    count = len(part_refs)
    heads = sum_ref.shape[1]
    half = keep_ref.shape[0]
    core = me_ref[0] % 2
    chip = me_ref[0] // 2 % count
    slice_rows = part_refs[0].shape[0]
    for k, part_ref in enumerate(part_refs):
        start = pl.multiple_of((chip ^ k) * slice_rows, slice_rows)
        order_ref[pl.ds(start, slice_rows), :] = part_ref[...]
    first = core == (1 if reverse else 0)
    logs = jnp.where(first, sum_ref[sum_ref.shape[0] - 1 :, :], get_logs(got_ref, heads))
    own = jnp.where(first, keep_ref[...].astype(F32), got_ref[0:half, :].astype(F32))
    incoming = order_ref[...].astype(F32)
    passed = times(logs, core * heads // 2, 2 * half // heads, incoming) + own
    mine_ref[...] = jnp.where(first, incoming, passed).astype(BF16)
    send_ref[...] = jnp.where(first, passed, incoming).astype(BF16)


def whole_state(me_ref, mine_ref, other_ref, both_ref):
    core = me_ref[0] % 2
    both_ref[core] = mine_ref[...]
    both_ref[1 - core] = other_ref[...]
    _, half, nstate = both_ref.shape
    return both_ref[...].reshape(2 * half, nstate)


def mixer_kernel(
    me_ref,
    input_ref,
    write_ref,
    read_ref,
    sum_ref,
    turned_ref,
    grow_ref,
    gate_ref,
    mine_ref,
    other_ref,
    gated_ref,
    inverse_ref,
    active_ref,
    slope_ref,
    both_ref,
    out_ref,
):
    rows, channels = input_ref.shape
    mheads = sum_ref.shape[1]
    mdim = channels // mheads
    cumulated, turned = sum_ref[...], turned_ref[...]
    carried = nt(read_ref[...], whole_state(me_ref, mine_ref, other_ref, both_ref))
    out_ref[...] = grow_ref[...] * carried
    products = nt(read_ref[...], write_ref[...])
    causal = iota((rows, rows), 0) >= iota((rows, rows), 1)

    def weights_of(head):
        spread = cumulated[:, head : head + 1] - turned[head : head + 1, :]
        return (jnp.exp(jnp.where(causal, spread, -jnp.inf)) * products).astype(BF16)

    for pair in range(mheads // 2):
        lanes = slice(pair * 2 * mdim, (pair + 1) * 2 * mdim)
        weights = jnp.concatenate([weights_of(2 * pair), weights_of(2 * pair + 1)], axis=1)
        out_ref[:, lanes] += nn(weights, split_pair(input_ref[:, lanes], mdim))

    mixer_out = out_ref[...]
    gate = gate_ref[...].astype(F32)
    sigmoid = jax.nn.sigmoid(gate)
    active = gate * sigmoid
    gated = mixer_out * active
    active_ref[...] = active
    gated_ref[...] = gated
    slope_ref[...] = mixer_out * sigmoid * (1.0 + gate * (1.0 - sigmoid))
    inverse = lax.rsqrt(jnp.mean(gated * gated, axis=-1, keepdims=True) + EPSILON)
    inverse_ref[...] = jnp.broadcast_to(inverse, inverse_ref.shape)


def attention_kernel(
    in_kernel, ctx_size, me_ref, query_ref, grad_ref, *rest
):
    plane_refs, rest = rest[:4], rest[4:]
    if in_kernel:
        keep_ref, give_ref, gathered_ref, acc_ref, raw_ref, back_ref, query_acc_ref = rest
    else:
        query_out_ref, pack_ref, gathered_ref, acc_ref, raw_ref, back_ref = rest
    tiles, wide, head_dim = query_ref.shape
    rows = gathered_ref.shape[1]
    tile = rows // tiles
    heads = wide // tile
    me = me_ref[0]
    scale = 1.0 / math.sqrt(head_dim)
    base2 = scale * math.log2(math.e)
    per = rows // ctx_size
    for offset, plane_ref in enumerate(plane_refs):
        for level in range(ctx_size // 4):
            gathered_ref[me ^ (4 * level + offset)] = plane_ref[level]

    def keys_of(b):
        return gathered_ref[:, b * tile : (b + 1) * tile, 0:head_dim].reshape(
            ctx_size * tile, head_dim
        )

    def values_of(b):
        return gathered_ref[:, b * tile : (b + 1) * tile, head_dim : 2 * head_dim].reshape(
            ctx_size * tile, head_dim
        )

    key_row = iota((ctx_size * tile, wide), 0)
    key_place = (key_row % tile) * ctx_size + key_row // tile
    query_place = (iota((ctx_size * tile, wide), 1) % tile) * ctx_size + me
    visible = key_place <= query_place

    for t in range(tiles - 1, -1, -1):
        query = query_ref[t]
        grad = grad_ref[t]
        highest = None
        for b in range(t, -1, -1):
            raw = nt(keys_of(b), query)
            if b == t:
                raw = jnp.where(visible, raw, -jnp.inf)
            raw_ref[b] = raw
            block_high = jnp.max(raw, axis=0, keepdims=True)
            highest = block_high if highest is None else jnp.maximum(highest, block_high)
        total = jnp.zeros((1, wide), F32)
        delta = jnp.zeros((1, wide), F32)
        for b in range(t + 1):
            probs = jnp.exp2((raw_ref[b] - highest) * base2)
            back = nt(values_of(b), grad)
            raw_ref[b] = probs
            back_ref[b] = back
            total = total + jnp.sum(probs, axis=0, keepdims=True)
            delta = delta + jnp.sum(probs * back, axis=0, keepdims=True)
        inverse = 1.0 / total
        delta = delta * inverse
        query_grad = jnp.zeros((head_dim, wide), F32)
        for b in range(t + 1):
            weights = raw_ref[b] * inverse
            score_grad = (weights * (back_ref[b] - delta)).astype(BF16)
            value_part = nn(weights.astype(BF16), grad).reshape(ctx_size, tile, head_dim)
            key_part = nn(score_grad, query).reshape(ctx_size, tile, head_dim)
            here = slice(b * tile, (b + 1) * tile)
            if t == tiles - 1:
                acc_ref[:, here, 0:head_dim] = key_part
                acc_ref[:, here, head_dim:] = value_part
            else:
                acc_ref[:, here, 0:head_dim] += key_part
                acc_ref[:, here, head_dim:] += value_part
            query_grad = query_grad + tn(keys_of(b), score_grad)
        turned = (query_grad * scale).T
        by_head = [turned[h * tile : (h + 1) * tile, :] for h in range(heads)]
        if in_kernel:
            pairs = [
                jnp.concatenate(by_head[h : h + 2], axis=1) for h in range(0, heads, 2)
            ]
            for k in range(tile // per):
                rows_here = [p[k * per : (k + 1) * per, :] for p in pairs]
                query_acc_ref[t * (tile // per) + k] = jnp.concatenate(rows_here, axis=0)
        else:
            for h in range(heads):
                query_out_ref[t * tile : (t + 1) * tile, h * head_dim : (h + 1) * head_dim] = (
                    by_head[h].astype(BF16)
                )

    both = jnp.where(iota((1, 1, 2 * head_dim), 2) < head_dim, scale, 1.0)
    if in_kernel:
        for chip in range(ctx_size // 2):
            for out_ref, core in ((keep_ref, me % 2), (give_ref, 1 - me % 2)):
                target = 2 * chip + core
                start = pl.multiple_of(target * per, per)
                block = acc_ref[:, pl.ds(start, per), :] * both
                out_ref[chip, 0:rows, :] = block.reshape(rows, 2 * head_dim).astype(BF16)
                out_ref[chip, rows:, :] = query_acc_ref[target].astype(BF16)
    else:
        pack_ref[...] = (acc_ref[...] * both).astype(BF16)


def join_kernel(me_ref, keep_ref, got_ref, *out_refs):
    mid = keep_ref.shape[1]
    rows = 2 * mid - out_refs[0].shape[0]
    chip = me_ref[0] // 2
    for k, out_ref in enumerate(out_refs):
        target = chip ^ k
        both = keep_ref[target, 0:rows, :].astype(F32) + got_ref[target, 0:rows, :].astype(F32)
        out_ref[0:rows, :] = both.astype(BF16)
        out_ref[rows:mid, :] = keep_ref[target, rows:, :]
        out_ref[mid:, :] = got_ref[target, rows:, :]


def in_token_order(ctx_size, devices, grads):
    rows = grads.shape[0]
    per = rows // ctx_size
    token, came = iota((rows, rows), 0), iota((rows, rows), 1)
    order = (token == (came % per) * ctx_size + devices(came // per)).astype(BF16)
    return nn(order, grads).astype(BF16)


def gate_kernel(
    order,
    me_ref,
    weight_ref,
    gated_ref,
    inverse_ref,
    active_ref,
    slope_ref,
    gain_ref,
    read_ref,
    grow_ref,
    sum_ref,
    *rest,
):
    *part_refs, gate_out_ref, grad_out_ref, keep_ref, give_ref, grown_ref = rest
    rows = gated_ref.shape[0]
    chips = len(part_refs)
    ctx_size = 2 * chips
    per = rows // ctx_size
    part_refs = [part_refs[order.index(k)] for k in range(chips)]
    me = me_ref[0]
    sums = part_refs[0][0:rows, :].astype(F32)
    for part_ref in part_refs[1:]:
        sums = sums + part_ref[0:rows, :].astype(F32)
    kv_grads = in_token_order(ctx_size, lambda place: place, sums.astype(BF16))
    extra = (part_refs[0].shape[0] - rows) // 2
    query_rows = [part_ref[rows:, :].astype(F32) for part_ref in part_refs]
    columns = []
    for part in range(extra // per):
        blocks = [
            block[core * extra + part * per : core * extra + (part + 1) * per, :]
            for core in range(2)
            for block in query_rows
        ]
        columns.append(jnp.concatenate(blocks, axis=0))
    query_grads = in_token_order(
        ctx_size,
        lambda place: (2 * (place % chips) + place // chips) ^ me,
        jnp.concatenate(columns, axis=1).astype(BF16),
    )
    grads = jnp.concatenate([query_grads, kv_grads], axis=1)
    mixer_grad = nt(grads, weight_ref[...]).astype(BF16).astype(F32)

    gated = gated_ref[...]
    inverse = inverse_ref[:, 0:1]
    scaled = gain_ref[...] * mixer_grad
    mean = jnp.mean(scaled * gated, axis=-1, keepdims=True)
    gated_grad = scaled * inverse - gated * (mean * inverse * inverse * inverse)
    gate_out_ref[...] = gated_grad * slope_ref[...]
    out_grad = (gated_grad * active_ref[...]).astype(BF16)
    grad_out_ref[...] = out_grad
    grown_ref[...] = (out_grad.astype(F32) * grow_ref[...]).astype(BF16)
    last = sum_ref[rows - 1 :, :]
    write_halves(me % 2, last, grown_ref, read_ref, keep_ref, give_ref)


def local_kernel(
    me_ref,
    grad_ref,
    grown_ref,
    input_ref,
    write_ref,
    read_ref,
    sum_ref,
    turned_ref,
    mine_ref,
    other_ref,
    value_ref,
    write_out_ref,
    read_out_ref,
    both_ref,
):
    rows, channels = input_ref.shape
    mheads = sum_ref.shape[1]
    mdim = channels // mheads
    cumulated, turned = sum_ref[...], turned_ref[...]
    turned_products = nt(write_ref[...], read_ref[...])
    causal = iota((rows, rows), 0) >= iota((rows, rows), 1)
    later = iota((rows, rows), 0) <= iota((rows, rows), 1)
    pair_sum = jnp.zeros((rows, rows), F32)

    def decays_of(head):
        spread = cumulated[:, head : head + 1] - turned[head : head + 1, :]
        return jnp.exp(jnp.where(causal, spread, -jnp.inf))

    def turned_weights_of(head):
        spread = turned[head : head + 1, :] - cumulated[:, head : head + 1]
        return (jnp.exp(jnp.where(later, spread, -jnp.inf)) * turned_products).astype(BF16)

    for pair in range(mheads // 2):
        lanes = slice(pair * 2 * mdim, (pair + 1) * 2 * mdim)
        grads = split_pair(grad_ref[:, lanes], mdim)
        weights = jnp.concatenate(
            [turned_weights_of(2 * pair), turned_weights_of(2 * pair + 1)], axis=1
        )
        value_ref[:, lanes] = nn(weights, grads)
        pairs = nt(grads, input_ref[:, lanes])
        pair_sum = (
            pair_sum + decays_of(2 * pair) * pairs[:rows] + decays_of(2 * pair + 1) * pairs[rows:]
        )
    pair_low = pair_sum.astype(BF16)
    incoming = whole_state(me_ref, mine_ref, other_ref, both_ref)
    read_out_ref[...] = nn(pair_low, write_ref[...]) + nn(grown_ref[...], incoming)
    write_out_ref[...] = tn(pair_low, read_ref[...])


def final_kernel(
    me_ref,
    value_ref,
    write_part_ref,
    scaled_ref,
    remain_ref,
    write_ref,
    mine_ref,
    other_ref,
    out_ref,
    write_out_ref,
    both_ref,
):
    adjoint = whole_state(me_ref, mine_ref, other_ref, both_ref)
    out_ref[...] = value_ref[...] + remain_ref[...] * nt(write_ref[...], adjoint)
    write_out_ref[...] = write_part_ref[...] + nn(scaled_ref[...], adjoint)


def crossed(array, bits):
    pairs = [(i, i ^ bits) for i in range(lax.axis_size("ctx"))]
    return lax.ppermute(array, "ctx", pairs)


def tied(arrays, after):
    return lax.optimization_barrier((arrays, after))[0]


def scan_slices(me, cumulated, keep, give, reverse):
    group = lax.axis_size("ctx") // 4
    half_rows, nstate = keep.shape
    got = crossed(give, 1)
    slices = call(
        functools.partial(chip_kernel, reverse),
        [struct((half_rows // group + EXTRA, nstate), BF16)] * group,
        [me, cumulated, keep, got],
        half_rows * nstate,
        smem=(0,),
        scratch=[pltpu.VMEM((half_rows, nstate), F32)],
    )
    return slices, got


def scan_parts(slices):
    return [slices[0]] + [crossed(slices[k], 2 * k) for k in range(1, len(slices))]


def scan_total(me, cumulated, keep, parts, reverse):
    group = len(parts)
    half_rows, nstate = keep.shape
    slice_rows = half_rows // group
    heads = cumulated.shape[1]
    (total,) = call(
        functools.partial(total_kernel, reverse, heads, 2 * half_rows // heads),
        [struct((slice_rows, nstate), BF16)],
        [me] + list(parts),
        half_rows * nstate,
        smem=(0,),
        scratch=[pltpu.VMEM((group, slice_rows + EXTRA, nstate), BF16)],
    )
    return total


def scan_carry(total, reverse):
    half = lax.axis_size("ctx") // 2
    if reverse:
        pairs = [(i + half, i) for i in range(half)]
    else:
        pairs = [(i, i + half) for i in range(half)]
    return lax.ppermute(total, "ctx", pairs)


def scan_back(me, cumulated, carry, keep, parts, reverse):
    group = len(parts)
    slice_rows, nstate = carry.shape
    heads = cumulated.shape[1]
    backs = call(
        functools.partial(scan_kernel, reverse, heads, 2 * keep.shape[0] // heads),
        [struct(carry.shape, BF16)] * group,
        [me, carry] + list(parts),
        group * slice_rows * nstate,
        smem=(0,),
        scratch=[
            pltpu.VMEM((group, slice_rows + EXTRA, nstate), BF16),
            pltpu.VMEM((group, slice_rows, nstate), BF16),
        ],
    )
    return backs


def scan_out(me, cumulated, returned, keep, got, reverse):
    mine, send = call(
        functools.partial(core_kernel, reverse),
        [struct(keep.shape, BF16)] * 2,
        [me, cumulated, keep, got] + list(returned),
        keep.size,
        smem=(0,),
        scratch=[pltpu.VMEM(keep.shape, BF16)],
    )
    return mine, crossed(send, 1)


def body(
    queries,
    keys,
    values,
    d_out,
    mixer_input,
    gate_input,
    state_write,
    state_read,
    log_decay,
    norm_gain,
    project_weight,
):
    ctx_size = lax.axis_size("ctx")
    ctx_index = lax.axis_index("ctx")
    rows, head_dim = keys.shape
    wide = queries.shape[1]
    channels = mixer_input.shape[1]
    nstate = state_write.shape[1]
    mheads = log_decay.shape[1]
    per = rows // ctx_size
    me = ctx_index.astype(jnp.int32).reshape(1)
    packed = jnp.pad(keys, ((0, 0), (0, head_dim))) + jnp.pad(values, ((0, 0), (head_dim, 0)))
    near_plane = [packed] + [crossed(packed, k) for k in range(4, ctx_size, 4)]
    (plane,) = call(
        plane_kernel,
        [struct((ctx_size // 4, rows, 2 * head_dim), BF16)],
        near_plane,
        rows * head_dim,
    )
    plane_other = crossed(plane, 1)
    half_states = [
        struct((channels // 2, nstate), BF16),
        struct((channels // 2 + EXTRA, nstate), BF16),
    ]
    tile = tile_of(rows)
    columns = tile * wide // head_dim
    stacked = struct((rows // tile, columns, head_dim), BF16)
    keep, give, scaled, remain, grow, cumulated, turned = call(
        state_kernel,
        [
            *half_states,
            struct((rows, channels), BF16),
            struct((rows, channels), F32),
            struct((rows, channels), F32),
            struct((rows, mheads), F32),
            struct((mheads, rows), F32),
        ],
        [me, mixer_input, state_write, tied(log_decay.T, packed)],
        2 * rows * channels * nstate,
        smem=(0,),
    )

    query_tiles, grad_tiles = call(
        stack_kernel, [stacked, stacked], [queries, d_out], rows * wide
    )
    slices, got = scan_slices(me, cumulated, keep, give, False)
    parts = scan_parts(slices)
    across = crossed(plane, 2)
    across_other = crossed(tied(across, (tuple(parts[1:]), query_tiles)), 1)

    total = scan_total(me, cumulated, keep, parts, False)
    carry = scan_carry(total, False)
    query_tiles = tied(query_tiles, total)

    in_kernel = per % 8 == 0
    flops = 10 * rows * wide * ctx_size * rows
    scratch = [
        pltpu.VMEM((ctx_size, rows, 2 * head_dim), BF16),
        pltpu.VMEM((ctx_size, rows, 2 * head_dim), F32),
        pltpu.VMEM((rows // tile, ctx_size * tile, columns), F32),
        pltpu.VMEM((rows // tile, ctx_size * tile, columns), F32),
    ]
    attention_args = [me, query_tiles, grad_tiles, plane, plane_other, across, across_other]
    chips = ctx_size // 2
    extra = per * wide // (2 * head_dim)
    if in_kernel:
        part = struct((chips, rows + extra, 2 * head_dim), BF16)
        kv_keep, kv_give = call(
            functools.partial(attention_kernel, True, ctx_size),
            [part, part],
            attention_args,
            flops,
            smem=(0,),
            scratch=scratch + [pltpu.VMEM((ctx_size, extra, 2 * head_dim), F32)],
        )
    else:
        query_grad, kv_grad = call(
            functools.partial(attention_kernel, False, ctx_size),
            [struct((rows, wide), BF16), struct((ctx_size, rows, 2 * head_dim), BF16)],
            attention_args,
            flops,
            smem=(0,),
            scratch=scratch,
        )
        by_target = kv_grad.reshape(ctx_size, ctx_size, per, 2 * head_dim).transpose(1, 0, 2, 3)
        by_pair = query_grad.reshape(ctx_size, per, -1, 2 * head_dim).transpose(0, 2, 1, 3)
        sent = jnp.concatenate(
            [
                by_target.reshape(ctx_size, rows, 2 * head_dim),
                by_pair.reshape(ctx_size, extra, 2 * head_dim),
            ],
            axis=1,
        ).reshape(chips, 2, rows + extra, 2 * head_dim)
        kv_keep = lax.dynamic_index_in_dim(sent, ctx_index % 2, 1, False)
        kv_give = lax.dynamic_index_in_dim(sent, 1 - ctx_index % 2, 1, False)

    carry, kv_keep, kv_give = lax.optimization_barrier((carry, kv_keep, kv_give))
    kv_got = crossed(kv_give, 1)
    backs = scan_back(me, cumulated, carry, keep, parts, False)
    sent = call(
        join_kernel,
        [struct((rows + 2 * extra, 2 * head_dim), BF16)] * chips,
        [me, kv_keep, tied(kv_got, backs[0])],
        chips * rows * 2 * head_dim,
        smem=(0,),
    )
    order = sorted(range(chips), key=lambda k: (-(k // 4), k % 2, -k))
    received = [crossed(sent[k], 2 * k) if k else sent[k] for k in order]
    returned = tied(tuple(scan_parts(backs)), tuple(received[:3]))
    incoming, incoming_other = scan_out(me, cumulated, returned, keep, got, False)

    both_states = pltpu.VMEM((2, channels // 2, nstate), BF16)
    whole = struct((rows, channels), F32)
    gated, inverse, active, slope = call(
        mixer_kernel,
        [whole, struct((rows, 128), F32), whole, whole],
        [
            me,
            mixer_input,
            state_write,
            state_read,
            cumulated,
            turned,
            grow,
            gate_input,
            incoming,
            incoming_other,
        ],
        2 * rows * channels * (nstate + rows),
        smem=(0,),
        scratch=[both_states, pltpu.VMEM((rows, channels), F32)],
    )
    gate_gradient, out_grad, adjoint_keep, adjoint_give, grown = call(
        functools.partial(gate_kernel, order),
        [
            struct((rows, channels), F32),
            struct((rows, channels), BF16),
            *half_states,
            struct((rows, channels), BF16),
        ],
        [
            me,
            project_weight,
            gated,
            inverse,
            active,
            slope,
            norm_gain.reshape(1, channels),
            state_read,
            grow,
            cumulated,
        ]
        + received,
        2 * rows * channels * (nstate + project_weight.shape[1]),
        smem=(0,),
    )
    value_part, write_part, read_gradient = call(
        local_kernel,
        [
            struct((rows, channels), F32),
            struct((rows, nstate), F32),
            struct((rows, nstate), F32),
        ],
        [
            me,
            out_grad,
            grown,
            mixer_input,
            state_write,
            state_read,
            cumulated,
            turned,
            incoming,
            incoming_other,
        ],
        2 * rows * channels * (nstate + 2 * rows),
        smem=(0,),
        scratch=[both_states],
    )
    slices, got = scan_slices(me, cumulated, adjoint_keep, adjoint_give, True)
    parts = scan_parts(slices)
    carry = scan_carry(scan_total(me, cumulated, adjoint_keep, parts, True), True)
    carry = tied(carry, write_part)
    backs = scan_back(me, cumulated, carry, adjoint_keep, parts, True)
    adjoint, adjoint_other = scan_out(
        me, cumulated, scan_parts(backs), adjoint_keep, got, True
    )
    input_gradient, write_gradient = call(
        final_kernel,
        [struct((rows, channels), F32), struct((rows, nstate), F32)],
        [
            me,
            value_part,
            write_part,
            scaled,
            remain,
            state_write,
            adjoint,
            adjoint_other,
        ],
        4 * rows * channels * nstate,
        smem=(0,),
        scratch=[both_states],
    )
    return (input_gradient, gate_gradient, write_gradient, read_gradient)


def solution(mesh):
    both = P("ctx", "groups")
    return jax.shard_map(
        body,
        mesh=mesh,
        in_specs=(both,) * 9 + (P("groups"), P(None, "groups")),
        out_specs=(both,) * 4,
        check_vma=False,
    )
```

profile of v0, /device:TPU:0, one launch (start us, length us, event | category | flops | bytes accessed | tf_op | source)
XLA Modules:
  0.0 112.7 jit_solution(13091695302922687101)
XLA Ops:
  0.6 0.8 pad_add_fusion.refs_0_
  1.4 1.0 copy-done
  2.5 0.8 copy-done.2
  3.3 0.7 copy-done.8
  4.0 1.7 %shard_map.138 = (bf16[1024,256]{1,0:T(8,128)(2,1)S(1)}, bf16[1040,256]{1,0:T(8,128)(2,1)S(1)}, bf16[128,2048]{1,0:T(8,128)(2,1)S(1)}, f32[128,2048]{1,0:T(8,128...) custom-call(s32[1]{0:T(128)} %bitcast.me_ref, bf16[128,2048]{1,0:T(8,128)(2,1)S(1)} %copy-done, ...), custom_call_target="tpu_custom_call" | custom-call | flops 134217728 | bytes 4317188 | tf_op jit(solution)/shard_map/pallas_call | solution.py:45
  5.7 0.5 collective-permute-start
  6.2 4.7 %collective-permute-start.7 = (bf16[128,256]{1,0:T(8,128)(2,1)S(1)}, bf16[128,256]{1,0:T(8,128)(2,1)S(1)}, u32[]{:S(2)}, u32[]{:S(2)}) collective-permute-start(bf16[128,256]{1,0:T(8,128)(2,1)S(1)} %pad_add_fusion.refs_0_), channel_id=1, source_target_pairs={{0,12},{1,13},{2,14},{3,15},{4,8},{5,9},{6,10},{7,11},{8,4},{9,5},... | collective-permute-start | bytes 196616 | tf_op jit(solution)/shard_map/ppermute | solution.py:543
  10.9 0.6 collective-permute-start.5
  11.5 2.2 %collective-permute-done.7.refs_3_ = bf16[128,256]{1,0:T(8,128)(2,1)S(1)} collective-permute-done((bf16[128,256]{1,0:T(8,128)(2,1)S(1)}, bf16[128,256]{1,0:T(8,128)(2,1)S(1)}, u32[]{:S(2)}, u32[]{:S(2)}) %collective-permute-start.7) | collective-permute-done | bytes 65568 | tf_op jit(solution)/shard_map/ppermute | solution.py:543
  13.8 3.2 %collective-permute-done.6.refs_2_ = bf16[128,256]{1,0:T(8,128)(2,1)S(1)} collective-permute-done((bf16[128,256]{1,0:T(8,128)(2,1)S(1)}, bf16[128,256]{1,0:T(8,128)(2,1)S(1)}, u32[]{:S(2)}, u32[]{:S(2)}) %collective-permute-start.6) | collective-permute-done | bytes 65568 | tf_op jit(solution)/shard_map/ppermute | solution.py:543
  17.0 1.6 %collective-permute-start.9 = (bf16[4,128,256]{2,1,0:T(8,128)(2,1)S(1)}, bf16[4,128,256]{2,1,0:T(8,128)(2,1)S(1)}, u32[]{:S(2)}, u32[]{:S(2)}) collective-permute-start(bf16[4,128,256]{2,1,0:T(8,128)(2,1)S(1)} %shard_map.142.rest_0_), channel_id=1, source_target_pairs={{0,2},{1,3},{2,0},{3,1},{4,6},{5,7},{6,4},{7,5},{8,10},{9,11},{10,... | collective-permute-start | bytes 786440 | tf_op jit(solution)/shard_map/ppermute | solution.py:543
  18.6 0.5 shard_map.139
  19.1 0.6 collective-permute-start.1
  19.7 1.2 %collective-permute-start.2 = (bf16[272,256]{1,0:T(8,128)(2,1)S(1)}, bf16[272,256]{1,0:T(8,128)(2,1)S(1)}, u32[]{:S(2)}, u32[]{:S(2)}) collective-permute-start(bf16[272,256]{1,0:T(8,128)(2,1)S(1)} %get-tuple-element.77), channel_id=1, source_target_pairs={{0,4},{1,5},{2,6},{3,7},{4,0},{5,1},{6,2},{7,3},{8,12},{9,13},{10,... | collective-permute-start | bytes 417800 | tf_op jit(solution)/shard_map/ppermute | solution.py:543
  20.9 1.8 %collective-permute-start.3 = (bf16[272,256]{1,0:T(8,128)(2,1)S(1)}, bf16[272,256]{1,0:T(8,128)(2,1)S(1)}, u32[]{:S(2)}, u32[]{:S(2)}) collective-permute-start(bf16[272,256]{1,0:T(8,128)(2,1)S(1)} %get-tuple-element.78), channel_id=1, source_target_pairs={{0,6},{1,7},{2,4},{3,5},{4,2},{5,3},{6,0},{7,1},{8,14},{9,15},{10,... | collective-permute-start | bytes 417800 | tf_op jit(solution)/shard_map/ppermute | solution.py:543
  22.7 0.9 copy-done.6
  23.6 0.9 copy-done.7
  24.6 0.1 shard_map.141
  24.6 0.1 collective-permute-start.8
  24.7 4.5 %collective-permute-done.9.rest_2_ = bf16[4,128,256]{2,1,0:T(8,128)(2,1)S(1)} collective-permute-done((bf16[4,128,256]{2,1,0:T(8,128)(2,1)S(1)}, bf16[4,128,256]{2,1,0:T(8,128)(2,1)S(1)}, u32[]{:S(2)}, u32[]{:S(2)}) %collective-permute-start.9) | collective-permute-done | bytes 262176 | tf_op jit(solution)/shard_map/ppermute | solution.py:543
  29.3 1.6 %collective-permute-done.1.rest_1_ = bf16[272,256]{1,0:T(8,128)(2,1)S(1)} collective-permute-done((bf16[272,256]{1,0:T(8,128)(2,1)S(1)}, bf16[272,256]{1,0:T(8,128)(2,1)S(1)}, u32[]{:S(2)}, u32[]{:S(2)}) %collective-permute-start.1) | collective-permute-done | bytes 139296 | tf_op jit(solution)/shard_map/ppermute | solution.py:543
  30.9 0.2 shard_map.140
  31.1 2.8 %collective-permute-start.4 = (bf16[256,256]{1,0:T(8,128)(2,1)S(1)}, bf16[256,256]{1,0:T(8,128)(2,1)S(1)}, u32[]{:S(2)}, u32[]{:S(2)}) collective-permute-start(bf16[256,256]{1,0:T(8,128)(2,1)S(1)} %shard_map.140), channel_id=1, source_target_pairs={{0,8},{1,9},{2,10},{3,11},{4,12},{5,13},{6,14},{7,15},{16,24},{17,... | collective-permute-start | bytes 393224 | tf_op jit(solution)/shard_map/ppermute | solution.py:591
  34.1 5.7 %shard_map.143 = (bf16[8,160,256]{2,1,0:T(8,128)(2,1)S(1)}, bf16[8,160,256]{2,1,0:T(8,128)(2,1)S(1)}) custom-call(s32[1]{0:T(128)} %bitcast.me_ref, bf16[4,256,128]{2,1,0:T(8,128)(2,1)S(1)} %get-tuple-element.80.query_ref, bf16[4,256,128]{2,1,0:T(8,128)(2,1)S(1)} %get-tuple-element.81.grad_ref, bf16[4,128,256]{2,1,0:T(8,128)(2,1)S(1)} %shard_map.142.rest_0_, ...), custom_call_target="tpu_custom_call" | custom-call | flops 2684354560 | bytes 2883588 | tf_op jit(solution)/shard_map/pallas_call | solution.py:45
  39.8 0.3 collective-permute-start.14
  40.1 0.3 shard_map.144
  40.4 1.6 %collective-permute-start.11 = (bf16[256,256]{1,0:T(8,128)(2,1)S(1)}, bf16[256,256]{1,0:T(8,128)(2,1)S(1)}, u32[]{:S(2)}, u32[]{:S(2)}) collective-permute-start(bf16[256,256]{1,0:T(8,128)(2,1)S(1)} %get-tuple-element.87), channel_id=1, source_target_pairs={{0,2},{1,3},{2,0},{3,1},{4,6},{5,7},{6,4},{7,5},{8,10},{9,11},{10,... | collective-permute-start | bytes 393224 | tf_op jit(solution)/shard_map/ppermute | solution.py:543
  42.0 2.4 %collective-permute-start.12 = (bf16[256,256]{1,0:T(8,128)(2,1)S(1)}, bf16[256,256]{1,0:T(8,128)(2,1)S(1)}, u32[]{:S(2)}, u32[]{:S(2)}) collective-permute-start(bf16[256,256]{1,0:T(8,128)(2,1)S(1)} %get-tuple-element.88), channel_id=1, source_target_pairs={{0,4},{1,5},{2,6},{3,7},{4,0},{5,1},{6,2},{7,3},{8,12},{9,13},{10,... | collective-permute-start | bytes 393224 | tf_op jit(solution)/shard_map/ppermute | solution.py:543
  44.3 0.1 shard_map.145
  44.4 3.9 %collective-permute-start.15 = (bf16[192,256]{1,0:T(8,128)(2,1)S(1)}, bf16[192,256]{1,0:T(8,128)(2,1)S(1)}, u32[]{:S(2)}, u32[]{:S(2)}) collective-permute-start(bf16[192,256]{1,0:T(8,128)(2,1)S(1)} %get-tuple-element.93), channel_id=1, source_target_pairs={{0,12},{1,13},{2,14},{3,15},{4,8},{5,9},{6,10},{7,11},{8,4},{9,5},... | collective-permute-start | bytes 294920 | tf_op jit(solution)/shard_map/ppermute | solution.py:543
  48.4 3.1 %collective-permute-start.17 = (bf16[192,256]{1,0:T(8,128)(2,1)S(1)}, bf16[192,256]{1,0:T(8,128)(2,1)S(1)}, u32[]{:S(2)}, u32[]{:S(2)}) collective-permute-start(bf16[192,256]{1,0:T(8,128)(2,1)S(1)} %get-tuple-element.95), channel_id=1, source_target_pairs={{0,14},{1,15},{2,12},{3,13},{4,10},{5,11},{6,8},{7,9},{8,6},{9,7},... | collective-permute-start | bytes 294920 | tf_op jit(solution)/shard_map/ppermute | solution.py:543
  51.5 4.0 %collective-permute-done.15.rest_0_ = bf16[192,256]{1,0:T(8,128)(2,1)S(1)} collective-permute-done((bf16[192,256]{1,0:T(8,128)(2,1)S(1)}, bf16[192,256]{1,0:T(8,128)(2,1)S(1)}, u32[]{:S(2)}, u32[]{:S(2)}) %collective-permute-start.15) | collective-permute-done | bytes 98336 | tf_op jit(solution)/shard_map/ppermute | solution.py:543
  55.5 5.2 %collective-permute-done.16.rest_1_ = bf16[192,256]{1,0:T(8,128)(2,1)S(1)} collective-permute-done((bf16[192,256]{1,0:T(8,128)(2,1)S(1)}, bf16[192,256]{1,0:T(8,128)(2,1)S(1)}, u32[]{:S(2)}, u32[]{:S(2)}) %collective-permute-start.16) | collective-permute-done | bytes 98336 | tf_op jit(solution)/shard_map/ppermute | solution.py:543
  60.7 0.6 shard_map.146
  61.4 2.4 %collective-permute-start.19 = (bf16[192,256]{1,0:T(8,128)(2,1)S(1)}, bf16[192,256]{1,0:T(8,128)(2,1)S(1)}, u32[]{:S(2)}, u32[]{:S(2)}) collective-permute-start(bf16[192,256]{1,0:T(8,128)(2,1)S(1)} %get-tuple-element.106), channel_id=1, source_target_pairs={{0,10},{1,11},{2,8},{3,9},{4,14},{5,15},{6,12},{7,13},{8,2},{9,3},... | collective-permute-start | bytes 294920 | tf_op jit(solution)/shard_map/ppermute | solution.py:543
  63.8 0.3 collective-permute-start.20
  64.1 2.7 %collective-permute-start.21 = (bf16[192,256]{1,0:T(8,128)(2,1)S(1)}, bf16[192,256]{1,0:T(8,128)(2,1)S(1)}, u32[]{:S(2)}, u32[]{:S(2)}) collective-permute-start(bf16[192,256]{1,0:T(8,128)(2,1)S(1)} %get-tuple-element.109), channel_id=1, source_target_pairs={{0,6},{1,7},{2,4},{3,5},{4,2},{5,3},{6,0},{7,1},{8,14},{9,15},{10,... | collective-permute-start | bytes 294920 | tf_op jit(solution)/shard_map/ppermute | solution.py:543
  66.7 0.6 collective-permute-start.22
  67.3 1.6 %shard_map.147 = (f32[128,2048]{1,0:T(8,128)S(1)}, f32[128,128]{1,0:T(8,128)S(1)}, f32[128,2048]{1,0:T(8,128)S(1)}, f32[128,2048]{1,0:T(8,128)S(1)}) custom-call(s32[1]{0:T(128)} %bitcast.me_ref, bf16[128,2048]{1,0:T(8,128)(2,1)S(1)} %copy-done.1, bf16[128,256]{1,0:T(8,128)(2,1)S(1)} %copy-done.3, bf16[128,256]{1,0:T(8,128)(2,1)S(1)} %copy-done.4, ...), custom_call_target="tpu_custom_call" | custom-call | flops 201326592 | bytes 6520836 | tf_op jit(solution)/shard_map/pallas_call | solution.py:45
  69.0 1.2 %collective-permute-done.19.rest_3_ = bf16[192,256]{1,0:T(8,128)(2,1)S(1)} collective-permute-done((bf16[192,256]{1,0:T(8,128)(2,1)S(1)}, bf16[192,256]{1,0:T(8,128)(2,1)S(1)}, u32[]{:S(2)}, u32[]{:S(2)}) %collective-permute-start.19) | collective-permute-done | bytes 98336 | tf_op jit(solution)/shard_map/ppermute | solution.py:543
  70.1 2.6 %collective-permute-done.21.rest_6_ = bf16[192,256]{1,0:T(8,128)(2,1)S(1)} collective-permute-done((bf16[192,256]{1,0:T(8,128)(2,1)S(1)}, bf16[192,256]{1,0:T(8,128)(2,1)S(1)}, u32[]{:S(2)}, u32[]{:S(2)}) %collective-permute-start.21) | collective-permute-done | bytes 98336 | tf_op jit(solution)/shard_map/ppermute | solution.py:543
  72.7 0.7 collective-permute-done.22.rest_7_
  73.5 3.6 %shard_map.148 = (f32[128,2048]{1,0:T(8,128)}, bf16[128,2048]{1,0:T(8,128)(2,1)S(1)}, bf16[1024,256]{1,0:T(8,128)(2,1)S(1)}, bf16[1040,256]{1,0:T(8,128)(2,1)S(1)}, bf16[128,2048]{1,0:T(8,128)(2,1)S(1)}) custom-call(s32[1]{0:T(128)} %bitcast.me_ref, bf16[2048,1280]{1,0:T(8,128)(2,1)S(1)} %bitcast.4, f32[128,2048]{1,0:T(8,128)S(1)} %get-tuple-element.102.gated_ref, ...), custom_call_target="tpu_custom_call" | custom-call | flops 805306368 | bytes 13533188 | tf_op jit(solution)/shard_map/pallas_call | solution.py:45
  77.0 1.9 %collective-permute-done.23.got_ref = bf16[1040,256]{1,0:T(8,128)(2,1)S(1)} collective-permute-done((bf16[1040,256]{1,0:T(8,128)(2,1)S(1)}, bf16[1040,256]{1,0:T(8,128)(2,1)S(1)}, u32[]{:S(2)}, u32[]{:S(2)}) %collective-permute-start.23) | collective-permute-done | bytes 532512 | tf_op jit(solution)/shard_map/ppermute | solution.py:543
  79.0 0.5 shard_map.150
  79.5 1.3 %collective-permute-start.24 = (bf16[272,256]{1,0:T(8,128)(2,1)S(1)}, bf16[272,256]{1,0:T(8,128)(2,1)S(1)}, u32[]{:S(2)}, u32[]{:S(2)}) collective-permute-start(bf16[272,256]{1,0:T(8,128)(2,1)S(1)} %get-tuple-element.120), channel_id=1, source_target_pairs={{0,2},{1,3},{2,0},{3,1},{4,6},{5,7},{6,4},{7,5},{8,10},{9,11},{10,... | collective-permute-start | bytes 417800 | tf_op jit(solution)/shard_map/ppermute | solution.py:543
  80.8 1.1 collective-permute-start.25
  81.9 1.1 %collective-permute-start.26 = (bf16[272,256]{1,0:T(8,128)(2,1)S(1)}, bf16[272,256]{1,0:T(8,128)(2,1)S(1)}, u32[]{:S(2)}, u32[]{:S(2)}) collective-permute-start(bf16[272,256]{1,0:T(8,128)(2,1)S(1)} %get-tuple-element.122), channel_id=1, source_target_pairs={{0,6},{1,7},{2,4},{3,5},{4,2},{5,3},{6,0},{7,1},{8,14},{9,15},{10,... | collective-permute-start | bytes 417800 | tf_op jit(solution)/shard_map/ppermute | solution.py:543
  83.0 2.2 %collective-permute-done.24.rest_1_ = bf16[272,256]{1,0:T(8,128)(2,1)S(1)} collective-permute-done((bf16[272,256]{1,0:T(8,128)(2,1)S(1)}, bf16[272,256]{1,0:T(8,128)(2,1)S(1)}, u32[]{:S(2)}, u32[]{:S(2)}) %collective-permute-start.24) | collective-permute-done | bytes 139296 | tf_op jit(solution)/shard_map/ppermute | solution.py:543
  85.3 2.1 %collective-permute-done.25.rest_2_ = bf16[272,256]{1,0:T(8,128)(2,1)S(1)} collective-permute-done((bf16[272,256]{1,0:T(8,128)(2,1)S(1)}, bf16[272,256]{1,0:T(8,128)(2,1)S(1)}, u32[]{:S(2)}, u32[]{:S(2)}) %collective-permute-start.25) | collective-permute-done | bytes 139296 | tf_op jit(solution)/shard_map/ppermute | solution.py:543
  87.3 2.1 %collective-permute-done.26.rest_3_ = bf16[272,256]{1,0:T(8,128)(2,1)S(1)} collective-permute-done((bf16[272,256]{1,0:T(8,128)(2,1)S(1)}, bf16[272,256]{1,0:T(8,128)(2,1)S(1)}, u32[]{:S(2)}, u32[]{:S(2)}) %collective-permute-start.26) | collective-permute-done | bytes 139296 | tf_op jit(solution)/shard_map/ppermute | solution.py:543
  89.5 0.2 shard_map.151
  89.7 1.5 %collective-permute-start.27 = (bf16[256,256]{1,0:T(8,128)(2,1)S(1)}, bf16[256,256]{1,0:T(8,128)(2,1)S(1)}, u32[]{:S(2)}, u32[]{:S(2)}) collective-permute-start(bf16[256,256]{1,0:T(8,128)(2,1)S(1)} %shard_map.151), channel_id=1, source_target_pairs={{8,0},{9,1},{10,2},{11,3},{12,4},{13,5},{14,6},{15,7},{24,16},{25,... | collective-permute-start | bytes 393224 | tf_op jit(solution)/shard_map/ppermute | solution.py:591
  91.2 2.4 %shard_map.149 = (f32[128,2048]{1,0:T(8,128)S(1)}, f32[128,256]{1,0:T(8,128)S(1)}, f32[128,256]{1,0:T(8,128)}) custom-call(s32[1]{0:T(128)} %bitcast.me_ref, bf16[128,2048]{1,0:T(8,128)(2,1)S(1)} %get-tuple-element.111.grad_ref, bf16[128,2048]{1,0:T(8,128)(2,1)S(1)} %get-tuple-element.112.grown_ref, bf16[128,2048]{1,0:T(8,128)(2,1)S(1)} %copy-done.1, ...), custom_call_target="tpu_custom_call" | custom-call | flops 268435456 | bytes 4096004 | tf_op jit(solution)/shard_map/pallas_call | solution.py:45
  93.6 6.1 %collective-permute-done.27.carry_ref = bf16[256,256]{1,0:T(8,128)(2,1)S(1)} collective-permute-done((bf16[256,256]{1,0:T(8,128)(2,1)S(1)}, bf16[256,256]{1,0:T(8,128)(2,1)S(1)}, u32[]{:S(2)}, u32[]{:S(2)}) %collective-permute-start.27) | collective-permute-done | bytes 131104 | tf_op jit(solution)/shard_map/ppermute | solution.py:591
  99.7 0.3 shard_map.152
  100.0 1.2 %collective-permute-start.28 = (bf16[256,256]{1,0:T(8,128)(2,1)S(1)}, bf16[256,256]{1,0:T(8,128)(2,1)S(1)}, u32[]{:S(2)}, u32[]{:S(2)}) collective-permute-start(bf16[256,256]{1,0:T(8,128)(2,1)S(1)} %get-tuple-element.125), channel_id=1, source_target_pairs={{0,2},{1,3},{2,0},{3,1},{4,6},{5,7},{6,4},{7,5},{8,10},{9,11},{10,... | collective-permute-start | bytes 393224 | tf_op jit(solution)/shard_map/ppermute | solution.py:543
  101.2 2.4 %collective-permute-start.30 = (bf16[256,256]{1,0:T(8,128)(2,1)S(1)}, bf16[256,256]{1,0:T(8,128)(2,1)S(1)}, u32[]{:S(2)}, u32[]{:S(2)}) collective-permute-start(bf16[256,256]{1,0:T(8,128)(2,1)S(1)} %get-tuple-element.127), channel_id=1, source_target_pairs={{0,6},{1,7},{2,4},{3,5},{4,2},{5,3},{6,0},{7,1},{8,14},{9,15},{10,... | collective-permute-start | bytes 393224 | tf_op jit(solution)/shard_map/ppermute | solution.py:543
  103.6 2.9 %collective-permute-done.28.rest_1_ = bf16[256,256]{1,0:T(8,128)(2,1)S(1)} collective-permute-done((bf16[256,256]{1,0:T(8,128)(2,1)S(1)}, bf16[256,256]{1,0:T(8,128)(2,1)S(1)}, u32[]{:S(2)}, u32[]{:S(2)}) %collective-permute-start.28) | collective-permute-done | bytes 131104 | tf_op jit(solution)/shard_map/ppermute | solution.py:543
  106.5 0.7 collective-permute-done.29.rest_2_
  107.1 1.2 %collective-permute-done.30.rest_3_ = bf16[256,256]{1,0:T(8,128)(2,1)S(1)} collective-permute-done((bf16[256,256]{1,0:T(8,128)(2,1)S(1)}, bf16[256,256]{1,0:T(8,128)(2,1)S(1)}, u32[]{:S(2)}, u32[]{:S(2)}) %collective-permute-start.30) | collective-permute-done | bytes 131104 | tf_op jit(solution)/shard_map/ppermute | solution.py:543
  108.4 0.6 shard_map.153
  109.1 1.9 %collective-permute-done.31.other_ref = bf16[1024,256]{1,0:T(8,128)(2,1)S(1)} collective-permute-done((bf16[1024,256]{1,0:T(8,128)(2,1)S(1)}, bf16[1024,256]{1,0:T(8,128)(2,1)S(1)}, u32[]{:S(2)}, u32[]{:S(2)}) %collective-permute-start.31) | collective-permute-done | bytes 524320 | tf_op jit(solution)/shard_map/ppermute | solution.py:543
  111.0 1.7 %shard_map.154 = (f32[128,2048]{1,0:T(8,128)}, f32[128,256]{1,0:T(8,128)}) custom-call(s32[1]{0:T(128)} %bitcast.me_ref, f32[128,2048]{1,0:T(8,128)S(1)} %get-tuple-element.113.value_ref, f32[128,256]{1,0:T(8,128)S(1)} %get-tuple-element.114.write_part_ref, bf16[128,2048]{1,0:T(8,128)(2,1)S(1)} %get-tuple-element.115.scaled_ref, ...), custom_call_target="tpu_custom_call" | custom-call | flops 268435456 | bytes 5046276 | tf_op jit(solution)/shard_map/pallas_call | solution.py:45
  (43 shorter events, 0.3 us)
Async XLA Ops:
  1.4 1.0 copy-start
  2.5 0.8 copy-start.2
  3.3 0.7 copy-start.8
  5.7 12.9 %collective-permute-start = (bf16[1040,256]{1,0:T(8,128)(2,1)S(1)}, bf16[1040,256]{1,0:T(8,128)(2,1)S(1)}, u32[]{:S(2)}, u32[]{:S(2)}) collective-permute-start(bf16[1040,256]{1,0:T(8,128)(2,1)S(1)} %get-tuple-element.74), channel_id=1, source_target_pairs={{0,1},{1,0},{2,3},{3,2},{4,5},{5,4},{6,7},{7,6},{8,9},{9,8},{10,11... | collective-permute-start | bytes 1597448 | tf_op jit(solution)/shard_map/ppermute | solution.py:543
  6.2 7.5 %collective-permute-start.7 = (bf16[128,256]{1,0:T(8,128)(2,1)S(1)}, bf16[128,256]{1,0:T(8,128)(2,1)S(1)}, u32[]{:S(2)}, u32[]{:S(2)}) collective-permute-start(bf16[128,256]{1,0:T(8,128)(2,1)S(1)} %pad_add_fusion.refs_0_), channel_id=1, source_target_pairs={{0,12},{1,13},{2,14},{3,15},{4,8},{5,9},{6,10},{7,11},{8,4},{9,5},... | collective-permute-start | bytes 196616 | tf_op jit(solution)/shard_map/ppermute | solution.py:543
  10.9 6.1 %collective-permute-start.6 = (bf16[128,256]{1,0:T(8,128)(2,1)S(1)}, bf16[128,256]{1,0:T(8,128)(2,1)S(1)}, u32[]{:S(2)}, u32[]{:S(2)}) collective-permute-start(bf16[128,256]{1,0:T(8,128)(2,1)S(1)} %pad_add_fusion.refs_0_), channel_id=1, source_target_pairs={{0,8},{1,9},{2,10},{3,11},{4,12},{5,13},{6,14},{7,15},{8,0},{9,1},... | collective-permute-start | bytes 196616 | tf_op jit(solution)/shard_map/ppermute | solution.py:543
  10.9 6.1 %collective-permute-start.5 = (bf16[128,256]{1,0:T(8,128)(2,1)S(1)}, bf16[128,256]{1,0:T(8,128)(2,1)S(1)}, u32[]{:S(2)}, u32[]{:S(2)}) collective-permute-start(bf16[128,256]{1,0:T(8,128)(2,1)S(1)} %pad_add_fusion.refs_0_), channel_id=1, source_target_pairs={{0,4},{1,5},{2,6},{3,7},{4,0},{5,1},{6,2},{7,3},{8,12},{9,13},{10,... | collective-permute-start | bytes 196616 | tf_op jit(solution)/shard_map/ppermute | solution.py:543
  17.0 12.3 %collective-permute-start.9 = (bf16[4,128,256]{2,1,0:T(8,128)(2,1)S(1)}, bf16[4,128,256]{2,1,0:T(8,128)(2,1)S(1)}, u32[]{:S(2)}, u32[]{:S(2)}) collective-permute-start(bf16[4,128,256]{2,1,0:T(8,128)(2,1)S(1)} %shard_map.142.rest_0_), channel_id=1, source_target_pairs={{0,2},{1,3},{2,0},{3,1},{4,6},{5,7},{6,4},{7,5},{8,10},{9,11},{10,... | collective-permute-start | bytes 786440 | tf_op jit(solution)/shard_map/ppermute | solution.py:543
  19.1 11.8 %collective-permute-start.1 = (bf16[272,256]{1,0:T(8,128)(2,1)S(1)}, bf16[272,256]{1,0:T(8,128)(2,1)S(1)}, u32[]{:S(2)}, u32[]{:S(2)}) collective-permute-start(bf16[272,256]{1,0:T(8,128)(2,1)S(1)} %get-tuple-element.76), channel_id=1, source_target_pairs={{0,2},{1,3},{2,0},{3,1},{4,6},{5,7},{6,4},{7,5},{8,10},{9,11},{10,... | collective-permute-start | bytes 417800 | tf_op jit(solution)/shard_map/ppermute | solution.py:543
  19.7 11.2 %collective-permute-start.2 = (bf16[272,256]{1,0:T(8,128)(2,1)S(1)}, bf16[272,256]{1,0:T(8,128)(2,1)S(1)}, u32[]{:S(2)}, u32[]{:S(2)}) collective-permute-start(bf16[272,256]{1,0:T(8,128)(2,1)S(1)} %get-tuple-element.77), channel_id=1, source_target_pairs={{0,4},{1,5},{2,6},{3,7},{4,0},{5,1},{6,2},{7,3},{8,12},{9,13},{10,... | collective-permute-start | bytes 417800 | tf_op jit(solution)/shard_map/ppermute | solution.py:543
  20.9 10.0 %collective-permute-start.3 = (bf16[272,256]{1,0:T(8,128)(2,1)S(1)}, bf16[272,256]{1,0:T(8,128)(2,1)S(1)}, u32[]{:S(2)}, u32[]{:S(2)}) collective-permute-start(bf16[272,256]{1,0:T(8,128)(2,1)S(1)} %get-tuple-element.78), channel_id=1, source_target_pairs={{0,6},{1,7},{2,4},{3,5},{4,2},{5,3},{6,0},{7,1},{8,14},{9,15},{10,... | collective-permute-start | bytes 417800 | tf_op jit(solution)/shard_map/ppermute | solution.py:543
  22.7 0.9 copy-start.6
  23.6 0.9 copy-start.7
  24.6 9.3 %collective-permute-start.8 = (bf16[4,128,256]{2,1,0:T(8,128)(2,1)S(1)}, bf16[4,128,256]{2,1,0:T(8,128)(2,1)S(1)}, u32[]{:S(2)}, u32[]{:S(2)}) collective-permute-start(bf16[4,128,256]{2,1,0:T(8,128)(2,1)S(1)} %shard_map.142.rest_0_), channel_id=1, source_target_pairs={{0,1},{1,0},{2,3},{3,2},{4,5},{5,4},{6,7},{7,6},{8,9},{9,8},{10,11... | collective-permute-start | bytes 786440 | tf_op jit(solution)/shard_map/ppermute | solution.py:543
  30.9 3.1 %collective-permute-start.10 = (bf16[4,128,256]{2,1,0:T(8,128)(2,1)S(1)}, bf16[4,128,256]{2,1,0:T(8,128)(2,1)S(1)}, u32[]{:S(2)}, u32[]{:S(2)}) collective-permute-start(bf16[4,128,256]{2,1,0:T(8,128)(2,1)S(1)} %collective-permute-done.9.rest_2_), channel_id=1, source_target_pairs={{0,1},{1,0},{2,3},{3,2},{4,5},{5,4},{6,7},{7,6},{8,9},{9,8},{10,11... | collective-permute-start | bytes 786440 | tf_op jit(solution)/shard_map/ppermute | solution.py:543
  31.1 8.6 %collective-permute-start.4 = (bf16[256,256]{1,0:T(8,128)(2,1)S(1)}, bf16[256,256]{1,0:T(8,128)(2,1)S(1)}, u32[]{:S(2)}, u32[]{:S(2)}) collective-permute-start(bf16[256,256]{1,0:T(8,128)(2,1)S(1)} %shard_map.140), channel_id=1, source_target_pairs={{0,8},{1,9},{2,10},{3,11},{4,12},{5,13},{6,14},{7,15},{16,24},{17,... | collective-permute-start | bytes 393224 | tf_op jit(solution)/shard_map/ppermute | solution.py:591
  34.0 39.5 %slice-start = ((s8[5242880]{0:T(1024)(128)(4,1)}), s8[4194304]{0:T(1024)(128)(4,1)S(1)}, s32[]{:S(2)}) async-start(s8[5242880]{0:T(1024)(128)(4,1)} %bitcast.3), calls=%async_computation | async-start | bytes 8388608
  34.0 33.3 %copy-start.1 = (bf16[128,2048]{1,0:T(8,128)(2,1)S(1)}, bf16[128,2048]{1,0:T(8,128)(2,1)}, u32[]{:S(2)}) copy-start(bf16[128,2048]{1,0:T(8,128)(2,1)} %input_ref.5) | copy-start | bytes 1572868
  34.0 33.3 %copy-start.3 = (bf16[128,256]{1,0:T(8,128)(2,1)S(1)}, bf16[128,256]{1,0:T(8,128)(2,1)}, u32[]{:S(2)}) copy-start(bf16[128,256]{1,0:T(8,128)(2,1)} %write_ref.7) | copy-start | bytes 196612
  34.0 33.3 %copy-start.4 = (bf16[128,256]{1,0:T(8,128)(2,1)S(1)}, bf16[128,256]{1,0:T(8,128)(2,1)}, u32[]{:S(2)}) copy-start(bf16[128,256]{1,0:T(8,128)(2,1)} %read_ref.5) | copy-start | bytes 196612
  34.0 33.3 %copy-start.5 = (bf16[128,2048]{1,0:T(8,128)(2,1)S(1)}, bf16[128,2048]{1,0:T(8,128)(2,1)}, u32[]{:S(2)}) copy-start(bf16[128,2048]{1,0:T(8,128)(2,1)} %gate_ref.1) | copy-start | bytes 1572868
  34.1 39.4 %slice-start.1 = ((s8[5242880]{0:T(1024)(128)(4,1)}), s8[1048576]{0:T(1024)(128)(4,1)S(1)}, s32[]{:S(2)}) async-start(s8[5242880]{0:T(1024)(128)(4,1)} %bitcast.3), calls=%async_computation.1 | async-start | bytes 2097152
  39.8 33.7 %copy-start.9 = (f32[2048]{0:T(1024)S(1)}, f32[2048]{0:T(1024)}, u32[]{:S(2)}) copy-start(f32[2048]{0:T(1024)} %param.20) | copy-start | bytes 24580
  39.8 4.5 %collective-permute-start.14 = (bf16[8,160,256]{2,1,0:T(8,128)(2,1)S(1)}, bf16[8,160,256]{2,1,0:T(8,128)(2,1)S(1)}, u32[]{:S(2)}, u32[]{:S(2)}) collective-permute-start(bf16[8,160,256]{2,1,0:T(8,128)(2,1)S(1)} %get-tuple-element.91), channel_id=1, source_target_pairs={{0,1},{1,0},{2,3},{3,2},{4,5},{5,4},{6,7},{7,6},{8,9},{9,8},{10,11... | collective-permute-start | bytes 1966088 | tf_op jit(solution)/shard_map/ppermute | solution.py:543
  40.4 8.0 %collective-permute-start.11 = (bf16[256,256]{1,0:T(8,128)(2,1)S(1)}, bf16[256,256]{1,0:T(8,128)(2,1)S(1)}, u32[]{:S(2)}, u32[]{:S(2)}) collective-permute-start(bf16[256,256]{1,0:T(8,128)(2,1)S(1)} %get-tuple-element.87), channel_id=1, source_target_pairs={{0,2},{1,3},{2,0},{3,1},{4,6},{5,7},{6,4},{7,5},{8,10},{9,11},{10,... | collective-permute-start | bytes 393224 | tf_op jit(solution)/shard_map/ppermute | solution.py:543
  42.0 9.5 %collective-permute-start.12 = (bf16[256,256]{1,0:T(8,128)(2,1)S(1)}, bf16[256,256]{1,0:T(8,128)(2,1)S(1)}, u32[]{:S(2)}, u32[]{:S(2)}) collective-permute-start(bf16[256,256]{1,0:T(8,128)(2,1)S(1)} %get-tuple-element.88), channel_id=1, source_target_pairs={{0,4},{1,5},{2,6},{3,7},{4,0},{5,1},{6,2},{7,3},{8,12},{9,13},{10,... | collective-permute-start | bytes 393224 | tf_op jit(solution)/shard_map/ppermute | solution.py:543
  44.3 7.2 %collective-permute-start.13 = (bf16[256,256]{1,0:T(8,128)(2,1)S(1)}, bf16[256,256]{1,0:T(8,128)(2,1)S(1)}, u32[]{:S(2)}, u32[]{:S(2)}) collective-permute-start(bf16[256,256]{1,0:T(8,128)(2,1)S(1)} %get-tuple-element.89), channel_id=1, source_target_pairs={{0,6},{1,7},{2,4},{3,5},{4,2},{5,3},{6,0},{7,1},{8,14},{9,15},{10,... | collective-permute-start | bytes 393224 | tf_op jit(solution)/shard_map/ppermute | solution.py:543
  44.4 11.1 %collective-permute-start.15 = (bf16[192,256]{1,0:T(8,128)(2,1)S(1)}, bf16[192,256]{1,0:T(8,128)(2,1)S(1)}, u32[]{:S(2)}, u32[]{:S(2)}) collective-permute-start(bf16[192,256]{1,0:T(8,128)(2,1)S(1)} %get-tuple-element.93), channel_id=1, source_target_pairs={{0,12},{1,13},{2,14},{3,15},{4,8},{5,9},{6,10},{7,11},{8,4},{9,5},... | collective-permute-start | bytes 294920 | tf_op jit(solution)/shard_map/ppermute | solution.py:543
  48.4 12.3 %collective-permute-start.16 = (bf16[192,256]{1,0:T(8,128)(2,1)S(1)}, bf16[192,256]{1,0:T(8,128)(2,1)S(1)}, u32[]{:S(2)}, u32[]{:S(2)}) collective-permute-start(bf16[192,256]{1,0:T(8,128)(2,1)S(1)} %get-tuple-element.94), channel_id=1, source_target_pairs={{0,8},{1,9},{2,10},{3,11},{4,12},{5,13},{6,14},{7,15},{8,0},{9,1},... | collective-permute-start | bytes 294920 | tf_op jit(solution)/shard_map/ppermute | solution.py:543
  48.4 12.3 %collective-permute-start.17 = (bf16[192,256]{1,0:T(8,128)(2,1)S(1)}, bf16[192,256]{1,0:T(8,128)(2,1)S(1)}, u32[]{:S(2)}, u32[]{:S(2)}) collective-permute-start(bf16[192,256]{1,0:T(8,128)(2,1)S(1)} %get-tuple-element.95), channel_id=1, source_target_pairs={{0,14},{1,15},{2,12},{3,13},{4,10},{5,11},{6,8},{7,9},{8,6},{9,7},... | collective-permute-start | bytes 294920 | tf_op jit(solution)/shard_map/ppermute | solution.py:543
  61.3 6.0 %collective-permute-start.18 = (bf16[1024,256]{1,0:T(8,128)(2,1)S(1)}, bf16[1024,256]{1,0:T(8,128)(2,1)S(1)}, u32[]{:S(2)}, u32[]{:S(2)}) collective-permute-start(bf16[1024,256]{1,0:T(8,128)(2,1)S(1)} %get-tuple-element.101), channel_id=1, source_target_pairs={{0,1},{1,0},{2,3},{3,2},{4,5},{5,4},{6,7},{7,6},{8,9},{9,8},{10,11... | collective-permute-start | bytes 1572872 | tf_op jit(solution)/shard_map/ppermute | solution.py:543
  61.4 8.8 %collective-permute-start.19 = (bf16[192,256]{1,0:T(8,128)(2,1)S(1)}, bf16[192,256]{1,0:T(8,128)(2,1)S(1)}, u32[]{:S(2)}, u32[]{:S(2)}) collective-permute-start(bf16[192,256]{1,0:T(8,128)(2,1)S(1)} %get-tuple-element.106), channel_id=1, source_target_pairs={{0,10},{1,11},{2,8},{3,9},{4,14},{5,15},{6,12},{7,13},{8,2},{9,3},... | collective-permute-start | bytes 294920 | tf_op jit(solution)/shard_map/ppermute | solution.py:543
  63.8 6.3 %collective-permute-start.20 = (bf16[192,256]{1,0:T(8,128)(2,1)S(1)}, bf16[192,256]{1,0:T(8,128)(2,1)S(1)}, u32[]{:S(2)}, u32[]{:S(2)}) collective-permute-start(bf16[192,256]{1,0:T(8,128)(2,1)S(1)} %get-tuple-element.107), channel_id=1, source_target_pairs={{0,4},{1,5},{2,6},{3,7},{4,0},{5,1},{6,2},{7,3},{8,12},{9,13},{10,... | collective-permute-start | bytes 294920 | tf_op jit(solution)/shard_map/ppermute | solution.py:543
  64.1 8.7 %collective-permute-start.21 = (bf16[192,256]{1,0:T(8,128)(2,1)S(1)}, bf16[192,256]{1,0:T(8,128)(2,1)S(1)}, u32[]{:S(2)}, u32[]{:S(2)}) collective-permute-start(bf16[192,256]{1,0:T(8,128)(2,1)S(1)} %get-tuple-element.109), channel_id=1, source_target_pairs={{0,6},{1,7},{2,4},{3,5},{4,2},{5,3},{6,0},{7,1},{8,14},{9,15},{10,... | collective-permute-start | bytes 294920 | tf_op jit(solution)/shard_map/ppermute | solution.py:543
  66.7 6.7 %collective-permute-start.22 = (bf16[192,256]{1,0:T(8,128)(2,1)S(1)}, bf16[192,256]{1,0:T(8,128)(2,1)S(1)}, u32[]{:S(2)}, u32[]{:S(2)}) collective-permute-start(bf16[192,256]{1,0:T(8,128)(2,1)S(1)} %get-tuple-element.110), channel_id=1, source_target_pairs={{0,2},{1,3},{2,0},{3,1},{4,6},{5,7},{6,4},{7,5},{8,10},{9,11},{10,... | collective-permute-start | bytes 294920 | tf_op jit(solution)/shard_map/ppermute | solution.py:543
  77.0 1.9 %collective-permute-start.23 = (bf16[1040,256]{1,0:T(8,128)(2,1)S(1)}, bf16[1040,256]{1,0:T(8,128)(2,1)S(1)}, u32[]{:S(2)}, u32[]{:S(2)}) collective-permute-start(bf16[1040,256]{1,0:T(8,128)(2,1)S(1)} %get-tuple-element.118), channel_id=1, source_target_pairs={{0,1},{1,0},{2,3},{3,2},{4,5},{5,4},{6,7},{7,6},{8,9},{9,8},{10,11... | collective-permute-start | bytes 1597448 | tf_op jit(solution)/shard_map/ppermute | solution.py:543
  79.5 5.8 %collective-permute-start.24 = (bf16[272,256]{1,0:T(8,128)(2,1)S(1)}, bf16[272,256]{1,0:T(8,128)(2,1)S(1)}, u32[]{:S(2)}, u32[]{:S(2)}) collective-permute-start(bf16[272,256]{1,0:T(8,128)(2,1)S(1)} %get-tuple-element.120), channel_id=1, source_target_pairs={{0,2},{1,3},{2,0},{3,1},{4,6},{5,7},{6,4},{7,5},{8,10},{9,11},{10,... | collective-permute-start | bytes 417800 | tf_op jit(solution)/shard_map/ppermute | solution.py:543
  80.8 6.6 %collective-permute-start.25 = (bf16[272,256]{1,0:T(8,128)(2,1)S(1)}, bf16[272,256]{1,0:T(8,128)(2,1)S(1)}, u32[]{:S(2)}, u32[]{:S(2)}) collective-permute-start(bf16[272,256]{1,0:T(8,128)(2,1)S(1)} %get-tuple-element.121), channel_id=1, source_target_pairs={{0,4},{1,5},{2,6},{3,7},{4,0},{5,1},{6,2},{7,3},{8,12},{9,13},{10,... | collective-permute-start | bytes 417800 | tf_op jit(solution)/shard_map/ppermute | solution.py:543
  81.9 7.6 %collective-permute-start.26 = (bf16[272,256]{1,0:T(8,128)(2,1)S(1)}, bf16[272,256]{1,0:T(8,128)(2,1)S(1)}, u32[]{:S(2)}, u32[]{:S(2)}) collective-permute-start(bf16[272,256]{1,0:T(8,128)(2,1)S(1)} %get-tuple-element.122), channel_id=1, source_target_pairs={{0,6},{1,7},{2,4},{3,5},{4,2},{5,3},{6,0},{7,1},{8,14},{9,15},{10,... | collective-permute-start | bytes 417800 | tf_op jit(solution)/shard_map/ppermute | solution.py:543
  89.7 10.0 %collective-permute-start.27 = (bf16[256,256]{1,0:T(8,128)(2,1)S(1)}, bf16[256,256]{1,0:T(8,128)(2,1)S(1)}, u32[]{:S(2)}, u32[]{:S(2)}) collective-permute-start(bf16[256,256]{1,0:T(8,128)(2,1)S(1)} %shard_map.151), channel_id=1, source_target_pairs={{8,0},{9,1},{10,2},{11,3},{12,4},{13,5},{14,6},{15,7},{24,16},{25,... | collective-permute-start | bytes 393224 | tf_op jit(solution)/shard_map/ppermute | solution.py:591
  100.0 6.4 %collective-permute-start.28 = (bf16[256,256]{1,0:T(8,128)(2,1)S(1)}, bf16[256,256]{1,0:T(8,128)(2,1)S(1)}, u32[]{:S(2)}, u32[]{:S(2)}) collective-permute-start(bf16[256,256]{1,0:T(8,128)(2,1)S(1)} %get-tuple-element.125), channel_id=1, source_target_pairs={{0,2},{1,3},{2,0},{3,1},{4,6},{5,7},{6,4},{7,5},{8,10},{9,11},{10,... | collective-permute-start | bytes 393224 | tf_op jit(solution)/shard_map/ppermute | solution.py:543
  101.2 5.9 %collective-permute-start.29 = (bf16[256,256]{1,0:T(8,128)(2,1)S(1)}, bf16[256,256]{1,0:T(8,128)(2,1)S(1)}, u32[]{:S(2)}, u32[]{:S(2)}) collective-permute-start(bf16[256,256]{1,0:T(8,128)(2,1)S(1)} %get-tuple-element.126), channel_id=1, source_target_pairs={{0,4},{1,5},{2,6},{3,7},{4,0},{5,1},{6,2},{7,3},{8,12},{9,13},{10,... | collective-permute-start | bytes 393224 | tf_op jit(solution)/shard_map/ppermute | solution.py:543
  101.2 7.2 %collective-permute-start.30 = (bf16[256,256]{1,0:T(8,128)(2,1)S(1)}, bf16[256,256]{1,0:T(8,128)(2,1)S(1)}, u32[]{:S(2)}, u32[]{:S(2)}) collective-permute-start(bf16[256,256]{1,0:T(8,128)(2,1)S(1)} %get-tuple-element.127), channel_id=1, source_target_pairs={{0,6},{1,7},{2,4},{3,5},{4,2},{5,3},{6,0},{7,1},{8,14},{9,15},{10,... | collective-permute-start | bytes 393224 | tf_op jit(solution)/shard_map/ppermute | solution.py:543
  109.0 2.0 %collective-permute-start.31 = (bf16[1024,256]{1,0:T(8,128)(2,1)S(1)}, bf16[1024,256]{1,0:T(8,128)(2,1)S(1)}, u32[]{:S(2)}, u32[]{:S(2)}) collective-permute-start(bf16[1024,256]{1,0:T(8,128)(2,1)S(1)} %get-tuple-element.129), channel_id=1, source_target_pairs={{0,1},{1,0},{2,3},{3,2},{4,5},{5,4},{6,7},{7,6},{8,9},{9,8},{10,11... | collective-permute-start | bytes 1572872 | tf_op jit(solution)/shard_map/ppermute | solution.py:543
where the time goes:
time: 113 us
  waiting for transfers between devices  46.4 us (41%)
  starting transfers between devices  39.8 us (35%)
  Pallas kernels  20.3 us (18%)
  local copies, waits for them, and re-layouts  4.53 us (4%)
    ppermute x30, waiting for transfers between devices, crossed(): return lax.ppermute(array, 'ctx', pairs)  40.3 us
    ppermute x30, starting transfers between devices, crossed(): return lax.ppermute(array, 'ctx', pairs)  35.5 us
    pallas_call x17, Pallas kernels, call(): pl.pallas_call(kernel, out_shape=tuple(outs), in_specs=specs, out_specs=t...  20.3 us
    ppermute x2, waiting for transfers between devices, scan_carry(): return lax.ppermute(total, 'ctx', pairs)  6.1 us
    unnamed x24, local copies, waits for them, and re-layouts  4.53 us
    ppermute x2, starting transfers between devices, scan_carry(): return lax.ppermute(total, 'ctx', pairs)  4.33 us
  transfers between devices with their start and end apart: 32, of which 18 were waited for; matrix products, arithmetic and copies ran while one was open for 0% of the time, Pallas kernels for 10%

commit v1 on v0

--- a/solution.py
+++ b/solution.py
@@ -182,8 +182,12 @@
     return range(count - 1, -1, -1) if reverse else range(count)
 
 
+def by_offset(part_refs):
+    return [part_refs[0], *part_refs[:0:-1]]
+
+
 def ordered(chip, part_refs, order_ref):
-    for k, part_ref in enumerate(part_refs):
+    for k, part_ref in enumerate(by_offset(part_refs)):
         order_ref[chip ^ k] = part_ref[...]
 
 
@@ -227,7 +231,7 @@
     core = me_ref[0] % 2
     chip = me_ref[0] // 2 % count
     slice_rows = part_refs[0].shape[0]
-    for k, part_ref in enumerate(part_refs):
+    for k, part_ref in enumerate(by_offset(part_refs)):
         start = pl.multiple_of((chip ^ k) * slice_rows, slice_rows)
         order_ref[pl.ds(start, slice_rows), :] = part_ref[...]
     first = core == (1 if reverse else 0)
@@ -563,7 +567,7 @@
 
 
 def scan_parts(slices):
-    return [slices[0]] + [crossed(slices[k], 2 * k) for k in range(1, len(slices))]
+    return [slices[0]] + [crossed(slices[k], 2 * k) for k in range(len(slices) - 1, 0, -1)]
 
 
 def scan_total(me, cumulated, keep, parts, reverse):
@@ -730,17 +734,17 @@
 
     carry, kv_keep, kv_give = lax.optimization_barrier((carry, kv_keep, kv_give))
     kv_got = crossed(kv_give, 1)
-    backs = scan_back(me, cumulated, carry, keep, parts, False)
     sent = call(
         join_kernel,
         [struct((rows + 2 * extra, 2 * head_dim), BF16)] * chips,
-        [me, kv_keep, tied(kv_got, backs[0])],
+        [me, kv_keep, kv_got],
         chips * rows * 2 * head_dim,
         smem=(0,),
     )
+    backs = scan_back(me, cumulated, tied(carry, sent[0]), keep, parts, False)
     order = sorted(range(chips), key=lambda k: (-(k // 4), k % 2, -k))
     received = [crossed(sent[k], 2 * k) if k else sent[k] for k in order]
-    returned = tied(tuple(scan_parts(backs)), tuple(received[:3]))
+    returned = tied(tuple(scan_parts(backs)), tuple(received[:5]))
     incoming, incoming_other = scan_out(me, cumulated, returned, keep, got, False)
 
     both_states = pltpu.VMEM((2, channels // 2, nstate), BF16)

time: 113 us -> 115 us (1.018)
  starting transfers between devices: 39.8 us -> 41.7 us
    ppermute x30, starting transfers between devices: 35.5 us -> 37.4 us  [crossed(): return lax.ppermute(array, 'ctx', pairs)]
    ppermute x30, waiting for transfers between devices: 40.3 us -> 39.1 us  [crossed(): return lax.ppermute(array, 'ctx', pairs)]
  transfers between devices with their start and end apart: 32 -> 32, of which waited for: 18 -> 19; matrix products, arithmetic and copies ran while one was open for 0% -> 0% of each run, Pallas kernels for 10% -> 10%
where the time goes in v1:
time: 115 us; the launch traced here: 114 us
  waiting for transfers between devices  46.2 us (40%)
  starting transfers between devices  41.7 us (36%)
  Pallas kernels  20.3 us (18%)
  local copies, waits for them, and re-layouts  4.53 us (4%)
    ppermute x30, waiting for transfers between devices, crossed(): return lax.ppermute(array, 'ctx', pairs)  39.1 us
    ppermute x30, starting transfers between devices, crossed(): return lax.ppermute(array, 'ctx', pairs)  37.4 us
    pallas_call x17, Pallas kernels, call(): pl.pallas_call(kernel, out_shape=tuple(outs), in_specs=specs, out_specs=t...  20.3 us
    ppermute x2, waiting for transfers between devices, scan_carry(): return lax.ppermute(total, 'ctx', pairs)  7.02 us
    unnamed x24, local copies, waits for them, and re-layouts  4.53 us
    ppermute x2, starting transfers between devices, scan_carry(): return lax.ppermute(total, 'ctx', pairs)  4.33 us
  transfers between devices with their start and end apart: 32, of which 19 were waited for; matrix products, arithmetic and copies ran while one was open for 0% of the time, Pallas kernels for 10%

profile of v1, /device:TPU:0, one launch (start us, length us, event | category | flops | bytes accessed | tf_op | source)
XLA Modules:
  0.0 114.4 jit_solution(6716634088952658534)
XLA Ops:
  0.6 0.8 pad_add_fusion.refs_0_
  1.4 1.0 copy-done
  2.5 0.8 copy-done.2
  3.3 0.7 copy-done.8
  4.0 1.7 %shard_map.138 = (bf16[1024,256]{1,0:T(8,128)(2,1)S(1)}, bf16[1040,256]{1,0:T(8,128)(2,1)S(1)}, bf16[128,2048]{1,0:T(8,128)(2,1)S(1)}, f32[128,2048]{1,0:T(8,128...) custom-call(s32[1]{0:T(128)} %bitcast.me_ref, bf16[128,2048]{1,0:T(8,128)(2,1)S(1)} %copy-done, ...), custom_call_target="tpu_custom_call" | custom-call | flops 134217728 | bytes 4317188 | tf_op jit(solution)/shard_map/pallas_call | solution.py:45
  5.7 0.5 collective-permute-start
  6.2 4.7 %collective-permute-start.7 = (bf16[128,256]{1,0:T(8,128)(2,1)S(1)}, bf16[128,256]{1,0:T(8,128)(2,1)S(1)}, u32[]{:S(2)}, u32[]{:S(2)}) collective-permute-start(bf16[128,256]{1,0:T(8,128)(2,1)S(1)} %pad_add_fusion.refs_0_), channel_id=1, source_target_pairs={{0,12},{1,13},{2,14},{3,15},{4,8},{5,9},{6,10},{7,11},{8,4},{9,5},... | collective-permute-start | bytes 196616 | tf_op jit(solution)/shard_map/ppermute | solution.py:547
  10.9 0.6 collective-permute-start.5
  11.5 2.2 %collective-permute-done.7.refs_3_ = bf16[128,256]{1,0:T(8,128)(2,1)S(1)} collective-permute-done((bf16[128,256]{1,0:T(8,128)(2,1)S(1)}, bf16[128,256]{1,0:T(8,128)(2,1)S(1)}, u32[]{:S(2)}, u32[]{:S(2)}) %collective-permute-start.7) | collective-permute-done | bytes 65568 | tf_op jit(solution)/shard_map/ppermute | solution.py:547
  13.8 3.2 %collective-permute-done.6.refs_2_ = bf16[128,256]{1,0:T(8,128)(2,1)S(1)} collective-permute-done((bf16[128,256]{1,0:T(8,128)(2,1)S(1)}, bf16[128,256]{1,0:T(8,128)(2,1)S(1)}, u32[]{:S(2)}, u32[]{:S(2)}) %collective-permute-start.6) | collective-permute-done | bytes 65568 | tf_op jit(solution)/shard_map/ppermute | solution.py:547
  17.0 1.6 %collective-permute-start.9 = (bf16[4,128,256]{2,1,0:T(8,128)(2,1)S(1)}, bf16[4,128,256]{2,1,0:T(8,128)(2,1)S(1)}, u32[]{:S(2)}, u32[]{:S(2)}) collective-permute-start(bf16[4,128,256]{2,1,0:T(8,128)(2,1)S(1)} %shard_map.142.rest_0_), channel_id=1, source_target_pairs={{0,2},{1,3},{2,0},{3,1},{4,6},{5,7},{6,4},{7,5},{8,10},{9,11},{10,... | collective-permute-start | bytes 786440 | tf_op jit(solution)/shard_map/ppermute | solution.py:547
  18.6 0.5 shard_map.139
  19.1 1.2 %collective-permute-start.1 = (bf16[272,256]{1,0:T(8,128)(2,1)S(1)}, bf16[272,256]{1,0:T(8,128)(2,1)S(1)}, u32[]{:S(2)}, u32[]{:S(2)}) collective-permute-start(bf16[272,256]{1,0:T(8,128)(2,1)S(1)} %get-tuple-element.76), channel_id=1, source_target_pairs={{0,6},{1,7},{2,4},{3,5},{4,2},{5,3},{6,0},{7,1},{8,14},{9,15},{10,... | collective-permute-start | bytes 417800 | tf_op jit(solution)/shard_map/ppermute | solution.py:547
  20.3 0.8 collective-permute-start.2
  21.1 1.5 %collective-permute-start.3 = (bf16[272,256]{1,0:T(8,128)(2,1)S(1)}, bf16[272,256]{1,0:T(8,128)(2,1)S(1)}, u32[]{:S(2)}, u32[]{:S(2)}) collective-permute-start(bf16[272,256]{1,0:T(8,128)(2,1)S(1)} %get-tuple-element.78), channel_id=1, source_target_pairs={{0,2},{1,3},{2,0},{3,1},{4,6},{5,7},{6,4},{7,5},{8,10},{9,11},{10,... | collective-permute-start | bytes 417800 | tf_op jit(solution)/shard_map/ppermute | solution.py:547
  22.7 0.9 copy-done.6
  23.6 0.9 copy-done.7
  24.6 0.1 shard_map.141
  24.7 4.5 %collective-permute-done.9.rest_2_ = bf16[4,128,256]{2,1,0:T(8,128)(2,1)S(1)} collective-permute-done((bf16[4,128,256]{2,1,0:T(8,128)(2,1)S(1)}, bf16[4,128,256]{2,1,0:T(8,128)(2,1)S(1)}, u32[]{:S(2)}, u32[]{:S(2)}) %collective-permute-start.9) | collective-permute-done | bytes 262176 | tf_op jit(solution)/shard_map/ppermute | solution.py:547
  29.3 1.6 %collective-permute-done.3.rest_3_ = bf16[272,256]{1,0:T(8,128)(2,1)S(1)} collective-permute-done((bf16[272,256]{1,0:T(8,128)(2,1)S(1)}, bf16[272,256]{1,0:T(8,128)(2,1)S(1)}, u32[]{:S(2)}, u32[]{:S(2)}) %collective-permute-start.3) | collective-permute-done | bytes 139296 | tf_op jit(solution)/shard_map/ppermute | solution.py:547
  30.9 0.2 shard_map.140
  31.1 2.8 %collective-permute-start.4 = (bf16[256,256]{1,0:T(8,128)(2,1)S(1)}, bf16[256,256]{1,0:T(8,128)(2,1)S(1)}, u32[]{:S(2)}, u32[]{:S(2)}) collective-permute-start(bf16[256,256]{1,0:T(8,128)(2,1)S(1)} %shard_map.140), channel_id=1, source_target_pairs={{0,8},{1,9},{2,10},{3,11},{4,12},{5,13},{6,14},{7,15},{16,24},{17,... | collective-permute-start | bytes 393224 | tf_op jit(solution)/shard_map/ppermute | solution.py:595
  34.0 5.7 %shard_map.143 = (bf16[8,160,256]{2,1,0:T(8,128)(2,1)S(1)}, bf16[8,160,256]{2,1,0:T(8,128)(2,1)S(1)}) custom-call(s32[1]{0:T(128)} %bitcast.me_ref, bf16[4,256,128]{2,1,0:T(8,128)(2,1)S(1)} %get-tuple-element.80.query_ref, bf16[4,256,128]{2,1,0:T(8,128)(2,1)S(1)} %get-tuple-element.81.grad_ref, bf16[4,128,256]{2,1,0:T(8,128)(2,1)S(1)} %shard_map.142.rest_0_, ...), custom_call_target="tpu_custom_call" | custom-call | flops 2684354560 | bytes 2883588 | tf_op jit(solution)/shard_map/pallas_call | solution.py:45
  39.8 0.3 collective-permute-start.11
  40.1 1.9 %collective-permute-done.11.got_ref = bf16[8,160,256]{2,1,0:T(8,128)(2,1)S(1)} collective-permute-done((bf16[8,160,256]{2,1,0:T(8,128)(2,1)S(1)}, bf16[8,160,256]{2,1,0:T(8,128)(2,1)S(1)}, u32[]{:S(2)}, u32[]{:S(2)}) %collective-permute-start.11) | collective-permute-done | bytes 655392 | tf_op jit(solution)/shard_map/ppermute | solution.py:547
  41.9 0.1 shard_map.144
  42.1 4.5 %collective-permute-start.15 = (bf16[192,256]{1,0:T(8,128)(2,1)S(1)}, bf16[192,256]{1,0:T(8,128)(2,1)S(1)}, u32[]{:S(2)}, u32[]{:S(2)}) collective-permute-start(bf16[192,256]{1,0:T(8,128)(2,1)S(1)} %get-tuple-element.94), channel_id=1, source_target_pairs={{0,12},{1,13},{2,14},{3,15},{4,8},{5,9},{6,10},{7,11},{8,4},{9,5},... | collective-permute-start | bytes 294920 | tf_op jit(solution)/shard_map/ppermute | solution.py:547
  46.6 1.3 %collective-permute-start.17 = (bf16[192,256]{1,0:T(8,128)(2,1)S(1)}, bf16[192,256]{1,0:T(8,128)(2,1)S(1)}, u32[]{:S(2)}, u32[]{:S(2)}) collective-permute-start(bf16[192,256]{1,0:T(8,128)(2,1)S(1)} %get-tuple-element.96), channel_id=1, source_target_pairs={{0,14},{1,15},{2,12},{3,13},{4,10},{5,11},{6,8},{7,9},{8,6},{9,7},... | collective-permute-start | bytes 294920 | tf_op jit(solution)/shard_map/ppermute | solution.py:547
  47.9 0.3 shard_map.145
  48.2 3.1 %collective-permute-start.12 = (bf16[256,256]{1,0:T(8,128)(2,1)S(1)}, bf16[256,256]{1,0:T(8,128)(2,1)S(1)}, u32[]{:S(2)}, u32[]{:S(2)}) collective-permute-start(bf16[256,256]{1,0:T(8,128)(2,1)S(1)} %get-tuple-element.91), channel_id=1, source_target_pairs={{0,6},{1,7},{2,4},{3,5},{4,2},{5,3},{6,0},{7,1},{8,14},{9,15},{10,... | collective-permute-start | bytes 393224 | tf_op jit(solution)/shard_map/ppermute | solution.py:547
  51.3 0.1 collective-permute-start.13
  51.4 1.4 %collective-permute-start.14 = (bf16[256,256]{1,0:T(8,128)(2,1)S(1)}, bf16[256,256]{1,0:T(8,128)(2,1)S(1)}, u32[]{:S(2)}, u32[]{:S(2)}) collective-permute-start(bf16[256,256]{1,0:T(8,128)(2,1)S(1)} %get-tuple-element.93), channel_id=1, source_target_pairs={{0,2},{1,3},{2,0},{3,1},{4,6},{5,7},{6,4},{7,5},{8,10},{9,11},{10,... | collective-permute-start | bytes 393224 | tf_op jit(solution)/shard_map/ppermute | solution.py:547
  52.8 5.1 %collective-permute-done.16.rest_1_ = bf16[192,256]{1,0:T(8,128)(2,1)S(1)} collective-permute-done((bf16[192,256]{1,0:T(8,128)(2,1)S(1)}, bf16[192,256]{1,0:T(8,128)(2,1)S(1)}, u32[]{:S(2)}, u32[]{:S(2)}) %collective-permute-start.16) | collective-permute-done | bytes 98336 | tf_op jit(solution)/shard_map/ppermute | solution.py:547
  58.0 0.5 collective-permute-start.18
  58.5 4.4 %collective-permute-start.19 = (bf16[192,256]{1,0:T(8,128)(2,1)S(1)}, bf16[192,256]{1,0:T(8,128)(2,1)S(1)}, u32[]{:S(2)}, u32[]{:S(2)}) collective-permute-start(bf16[192,256]{1,0:T(8,128)(2,1)S(1)} %get-tuple-element.98), channel_id=1, source_target_pairs={{0,4},{1,5},{2,6},{3,7},{4,0},{5,1},{6,2},{7,3},{8,12},{9,13},{10,... | collective-permute-start | bytes 294920 | tf_op jit(solution)/shard_map/ppermute | solution.py:547
  62.8 2.4 %collective-permute-done.18.rest_3_ = bf16[192,256]{1,0:T(8,128)(2,1)S(1)} collective-permute-done((bf16[192,256]{1,0:T(8,128)(2,1)S(1)}, bf16[192,256]{1,0:T(8,128)(2,1)S(1)}, u32[]{:S(2)}, u32[]{:S(2)}) %collective-permute-start.18) | collective-permute-done | bytes 98336 | tf_op jit(solution)/shard_map/ppermute | solution.py:547
  65.3 0.3 collective-permute-done.19.rest_4_
  65.6 0.6 shard_map.146
  66.3 1.7 %collective-permute-start.21 = (bf16[192,256]{1,0:T(8,128)(2,1)S(1)}, bf16[192,256]{1,0:T(8,128)(2,1)S(1)}, u32[]{:S(2)}, u32[]{:S(2)}) collective-permute-start(bf16[192,256]{1,0:T(8,128)(2,1)S(1)} %get-tuple-element.109), channel_id=1, source_target_pairs={{0,6},{1,7},{2,4},{3,5},{4,2},{5,3},{6,0},{7,1},{8,14},{9,15},{10,... | collective-permute-start | bytes 294920 | tf_op jit(solution)/shard_map/ppermute | solution.py:547
  68.0 1.7 %collective-permute-start.22 = (bf16[192,256]{1,0:T(8,128)(2,1)S(1)}, bf16[192,256]{1,0:T(8,128)(2,1)S(1)}, u32[]{:S(2)}, u32[]{:S(2)}) collective-permute-start(bf16[192,256]{1,0:T(8,128)(2,1)S(1)} %get-tuple-element.110), channel_id=1, source_target_pairs={{0,2},{1,3},{2,0},{3,1},{4,6},{5,7},{6,4},{7,5},{8,10},{9,11},{10,... | collective-permute-start | bytes 294920 | tf_op jit(solution)/shard_map/ppermute | solution.py:547
  69.7 1.6 %shard_map.147 = (f32[128,2048]{1,0:T(8,128)S(1)}, f32[128,128]{1,0:T(8,128)S(1)}, f32[128,2048]{1,0:T(8,128)S(1)}, f32[128,2048]{1,0:T(8,128)S(1)}) custom-call(s32[1]{0:T(128)} %bitcast.me_ref, bf16[128,2048]{1,0:T(8,128)(2,1)S(1)} %copy-done.1, bf16[128,256]{1,0:T(8,128)(2,1)S(1)} %copy-done.3, bf16[128,256]{1,0:T(8,128)(2,1)S(1)} %copy-done.4, ...), custom_call_target="tpu_custom_call" | custom-call | flops 201326592 | bytes 6520836 | tf_op jit(solution)/shard_map/pallas_call | solution.py:45
  71.4 1.1 collective-permute-done.21.rest_6_
  72.5 2.0 %collective-permute-done.22.rest_7_ = bf16[192,256]{1,0:T(8,128)(2,1)S(1)} collective-permute-done((bf16[192,256]{1,0:T(8,128)(2,1)S(1)}, bf16[192,256]{1,0:T(8,128)(2,1)S(1)}, u32[]{:S(2)}, u32[]{:S(2)}) %collective-permute-start.22) | collective-permute-done | bytes 98336 | tf_op jit(solution)/shard_map/ppermute | solution.py:547
  74.5 3.6 %shard_map.148 = (f32[128,2048]{1,0:T(8,128)}, bf16[128,2048]{1,0:T(8,128)(2,1)S(1)}, bf16[1024,256]{1,0:T(8,128)(2,1)S(1)}, bf16[1040,256]{1,0:T(8,128)(2,1)S(1)}, bf16[128,2048]{1,0:T(8,128)(2,1)S(1)}) custom-call(s32[1]{0:T(128)} %bitcast.me_ref, bf16[2048,1280]{1,0:T(8,128)(2,1)S(1)} %bitcast.4, f32[128,2048]{1,0:T(8,128)S(1)} %get-tuple-element.105.gated_ref, ...), custom_call_target="tpu_custom_call" | custom-call | flops 805306368 | bytes 13533188 | tf_op jit(solution)/shard_map/pallas_call | solution.py:45
  78.1 1.9 %collective-permute-done.23.got_ref = bf16[1040,256]{1,0:T(8,128)(2,1)S(1)} collective-permute-done((bf16[1040,256]{1,0:T(8,128)(2,1)S(1)}, bf16[1040,256]{1,0:T(8,128)(2,1)S(1)}, u32[]{:S(2)}, u32[]{:S(2)}) %collective-permute-start.23) | collective-permute-done | bytes 532512 | tf_op jit(solution)/shard_map/ppermute | solution.py:547
  80.0 0.5 shard_map.150
  80.5 1.8 %collective-permute-start.24 = (bf16[272,256]{1,0:T(8,128)(2,1)S(1)}, bf16[272,256]{1,0:T(8,128)(2,1)S(1)}, u32[]{:S(2)}, u32[]{:S(2)}) collective-permute-start(bf16[272,256]{1,0:T(8,128)(2,1)S(1)} %get-tuple-element.120), channel_id=1, source_target_pairs={{0,6},{1,7},{2,4},{3,5},{4,2},{5,3},{6,0},{7,1},{8,14},{9,15},{10,... | collective-permute-start | bytes 417800 | tf_op jit(solution)/shard_map/ppermute | solution.py:547
  82.3 0.8 collective-permute-start.25
  83.1 1.0 collective-permute-start.26
  84.1 3.9 %collective-permute-done.24.rest_1_ = bf16[272,256]{1,0:T(8,128)(2,1)S(1)} collective-permute-done((bf16[272,256]{1,0:T(8,128)(2,1)S(1)}, bf16[272,256]{1,0:T(8,128)(2,1)S(1)}, u32[]{:S(2)}, u32[]{:S(2)}) %collective-permute-start.24) | collective-permute-done | bytes 139296 | tf_op jit(solution)/shard_map/ppermute | solution.py:547
  88.0 1.8 %collective-permute-done.25.rest_2_ = bf16[272,256]{1,0:T(8,128)(2,1)S(1)} collective-permute-done((bf16[272,256]{1,0:T(8,128)(2,1)S(1)}, bf16[272,256]{1,0:T(8,128)(2,1)S(1)}, u32[]{:S(2)}, u32[]{:S(2)}) %collective-permute-start.25) | collective-permute-done | bytes 139296 | tf_op jit(solution)/shard_map/ppermute | solution.py:547
  89.8 0.4 collective-permute-done.26.rest_3_
  90.2 0.2 shard_map.151
  90.4 1.5 %collective-permute-start.27 = (bf16[256,256]{1,0:T(8,128)(2,1)S(1)}, bf16[256,256]{1,0:T(8,128)(2,1)S(1)}, u32[]{:S(2)}, u32[]{:S(2)}) collective-permute-start(bf16[256,256]{1,0:T(8,128)(2,1)S(1)} %shard_map.151), channel_id=1, source_target_pairs={{8,0},{9,1},{10,2},{11,3},{12,4},{13,5},{14,6},{15,7},{24,16},{25,... | collective-permute-start | bytes 393224 | tf_op jit(solution)/shard_map/ppermute | solution.py:595
  91.9 2.4 %shard_map.149 = (f32[128,2048]{1,0:T(8,128)S(1)}, f32[128,256]{1,0:T(8,128)S(1)}, f32[128,256]{1,0:T(8,128)}) custom-call(s32[1]{0:T(128)} %bitcast.me_ref, bf16[128,2048]{1,0:T(8,128)(2,1)S(1)} %get-tuple-element.111.grad_ref, bf16[128,2048]{1,0:T(8,128)(2,1)S(1)} %get-tuple-element.112.grown_ref, bf16[128,2048]{1,0:T(8,128)(2,1)S(1)} %copy-done.1, ...), custom_call_target="tpu_custom_call" | custom-call | flops 268435456 | bytes 4096004 | tf_op jit(solution)/shard_map/pallas_call | solution.py:45
  94.4 7.0 %collective-permute-done.27.carry_ref = bf16[256,256]{1,0:T(8,128)(2,1)S(1)} collective-permute-done((bf16[256,256]{1,0:T(8,128)(2,1)S(1)}, bf16[256,256]{1,0:T(8,128)(2,1)S(1)}, u32[]{:S(2)}, u32[]{:S(2)}) %collective-permute-start.27) | collective-permute-done | bytes 131104 | tf_op jit(solution)/shard_map/ppermute | solution.py:595
  101.4 0.3 shard_map.152
  101.8 2.6 %collective-permute-start.29 = (bf16[256,256]{1,0:T(8,128)(2,1)S(1)}, bf16[256,256]{1,0:T(8,128)(2,1)S(1)}, u32[]{:S(2)}, u32[]{:S(2)}) collective-permute-start(bf16[256,256]{1,0:T(8,128)(2,1)S(1)} %get-tuple-element.126), channel_id=1, source_target_pairs={{0,4},{1,5},{2,6},{3,7},{4,0},{5,1},{6,2},{7,3},{8,12},{9,13},{10,... | collective-permute-start | bytes 393224 | tf_op jit(solution)/shard_map/ppermute | solution.py:547
  104.3 0.9 collective-permute-start.30
  105.2 3.5 %collective-permute-done.28.rest_1_ = bf16[256,256]{1,0:T(8,128)(2,1)S(1)} collective-permute-done((bf16[256,256]{1,0:T(8,128)(2,1)S(1)}, bf16[256,256]{1,0:T(8,128)(2,1)S(1)}, u32[]{:S(2)}, u32[]{:S(2)}) %collective-permute-start.28) | collective-permute-done | bytes 131104 | tf_op jit(solution)/shard_map/ppermute | solution.py:547
  108.7 1.2 %collective-permute-done.29.rest_2_ = bf16[256,256]{1,0:T(8,128)(2,1)S(1)} collective-permute-done((bf16[256,256]{1,0:T(8,128)(2,1)S(1)}, bf16[256,256]{1,0:T(8,128)(2,1)S(1)}, u32[]{:S(2)}, u32[]{:S(2)}) %collective-permute-start.29) | collective-permute-done | bytes 131104 | tf_op jit(solution)/shard_map/ppermute | solution.py:547
  110.0 0.6 shard_map.153
  110.7 1.9 %collective-permute-done.31.other_ref = bf16[1024,256]{1,0:T(8,128)(2,1)S(1)} collective-permute-done((bf16[1024,256]{1,0:T(8,128)(2,1)S(1)}, bf16[1024,256]{1,0:T(8,128)(2,1)S(1)}, u32[]{:S(2)}, u32[]{:S(2)}) %collective-permute-start.31) | collective-permute-done | bytes 524320 | tf_op jit(solution)/shard_map/ppermute | solution.py:547
  112.6 1.7 %shard_map.154 = (f32[128,2048]{1,0:T(8,128)}, f32[128,256]{1,0:T(8,128)}) custom-call(s32[1]{0:T(128)} %bitcast.me_ref, f32[128,2048]{1,0:T(8,128)S(1)} %get-tuple-element.113.value_ref, f32[128,256]{1,0:T(8,128)S(1)} %get-tuple-element.114.write_part_ref, bf16[128,2048]{1,0:T(8,128)(2,1)S(1)} %get-tuple-element.115.scaled_ref, ...), custom_call_target="tpu_custom_call" | custom-call | flops 268435456 | bytes 5046276 | tf_op jit(solution)/shard_map/pallas_call | solution.py:45
  (43 shorter events, 0.5 us)
Async XLA Ops:
  1.4 1.0 copy-start
  2.5 0.8 copy-start.2
  3.3 0.7 copy-start.8
  5.7 12.9 %collective-permute-start = (bf16[1040,256]{1,0:T(8,128)(2,1)S(1)}, bf16[1040,256]{1,0:T(8,128)(2,1)S(1)}, u32[]{:S(2)}, u32[]{:S(2)}) collective-permute-start(bf16[1040,256]{1,0:T(8,128)(2,1)S(1)} %get-tuple-element.74), channel_id=1, source_target_pairs={{0,1},{1,0},{2,3},{3,2},{4,5},{5,4},{6,7},{7,6},{8,9},{9,8},{10,11... | collective-permute-start | bytes 1597448 | tf_op jit(solution)/shard_map/ppermute | solution.py:547
  6.2 7.5 %collective-permute-start.7 = (bf16[128,256]{1,0:T(8,128)(2,1)S(1)}, bf16[128,256]{1,0:T(8,128)(2,1)S(1)}, u32[]{:S(2)}, u32[]{:S(2)}) collective-permute-start(bf16[128,256]{1,0:T(8,128)(2,1)S(1)} %pad_add_fusion.refs_0_), channel_id=1, source_target_pairs={{0,12},{1,13},{2,14},{3,15},{4,8},{5,9},{6,10},{7,11},{8,4},{9,5},... | collective-permute-start | bytes 196616 | tf_op jit(solution)/shard_map/ppermute | solution.py:547
  10.9 6.1 %collective-permute-start.6 = (bf16[128,256]{1,0:T(8,128)(2,1)S(1)}, bf16[128,256]{1,0:T(8,128)(2,1)S(1)}, u32[]{:S(2)}, u32[]{:S(2)}) collective-permute-start(bf16[128,256]{1,0:T(8,128)(2,1)S(1)} %pad_add_fusion.refs_0_), channel_id=1, source_target_pairs={{0,8},{1,9},{2,10},{3,11},{4,12},{5,13},{6,14},{7,15},{8,0},{9,1},... | collective-permute-start | bytes 196616 | tf_op jit(solution)/shard_map/ppermute | solution.py:547
  10.9 6.1 %collective-permute-start.5 = (bf16[128,256]{1,0:T(8,128)(2,1)S(1)}, bf16[128,256]{1,0:T(8,128)(2,1)S(1)}, u32[]{:S(2)}, u32[]{:S(2)}) collective-permute-start(bf16[128,256]{1,0:T(8,128)(2,1)S(1)} %pad_add_fusion.refs_0_), channel_id=1, source_target_pairs={{0,4},{1,5},{2,6},{3,7},{4,0},{5,1},{6,2},{7,3},{8,12},{9,13},{10,... | collective-permute-start | bytes 196616 | tf_op jit(solution)/shard_map/ppermute | solution.py:547
  17.0 12.3 %collective-permute-start.9 = (bf16[4,128,256]{2,1,0:T(8,128)(2,1)S(1)}, bf16[4,128,256]{2,1,0:T(8,128)(2,1)S(1)}, u32[]{:S(2)}, u32[]{:S(2)}) collective-permute-start(bf16[4,128,256]{2,1,0:T(8,128)(2,1)S(1)} %shard_map.142.rest_0_), channel_id=1, source_target_pairs={{0,2},{1,3},{2,0},{3,1},{4,6},{5,7},{6,4},{7,5},{8,10},{9,11},{10,... | collective-permute-start | bytes 786440 | tf_op jit(solution)/shard_map/ppermute | solution.py:547
  19.1 10.2 %collective-permute-start.1 = (bf16[272,256]{1,0:T(8,128)(2,1)S(1)}, bf16[272,256]{1,0:T(8,128)(2,1)S(1)}, u32[]{:S(2)}, u32[]{:S(2)}) collective-permute-start(bf16[272,256]{1,0:T(8,128)(2,1)S(1)} %get-tuple-element.76), channel_id=1, source_target_pairs={{0,6},{1,7},{2,4},{3,5},{4,2},{5,3},{6,0},{7,1},{8,14},{9,15},{10,... | collective-permute-start | bytes 417800 | tf_op jit(solution)/shard_map/ppermute | solution.py:547
  20.3 8.9 %collective-permute-start.2 = (bf16[272,256]{1,0:T(8,128)(2,1)S(1)}, bf16[272,256]{1,0:T(8,128)(2,1)S(1)}, u32[]{:S(2)}, u32[]{:S(2)}) collective-permute-start(bf16[272,256]{1,0:T(8,128)(2,1)S(1)} %get-tuple-element.77), channel_id=1, source_target_pairs={{0,4},{1,5},{2,6},{3,7},{4,0},{5,1},{6,2},{7,3},{8,12},{9,13},{10,... | collective-permute-start | bytes 417800 | tf_op jit(solution)/shard_map/ppermute | solution.py:547
  21.1 9.8 %collective-permute-start.3 = (bf16[272,256]{1,0:T(8,128)(2,1)S(1)}, bf16[272,256]{1,0:T(8,128)(2,1)S(1)}, u32[]{:S(2)}, u32[]{:S(2)}) collective-permute-start(bf16[272,256]{1,0:T(8,128)(2,1)S(1)} %get-tuple-element.78), channel_id=1, source_target_pairs={{0,2},{1,3},{2,0},{3,1},{4,6},{5,7},{6,4},{7,5},{8,10},{9,11},{10,... | collective-permute-start | bytes 417800 | tf_op jit(solution)/shard_map/ppermute | solution.py:547
  22.7 0.9 copy-start.6
  23.6 0.9 copy-start.7
  24.6 9.3 %collective-permute-start.8 = (bf16[4,128,256]{2,1,0:T(8,128)(2,1)S(1)}, bf16[4,128,256]{2,1,0:T(8,128)(2,1)S(1)}, u32[]{:S(2)}, u32[]{:S(2)}) collective-permute-start(bf16[4,128,256]{2,1,0:T(8,128)(2,1)S(1)} %shard_map.142.rest_0_), channel_id=1, source_target_pairs={{0,1},{1,0},{2,3},{3,2},{4,5},{5,4},{6,7},{7,6},{8,9},{9,8},{10,11... | collective-permute-start | bytes 786440 | tf_op jit(solution)/shard_map/ppermute | solution.py:547
  30.9 3.1 %collective-permute-start.10 = (bf16[4,128,256]{2,1,0:T(8,128)(2,1)S(1)}, bf16[4,128,256]{2,1,0:T(8,128)(2,1)S(1)}, u32[]{:S(2)}, u32[]{:S(2)}) collective-permute-start(bf16[4,128,256]{2,1,0:T(8,128)(2,1)S(1)} %collective-permute-done.9.rest_2_), channel_id=1, source_target_pairs={{0,1},{1,0},{2,3},{3,2},{4,5},{5,4},{6,7},{7,6},{8,9},{9,8},{10,11... | collective-permute-start | bytes 786440 | tf_op jit(solution)/shard_map/ppermute | solution.py:547
  31.1 8.6 %collective-permute-start.4 = (bf16[256,256]{1,0:T(8,128)(2,1)S(1)}, bf16[256,256]{1,0:T(8,128)(2,1)S(1)}, u32[]{:S(2)}, u32[]{:S(2)}) collective-permute-start(bf16[256,256]{1,0:T(8,128)(2,1)S(1)} %shard_map.140), channel_id=1, source_target_pairs={{0,8},{1,9},{2,10},{3,11},{4,12},{5,13},{6,14},{7,15},{16,24},{17,... | collective-permute-start | bytes 393224 | tf_op jit(solution)/shard_map/ppermute | solution.py:595
  34.0 40.5 %slice-start = ((s8[5242880]{0:T(1024)(128)(4,1)}), s8[4194304]{0:T(1024)(128)(4,1)S(1)}, s32[]{:S(2)}) async-start(s8[5242880]{0:T(1024)(128)(4,1)} %bitcast.3), calls=%async_computation | async-start | bytes 8388608
  34.0 35.7 %copy-start.1 = (bf16[128,2048]{1,0:T(8,128)(2,1)S(1)}, bf16[128,2048]{1,0:T(8,128)(2,1)}, u32[]{:S(2)}) copy-start(bf16[128,2048]{1,0:T(8,128)(2,1)} %input_ref.5) | copy-start | bytes 1572868
  34.0 35.7 %copy-start.3 = (bf16[128,256]{1,0:T(8,128)(2,1)S(1)}, bf16[128,256]{1,0:T(8,128)(2,1)}, u32[]{:S(2)}) copy-start(bf16[128,256]{1,0:T(8,128)(2,1)} %write_ref.7) | copy-start | bytes 196612
  34.0 35.7 %copy-start.4 = (bf16[128,256]{1,0:T(8,128)(2,1)S(1)}, bf16[128,256]{1,0:T(8,128)(2,1)}, u32[]{:S(2)}) copy-start(bf16[128,256]{1,0:T(8,128)(2,1)} %read_ref.5) | copy-start | bytes 196612
  34.0 35.7 %copy-start.5 = (bf16[128,2048]{1,0:T(8,128)(2,1)S(1)}, bf16[128,2048]{1,0:T(8,128)(2,1)}, u32[]{:S(2)}) copy-start(bf16[128,2048]{1,0:T(8,128)(2,1)} %gate_ref.1) | copy-start | bytes 1572868
  34.0 40.5 %slice-start.1 = ((s8[5242880]{0:T(1024)(128)(4,1)}), s8[1048576]{0:T(1024)(128)(4,1)S(1)}, s32[]{:S(2)}) async-start(s8[5242880]{0:T(1024)(128)(4,1)} %bitcast.3), calls=%async_computation.1 | async-start | bytes 2097152
  39.7 34.8 %copy-start.9 = (f32[2048]{0:T(1024)S(1)}, f32[2048]{0:T(1024)}, u32[]{:S(2)}) copy-start(f32[2048]{0:T(1024)} %param.20) | copy-start | bytes 24580
  39.8 2.2 %collective-permute-start.11 = (bf16[8,160,256]{2,1,0:T(8,128)(2,1)S(1)}, bf16[8,160,256]{2,1,0:T(8,128)(2,1)S(1)}, u32[]{:S(2)}, u32[]{:S(2)}) collective-permute-start(bf16[8,160,256]{2,1,0:T(8,128)(2,1)S(1)} %get-tuple-element.87), channel_id=1, source_target_pairs={{0,1},{1,0},{2,3},{3,2},{4,5},{5,4},{6,7},{7,6},{8,9},{9,8},{10,11... | collective-permute-start | bytes 1966088 | tf_op jit(solution)/shard_map/ppermute | solution.py:547
  42.1 9.4 %collective-permute-start.15 = (bf16[192,256]{1,0:T(8,128)(2,1)S(1)}, bf16[192,256]{1,0:T(8,128)(2,1)S(1)}, u32[]{:S(2)}, u32[]{:S(2)}) collective-permute-start(bf16[192,256]{1,0:T(8,128)(2,1)S(1)} %get-tuple-element.94), channel_id=1, source_target_pairs={{0,12},{1,13},{2,14},{3,15},{4,8},{5,9},{6,10},{7,11},{8,4},{9,5},... | collective-permute-start | bytes 294920 | tf_op jit(solution)/shard_map/ppermute | solution.py:547
  46.5 11.4 %collective-permute-start.16 = (bf16[192,256]{1,0:T(8,128)(2,1)S(1)}, bf16[192,256]{1,0:T(8,128)(2,1)S(1)}, u32[]{:S(2)}, u32[]{:S(2)}) collective-permute-start(bf16[192,256]{1,0:T(8,128)(2,1)S(1)} %get-tuple-element.95), channel_id=1, source_target_pairs={{0,8},{1,9},{2,10},{3,11},{4,12},{5,13},{6,14},{7,15},{8,0},{9,1},... | collective-permute-start | bytes 294920 | tf_op jit(solution)/shard_map/ppermute | solution.py:547
  46.6 11.9 %collective-permute-start.17 = (bf16[192,256]{1,0:T(8,128)(2,1)S(1)}, bf16[192,256]{1,0:T(8,128)(2,1)S(1)}, u32[]{:S(2)}, u32[]{:S(2)}) collective-permute-start(bf16[192,256]{1,0:T(8,128)(2,1)S(1)} %get-tuple-element.96), channel_id=1, source_target_pairs={{0,14},{1,15},{2,12},{3,13},{4,10},{5,11},{6,8},{7,9},{8,6},{9,7},... | collective-permute-start | bytes 294920 | tf_op jit(solution)/shard_map/ppermute | solution.py:547
  48.2 17.4 %collective-permute-start.12 = (bf16[256,256]{1,0:T(8,128)(2,1)S(1)}, bf16[256,256]{1,0:T(8,128)(2,1)S(1)}, u32[]{:S(2)}, u32[]{:S(2)}) collective-permute-start(bf16[256,256]{1,0:T(8,128)(2,1)S(1)} %get-tuple-element.91), channel_id=1, source_target_pairs={{0,6},{1,7},{2,4},{3,5},{4,2},{5,3},{6,0},{7,1},{8,14},{9,15},{10,... | collective-permute-start | bytes 393224 | tf_op jit(solution)/shard_map/ppermute | solution.py:547
  51.3 14.3 %collective-permute-start.13 = (bf16[256,256]{1,0:T(8,128)(2,1)S(1)}, bf16[256,256]{1,0:T(8,128)(2,1)S(1)}, u32[]{:S(2)}, u32[]{:S(2)}) collective-permute-start(bf16[256,256]{1,0:T(8,128)(2,1)S(1)} %get-tuple-element.92), channel_id=1, source_target_pairs={{0,4},{1,5},{2,6},{3,7},{4,0},{5,1},{6,2},{7,3},{8,12},{9,13},{10,... | collective-permute-start | bytes 393224 | tf_op jit(solution)/shard_map/ppermute | solution.py:547
  51.4 14.1 %collective-permute-start.14 = (bf16[256,256]{1,0:T(8,128)(2,1)S(1)}, bf16[256,256]{1,0:T(8,128)(2,1)S(1)}, u32[]{:S(2)}, u32[]{:S(2)}) collective-permute-start(bf16[256,256]{1,0:T(8,128)(2,1)S(1)} %get-tuple-element.93), channel_id=1, source_target_pairs={{0,2},{1,3},{2,0},{3,1},{4,6},{5,7},{6,4},{7,5},{8,10},{9,11},{10,... | collective-permute-start | bytes 393224 | tf_op jit(solution)/shard_map/ppermute | solution.py:547
  58.0 7.3 %collective-permute-start.18 = (bf16[192,256]{1,0:T(8,128)(2,1)S(1)}, bf16[192,256]{1,0:T(8,128)(2,1)S(1)}, u32[]{:S(2)}, u32[]{:S(2)}) collective-permute-start(bf16[192,256]{1,0:T(8,128)(2,1)S(1)} %get-tuple-element.97), channel_id=1, source_target_pairs={{0,10},{1,11},{2,8},{3,9},{4,14},{5,15},{6,12},{7,13},{8,2},{9,3},... | collective-permute-start | bytes 294920 | tf_op jit(solution)/shard_map/ppermute | solution.py:547
  58.5 7.1 %collective-permute-start.19 = (bf16[192,256]{1,0:T(8,128)(2,1)S(1)}, bf16[192,256]{1,0:T(8,128)(2,1)S(1)}, u32[]{:S(2)}, u32[]{:S(2)}) collective-permute-start(bf16[192,256]{1,0:T(8,128)(2,1)S(1)} %get-tuple-element.98), channel_id=1, source_target_pairs={{0,4},{1,5},{2,6},{3,7},{4,0},{5,1},{6,2},{7,3},{8,12},{9,13},{10,... | collective-permute-start | bytes 294920 | tf_op jit(solution)/shard_map/ppermute | solution.py:547
  66.2 3.5 %collective-permute-start.20 = (bf16[1024,256]{1,0:T(8,128)(2,1)S(1)}, bf16[1024,256]{1,0:T(8,128)(2,1)S(1)}, u32[]{:S(2)}, u32[]{:S(2)}) collective-permute-start(bf16[1024,256]{1,0:T(8,128)(2,1)S(1)} %get-tuple-element.104), channel_id=1, source_target_pairs={{0,1},{1,0},{2,3},{3,2},{4,5},{5,4},{6,7},{7,6},{8,9},{9,8},{10,11... | collective-permute-start | bytes 1572872 | tf_op jit(solution)/shard_map/ppermute | solution.py:547
  66.3 6.2 %collective-permute-start.21 = (bf16[192,256]{1,0:T(8,128)(2,1)S(1)}, bf16[192,256]{1,0:T(8,128)(2,1)S(1)}, u32[]{:S(2)}, u32[]{:S(2)}) collective-permute-start(bf16[192,256]{1,0:T(8,128)(2,1)S(1)} %get-tuple-element.109), channel_id=1, source_target_pairs={{0,6},{1,7},{2,4},{3,5},{4,2},{5,3},{6,0},{7,1},{8,14},{9,15},{10,... | collective-permute-start | bytes 294920 | tf_op jit(solution)/shard_map/ppermute | solution.py:547
  68.0 6.5 %collective-permute-start.22 = (bf16[192,256]{1,0:T(8,128)(2,1)S(1)}, bf16[192,256]{1,0:T(8,128)(2,1)S(1)}, u32[]{:S(2)}, u32[]{:S(2)}) collective-permute-start(bf16[192,256]{1,0:T(8,128)(2,1)S(1)} %get-tuple-element.110), channel_id=1, source_target_pairs={{0,2},{1,3},{2,0},{3,1},{4,6},{5,7},{6,4},{7,5},{8,10},{9,11},{10,... | collective-permute-start | bytes 294920 | tf_op jit(solution)/shard_map/ppermute | solution.py:547
  78.1 1.9 %collective-permute-start.23 = (bf16[1040,256]{1,0:T(8,128)(2,1)S(1)}, bf16[1040,256]{1,0:T(8,128)(2,1)S(1)}, u32[]{:S(2)}, u32[]{:S(2)}) collective-permute-start(bf16[1040,256]{1,0:T(8,128)(2,1)S(1)} %get-tuple-element.118), channel_id=1, source_target_pairs={{0,1},{1,0},{2,3},{3,2},{4,5},{5,4},{6,7},{7,6},{8,9},{9,8},{10,11... | collective-permute-start | bytes 1597448 | tf_op jit(solution)/shard_map/ppermute | solution.py:547
  80.5 7.5 %collective-permute-start.24 = (bf16[272,256]{1,0:T(8,128)(2,1)S(1)}, bf16[272,256]{1,0:T(8,128)(2,1)S(1)}, u32[]{:S(2)}, u32[]{:S(2)}) collective-permute-start(bf16[272,256]{1,0:T(8,128)(2,1)S(1)} %get-tuple-element.120), channel_id=1, source_target_pairs={{0,6},{1,7},{2,4},{3,5},{4,2},{5,3},{6,0},{7,1},{8,14},{9,15},{10,... | collective-permute-start | bytes 417800 | tf_op jit(solution)/shard_map/ppermute | solution.py:547
  82.3 7.5 %collective-permute-start.25 = (bf16[272,256]{1,0:T(8,128)(2,1)S(1)}, bf16[272,256]{1,0:T(8,128)(2,1)S(1)}, u32[]{:S(2)}, u32[]{:S(2)}) collective-permute-start(bf16[272,256]{1,0:T(8,128)(2,1)S(1)} %get-tuple-element.121), channel_id=1, source_target_pairs={{0,4},{1,5},{2,6},{3,7},{4,0},{5,1},{6,2},{7,3},{8,12},{9,13},{10,... | collective-permute-start | bytes 417800 | tf_op jit(solution)/shard_map/ppermute | solution.py:547
  83.1 7.1 %collective-permute-start.26 = (bf16[272,256]{1,0:T(8,128)(2,1)S(1)}, bf16[272,256]{1,0:T(8,128)(2,1)S(1)}, u32[]{:S(2)}, u32[]{:S(2)}) collective-permute-start(bf16[272,256]{1,0:T(8,128)(2,1)S(1)} %get-tuple-element.122), channel_id=1, source_target_pairs={{0,2},{1,3},{2,0},{3,1},{4,6},{5,7},{6,4},{7,5},{8,10},{9,11},{10,... | collective-permute-start | bytes 417800 | tf_op jit(solution)/shard_map/ppermute | solution.py:547
  90.4 11.0 %collective-permute-start.27 = (bf16[256,256]{1,0:T(8,128)(2,1)S(1)}, bf16[256,256]{1,0:T(8,128)(2,1)S(1)}, u32[]{:S(2)}, u32[]{:S(2)}) collective-permute-start(bf16[256,256]{1,0:T(8,128)(2,1)S(1)} %shard_map.151), channel_id=1, source_target_pairs={{8,0},{9,1},{10,2},{11,3},{12,4},{13,5},{14,6},{15,7},{24,16},{25,... | collective-permute-start | bytes 393224 | tf_op jit(solution)/shard_map/ppermute | solution.py:595
  101.7 7.1 %collective-permute-start.28 = (bf16[256,256]{1,0:T(8,128)(2,1)S(1)}, bf16[256,256]{1,0:T(8,128)(2,1)S(1)}, u32[]{:S(2)}, u32[]{:S(2)}) collective-permute-start(bf16[256,256]{1,0:T(8,128)(2,1)S(1)} %get-tuple-element.125), channel_id=1, source_target_pairs={{0,6},{1,7},{2,4},{3,5},{4,2},{5,3},{6,0},{7,1},{8,14},{9,15},{10,... | collective-permute-start | bytes 393224 | tf_op jit(solution)/shard_map/ppermute | solution.py:547
  101.8 8.2 %collective-permute-start.29 = (bf16[256,256]{1,0:T(8,128)(2,1)S(1)}, bf16[256,256]{1,0:T(8,128)(2,1)S(1)}, u32[]{:S(2)}, u32[]{:S(2)}) collective-permute-start(bf16[256,256]{1,0:T(8,128)(2,1)S(1)} %get-tuple-element.126), channel_id=1, source_target_pairs={{0,4},{1,5},{2,6},{3,7},{4,0},{5,1},{6,2},{7,3},{8,12},{9,13},{10,... | collective-permute-start | bytes 393224 | tf_op jit(solution)/shard_map/ppermute | solution.py:547
  104.3 5.7 %collective-permute-start.30 = (bf16[256,256]{1,0:T(8,128)(2,1)S(1)}, bf16[256,256]{1,0:T(8,128)(2,1)S(1)}, u32[]{:S(2)}, u32[]{:S(2)}) collective-permute-start(bf16[256,256]{1,0:T(8,128)(2,1)S(1)} %get-tuple-element.127), channel_id=1, source_target_pairs={{0,2},{1,3},{2,0},{3,1},{4,6},{5,7},{6,4},{7,5},{8,10},{9,11},{10,... | collective-permute-start | bytes 393224 | tf_op jit(solution)/shard_map/ppermute | solution.py:547
  110.7 2.0 %collective-permute-start.31 = (bf16[1024,256]{1,0:T(8,128)(2,1)S(1)}, bf16[1024,256]{1,0:T(8,128)(2,1)S(1)}, u32[]{:S(2)}, u32[]{:S(2)}) collective-permute-start(bf16[1024,256]{1,0:T(8,128)(2,1)S(1)} %get-tuple-element.129), channel_id=1, source_target_pairs={{0,1},{1,0},{2,3},{3,2},{4,5},{5,4},{6,7},{7,6},{8,9},{9,8},{10,11... | collective-permute-start | bytes 1572872 | tf_op jit(solution)/shard_map/ppermute | solution.py:547

commit v2 on v0

--- a/solution.py
+++ b/solution.py
@@ -330,32 +330,41 @@
     query_place = (iota((ctx_size * tile, wide), 1) % tile) * ctx_size + me
     visible = key_place <= query_place
 
-    for t in range(tiles - 1, -1, -1):
+    def score(t):
+        slot = t % 2
         query = query_ref[t]
-        grad = grad_ref[t]
         highest = None
         for b in range(t, -1, -1):
             raw = nt(keys_of(b), query)
             if b == t:
                 raw = jnp.where(visible, raw, -jnp.inf)
-            raw_ref[b] = raw
+            raw_ref[slot, b] = raw
             block_high = jnp.max(raw, axis=0, keepdims=True)
             highest = block_high if highest is None else jnp.maximum(highest, block_high)
+        return highest
+
+    def weigh(t, highest):
+        slot = t % 2
+        grad = grad_ref[t]
         total = jnp.zeros((1, wide), F32)
         delta = jnp.zeros((1, wide), F32)
         for b in range(t + 1):
-            probs = jnp.exp2((raw_ref[b] - highest) * base2)
+            probs = jnp.exp2((raw_ref[slot, b] - highest) * base2)
             back = nt(values_of(b), grad)
-            raw_ref[b] = probs
-            back_ref[b] = back
+            raw_ref[slot, b] = probs
+            back_ref[slot, b] = back
             total = total + jnp.sum(probs, axis=0, keepdims=True)
             delta = delta + jnp.sum(probs * back, axis=0, keepdims=True)
         inverse = 1.0 / total
-        delta = delta * inverse
+        return inverse, delta * inverse
+
+    def gather(t, inverse, delta):
+        slot = t % 2
+        query, grad = query_ref[t], grad_ref[t]
         query_grad = jnp.zeros((head_dim, wide), F32)
         for b in range(t + 1):
-            weights = raw_ref[b] * inverse
-            score_grad = (weights * (back_ref[b] - delta)).astype(BF16)
+            weights = raw_ref[slot, b] * inverse
+            score_grad = (weights * (back_ref[slot, b] - delta)).astype(BF16)
             value_part = nn(weights.astype(BF16), grad).reshape(ctx_size, tile, head_dim)
             key_part = nn(score_grad, query).reshape(ctx_size, tile, head_dim)
             here = slice(b * tile, (b + 1) * tile)
@@ -381,6 +390,15 @@
                     by_head[h].astype(BF16)
                 )
 
+    last = tiles - 1
+    state = weigh(last, score(last))
+    for t in range(last, -1, -1):
+        if t:
+            highest = score(t - 1)
+        gather(t, *state)
+        if t:
+            state = weigh(t - 1, highest)
+
     both = jnp.where(iota((1, 1, 2 * head_dim), 2) < head_dim, scale, 1.0)
     if in_kernel:
         for chip in range(ctx_size // 2):
@@ -421,14 +439,13 @@
     gated_ref,
     inverse_ref,
     active_ref,
-    slope_ref,
     gain_ref,
     read_ref,
     grow_ref,
     sum_ref,
     *rest,
 ):
-    *part_refs, gate_out_ref, grad_out_ref, keep_ref, give_ref, grown_ref = rest
+    *part_refs, gated_grad_ref, grad_out_ref, keep_ref, give_ref, grown_ref = rest
     rows = gated_ref.shape[0]
     chips = len(part_refs)
     ctx_size = 2 * chips
@@ -462,7 +479,7 @@
     scaled = gain_ref[...] * mixer_grad
     mean = jnp.mean(scaled * gated, axis=-1, keepdims=True)
     gated_grad = scaled * inverse - gated * (mean * inverse * inverse * inverse)
-    gate_out_ref[...] = gated_grad * slope_ref[...]
+    gated_grad_ref[...] = gated_grad
     out_grad = (gated_grad * active_ref[...]).astype(BF16)
     grad_out_ref[...] = out_grad
     grown_ref[...] = (out_grad.astype(F32) * grow_ref[...]).astype(BF16)
@@ -481,14 +498,18 @@
     turned_ref,
     mine_ref,
     other_ref,
+    gated_grad_ref,
+    slope_ref,
     value_ref,
     write_out_ref,
     read_out_ref,
+    gate_out_ref,
     both_ref,
 ):
     rows, channels = input_ref.shape
     mheads = sum_ref.shape[1]
     mdim = channels // mheads
+    gate_out_ref[...] = gated_grad_ref[...] * slope_ref[...]
     cumulated, turned = sum_ref[...], turned_ref[...]
     turned_products = nt(write_ref[...], read_ref[...])
     causal = iota((rows, rows), 0) >= iota((rows, rows), 1)
@@ -520,22 +541,38 @@
     write_out_ref[...] = tn(pair_low, read_ref[...])
 
 
+def half_of(which, half):
+    return pl.ds(pl.multiple_of(which * half, half), half)
+
+
+def half_kernel(me_ref, scaled_ref, remain_ref, write_ref, mine_ref, half_ref, write_half_ref):
+    lanes = half_of(me_ref[0] % 2, mine_ref.shape[0])
+    half_ref[...] = remain_ref[:, lanes] * nt(write_ref[...], mine_ref[...])
+    write_half_ref[...] = nn(scaled_ref[:, lanes], mine_ref[...])
+
+
 def final_kernel(
     me_ref,
     value_ref,
     write_part_ref,
+    half_ref,
+    write_half_ref,
     scaled_ref,
     remain_ref,
     write_ref,
-    mine_ref,
     other_ref,
     out_ref,
     write_out_ref,
-    both_ref,
 ):
-    adjoint = whole_state(me_ref, mine_ref, other_ref, both_ref)
-    out_ref[...] = value_ref[...] + remain_ref[...] * nt(write_ref[...], adjoint)
-    write_out_ref[...] = write_part_ref[...] + nn(scaled_ref[...], adjoint)
+    core = me_ref[0] % 2
+    half = other_ref.shape[0]
+    lanes = half_of(core, half)
+    out_ref[:, lanes] = value_ref[:, lanes] + half_ref[...]
+    lanes = half_of(1 - core, half)
+    out_ref[:, lanes] = value_ref[:, lanes] + remain_ref[:, lanes] * nt(write_ref[...], other_ref[...])
+    write_out_ref[...] = (
+        write_part_ref[...] + write_half_ref[...] + nn(scaled_ref[:, lanes], other_ref[...])
+    )
 
 
 def crossed(array, bits):
@@ -691,8 +728,8 @@
     scratch = [
         pltpu.VMEM((ctx_size, rows, 2 * head_dim), BF16),
         pltpu.VMEM((ctx_size, rows, 2 * head_dim), F32),
-        pltpu.VMEM((rows // tile, ctx_size * tile, columns), F32),
-        pltpu.VMEM((rows // tile, ctx_size * tile, columns), F32),
+        pltpu.VMEM((2, rows // tile, ctx_size * tile, columns), F32),
+        pltpu.VMEM((2, rows // tile, ctx_size * tile, columns), F32),
     ]
     attention_args = [me, query_tiles, grad_tiles, plane, plane_other, across, across_other]
     chips = ctx_size // 2
@@ -764,7 +801,7 @@
         smem=(0,),
         scratch=[both_states, pltpu.VMEM((rows, channels), F32)],
     )
-    gate_gradient, out_grad, adjoint_keep, adjoint_give, grown = call(
+    gated_grad, out_grad, adjoint_keep, adjoint_give, grown = call(
         functools.partial(gate_kernel, order),
         [
             struct((rows, channels), F32),
@@ -778,7 +815,6 @@
             gated,
             inverse,
             active,
-            slope,
             norm_gain.reshape(1, channels),
             state_read,
             grow,
@@ -788,12 +824,13 @@
         2 * rows * channels * (nstate + project_weight.shape[1]),
         smem=(0,),
     )
-    value_part, write_part, read_gradient = call(
+    value_part, write_part, read_gradient, gate_gradient = call(
         local_kernel,
         [
             struct((rows, channels), F32),
             struct((rows, nstate), F32),
             struct((rows, nstate), F32),
+            whole,
         ],
         [
             me,
@@ -806,6 +843,8 @@
             turned,
             incoming,
             incoming_other,
+            gated_grad,
+            slope,
         ],
         2 * rows * channels * (nstate + 2 * rows),
         smem=(0,),
@@ -819,22 +858,29 @@
     adjoint, adjoint_other = scan_out(
         me, cumulated, scan_parts(backs), adjoint_keep, got, True
     )
+    half_out, write_half = call(
+        half_kernel,
+        [struct((rows, channels // 2), F32), struct((rows, nstate), F32)],
+        [me, scaled, remain, state_write, adjoint],
+        2 * rows * channels * nstate,
+        smem=(0,),
+    )
     input_gradient, write_gradient = call(
         final_kernel,
-        [struct((rows, channels), F32), struct((rows, nstate), F32)],
+        [whole, struct((rows, nstate), F32)],
         [
             me,
             value_part,
             write_part,
+            half_out,
+            write_half,
             scaled,
             remain,
             state_write,
-            adjoint,
             adjoint_other,
         ],
-        4 * rows * channels * nstate,
-        smem=(0,),
-        scratch=[both_states],
+        2 * rows * channels * nstate,
+        smem=(0,),
     )
     return (input_gradient, gate_gradient, write_gradient, read_gradient)
 

time: 113 us -> 112 us (level)
    pallas_call x17 -> x18, Pallas kernels: 20.3 us -> 19.2 us  [call(): pl.pallas_call(kernel, out_shape=tuple(outs), in_specs=specs, out_specs=t...]
where the time goes in v2:
time: 112 us
  waiting for transfers between devices  45.6 us (41%)
  starting transfers between devices  40.6 us (36%)
  Pallas kernels  19.2 us (17%)
  local copies, waits for them, and re-layouts  4.53 us (4%)
    ppermute x30, waiting for transfers between devices, crossed(): return lax.ppermute(array, 'ctx', pairs)  39.9 us
    ppermute x30, starting transfers between devices, crossed(): return lax.ppermute(array, 'ctx', pairs)  36.2 us
    pallas_call x18, Pallas kernels, call(): pl.pallas_call(kernel, out_shape=tuple(outs), in_specs=specs, out_specs=t...  19.2 us
    ppermute x2, waiting for transfers between devices, scan_carry(): return lax.ppermute(total, 'ctx', pairs)  5.69 us
    unnamed x24, local copies, waits for them, and re-layouts  4.53 us
    ppermute x2, starting transfers between devices, scan_carry(): return lax.ppermute(total, 'ctx', pairs)  4.33 us
  transfers between devices with their start and end apart: 32, of which 18 were waited for; matrix products, arithmetic and copies ran while one was open for 0% of the time, Pallas kernels for 10%

profile of v2, /device:TPU:0, one launch (start us, length us, event | category | flops | bytes accessed | tf_op | source)
XLA Modules:
  0.0 111.6 jit_solution(8743846409768833928)
XLA Ops:
  0.6 0.8 pad_add_fusion.refs_0_
  1.4 1.0 copy-done
  2.5 0.8 copy-done.2
  3.3 0.7 copy-done.8
  4.0 1.7 %shard_map.138 = (bf16[1024,256]{1,0:T(8,128)(2,1)S(1)}, bf16[1040,256]{1,0:T(8,128)(2,1)S(1)}, bf16[128,2048]{1,0:T(8,128)(2,1)S(1)}, f32[128,2048]{1,0:T(8,128...) custom-call(s32[1]{0:T(128)} %bitcast.me_ref, bf16[128,2048]{1,0:T(8,128)(2,1)S(1)} %copy-done, ...), custom_call_target="tpu_custom_call" | custom-call | flops 134217728 | bytes 4317188 | tf_op jit(solution)/shard_map/pallas_call | solution.py:45
  5.7 0.5 collective-permute-start
  6.2 4.7 %collective-permute-start.7 = (bf16[128,256]{1,0:T(8,128)(2,1)S(1)}, bf16[128,256]{1,0:T(8,128)(2,1)S(1)}, u32[]{:S(2)}, u32[]{:S(2)}) collective-permute-start(bf16[128,256]{1,0:T(8,128)(2,1)S(1)} %pad_add_fusion.refs_0_), channel_id=1, source_target_pairs={{0,12},{1,13},{2,14},{3,15},{4,8},{5,9},{6,10},{7,11},{8,4},{9,5},... | collective-permute-start | bytes 196616 | tf_op jit(solution)/shard_map/ppermute | solution.py:580
  10.9 0.6 collective-permute-start.5
  11.5 2.2 %collective-permute-done.7.refs_3_ = bf16[128,256]{1,0:T(8,128)(2,1)S(1)} collective-permute-done((bf16[128,256]{1,0:T(8,128)(2,1)S(1)}, bf16[128,256]{1,0:T(8,128)(2,1)S(1)}, u32[]{:S(2)}, u32[]{:S(2)}) %collective-permute-start.7) | collective-permute-done | bytes 65568 | tf_op jit(solution)/shard_map/ppermute | solution.py:580
  13.8 3.2 %collective-permute-done.6.refs_2_ = bf16[128,256]{1,0:T(8,128)(2,1)S(1)} collective-permute-done((bf16[128,256]{1,0:T(8,128)(2,1)S(1)}, bf16[128,256]{1,0:T(8,128)(2,1)S(1)}, u32[]{:S(2)}, u32[]{:S(2)}) %collective-permute-start.6) | collective-permute-done | bytes 65568 | tf_op jit(solution)/shard_map/ppermute | solution.py:580
  17.0 1.6 %collective-permute-start.9 = (bf16[4,128,256]{2,1,0:T(8,128)(2,1)S(1)}, bf16[4,128,256]{2,1,0:T(8,128)(2,1)S(1)}, u32[]{:S(2)}, u32[]{:S(2)}) collective-permute-start(bf16[4,128,256]{2,1,0:T(8,128)(2,1)S(1)} %shard_map.142.rest_0_), channel_id=1, source_target_pairs={{0,2},{1,3},{2,0},{3,1},{4,6},{5,7},{6,4},{7,5},{8,10},{9,11},{10,... | collective-permute-start | bytes 786440 | tf_op jit(solution)/shard_map/ppermute | solution.py:580
  18.6 0.5 shard_map.139
  19.1 0.6 collective-permute-start.1
  19.7 1.2 %collective-permute-start.2 = (bf16[272,256]{1,0:T(8,128)(2,1)S(1)}, bf16[272,256]{1,0:T(8,128)(2,1)S(1)}, u32[]{:S(2)}, u32[]{:S(2)}) collective-permute-start(bf16[272,256]{1,0:T(8,128)(2,1)S(1)} %get-tuple-element.80), channel_id=1, source_target_pairs={{0,4},{1,5},{2,6},{3,7},{4,0},{5,1},{6,2},{7,3},{8,12},{9,13},{10,... | collective-permute-start | bytes 417800 | tf_op jit(solution)/shard_map/ppermute | solution.py:580
  20.9 1.8 %collective-permute-start.3 = (bf16[272,256]{1,0:T(8,128)(2,1)S(1)}, bf16[272,256]{1,0:T(8,128)(2,1)S(1)}, u32[]{:S(2)}, u32[]{:S(2)}) collective-permute-start(bf16[272,256]{1,0:T(8,128)(2,1)S(1)} %get-tuple-element.81), channel_id=1, source_target_pairs={{0,6},{1,7},{2,4},{3,5},{4,2},{5,3},{6,0},{7,1},{8,14},{9,15},{10,... | collective-permute-start | bytes 417800 | tf_op jit(solution)/shard_map/ppermute | solution.py:580
  22.7 0.9 copy-done.6
  23.6 0.9 copy-done.7
  24.6 0.1 shard_map.141
  24.7 4.5 %collective-permute-done.9.rest_2_ = bf16[4,128,256]{2,1,0:T(8,128)(2,1)S(1)} collective-permute-done((bf16[4,128,256]{2,1,0:T(8,128)(2,1)S(1)}, bf16[4,128,256]{2,1,0:T(8,128)(2,1)S(1)}, u32[]{:S(2)}, u32[]{:S(2)}) %collective-permute-start.9) | collective-permute-done | bytes 262176 | tf_op jit(solution)/shard_map/ppermute | solution.py:580
  29.3 1.6 %collective-permute-done.1.rest_1_ = bf16[272,256]{1,0:T(8,128)(2,1)S(1)} collective-permute-done((bf16[272,256]{1,0:T(8,128)(2,1)S(1)}, bf16[272,256]{1,0:T(8,128)(2,1)S(1)}, u32[]{:S(2)}, u32[]{:S(2)}) %collective-permute-start.1) | collective-permute-done | bytes 139296 | tf_op jit(solution)/shard_map/ppermute | solution.py:580
  30.9 0.2 shard_map.140
  31.1 2.8 %collective-permute-start.4 = (bf16[256,256]{1,0:T(8,128)(2,1)S(1)}, bf16[256,256]{1,0:T(8,128)(2,1)S(1)}, u32[]{:S(2)}, u32[]{:S(2)}) collective-permute-start(bf16[256,256]{1,0:T(8,128)(2,1)S(1)} %shard_map.140), channel_id=1, source_target_pairs={{0,8},{1,9},{2,10},{3,11},{4,12},{5,13},{6,14},{7,15},{16,24},{17,... | collective-permute-start | bytes 393224 | tf_op jit(solution)/shard_map/ppermute | solution.py:628
  34.1 5.0 %shard_map.143 = (bf16[8,160,256]{2,1,0:T(8,128)(2,1)S(1)}, bf16[8,160,256]{2,1,0:T(8,128)(2,1)S(1)}) custom-call(s32[1]{0:T(128)} %bitcast.me_ref, bf16[4,256,128]{2,1,0:T(8,128)(2,1)S(1)} %get-tuple-element.83.query_ref, bf16[4,256,128]{2,1,0:T(8,128)(2,1)S(1)} %get-tuple-element.84.grad_ref, bf16[4,128,256]{2,1,0:T(8,128)(2,1)S(1)} %shard_map.142.rest_0_, ...), custom_call_target="tpu_custom_call" | custom-call | flops 2684354560 | bytes 2883588 | tf_op jit(solution)/shard_map/pallas_call | solution.py:45
  39.1 0.3 collective-permute-start.14
  39.4 0.3 shard_map.144
  39.7 1.6 %collective-permute-start.11 = (bf16[256,256]{1,0:T(8,128)(2,1)S(1)}, bf16[256,256]{1,0:T(8,128)(2,1)S(1)}, u32[]{:S(2)}, u32[]{:S(2)}) collective-permute-start(bf16[256,256]{1,0:T(8,128)(2,1)S(1)} %get-tuple-element.90), channel_id=1, source_target_pairs={{0,2},{1,3},{2,0},{3,1},{4,6},{5,7},{6,4},{7,5},{8,10},{9,11},{10,... | collective-permute-start | bytes 393224 | tf_op jit(solution)/shard_map/ppermute | solution.py:580
  41.3 2.4 %collective-permute-start.12 = (bf16[256,256]{1,0:T(8,128)(2,1)S(1)}, bf16[256,256]{1,0:T(8,128)(2,1)S(1)}, u32[]{:S(2)}, u32[]{:S(2)}) collective-permute-start(bf16[256,256]{1,0:T(8,128)(2,1)S(1)} %get-tuple-element.91), channel_id=1, source_target_pairs={{0,4},{1,5},{2,6},{3,7},{4,0},{5,1},{6,2},{7,3},{8,12},{9,13},{10,... | collective-permute-start | bytes 393224 | tf_op jit(solution)/shard_map/ppermute | solution.py:580
  43.6 0.1 shard_map.145
  43.8 4.6 %collective-permute-start.15 = (bf16[192,256]{1,0:T(8,128)(2,1)S(1)}, bf16[192,256]{1,0:T(8,128)(2,1)S(1)}, u32[]{:S(2)}, u32[]{:S(2)}) collective-permute-start(bf16[192,256]{1,0:T(8,128)(2,1)S(1)} %get-tuple-element.96), channel_id=1, source_target_pairs={{0,12},{1,13},{2,14},{3,15},{4,8},{5,9},{6,10},{7,11},{8,4},{9,5},... | collective-permute-start | bytes 294920 | tf_op jit(solution)/shard_map/ppermute | solution.py:580
  48.4 3.1 %collective-permute-start.17 = (bf16[192,256]{1,0:T(8,128)(2,1)S(1)}, bf16[192,256]{1,0:T(8,128)(2,1)S(1)}, u32[]{:S(2)}, u32[]{:S(2)}) collective-permute-start(bf16[192,256]{1,0:T(8,128)(2,1)S(1)} %get-tuple-element.98), channel_id=1, source_target_pairs={{0,14},{1,15},{2,12},{3,13},{4,10},{5,11},{6,8},{7,9},{8,6},{9,7},... | collective-permute-start | bytes 294920 | tf_op jit(solution)/shard_map/ppermute | solution.py:580
  51.5 4.0 %collective-permute-done.15.rest_0_ = bf16[192,256]{1,0:T(8,128)(2,1)S(1)} collective-permute-done((bf16[192,256]{1,0:T(8,128)(2,1)S(1)}, bf16[192,256]{1,0:T(8,128)(2,1)S(1)}, u32[]{:S(2)}, u32[]{:S(2)}) %collective-permute-start.15) | collective-permute-done | bytes 98336 | tf_op jit(solution)/shard_map/ppermute | solution.py:580
  55.5 5.2 %collective-permute-done.16.rest_1_ = bf16[192,256]{1,0:T(8,128)(2,1)S(1)} collective-permute-done((bf16[192,256]{1,0:T(8,128)(2,1)S(1)}, bf16[192,256]{1,0:T(8,128)(2,1)S(1)}, u32[]{:S(2)}, u32[]{:S(2)}) %collective-permute-start.16) | collective-permute-done | bytes 98336 | tf_op jit(solution)/shard_map/ppermute | solution.py:580
  60.7 0.6 shard_map.146
  61.4 2.4 %collective-permute-start.19 = (bf16[192,256]{1,0:T(8,128)(2,1)S(1)}, bf16[192,256]{1,0:T(8,128)(2,1)S(1)}, u32[]{:S(2)}, u32[]{:S(2)}) collective-permute-start(bf16[192,256]{1,0:T(8,128)(2,1)S(1)} %get-tuple-element.108), channel_id=1, source_target_pairs={{0,10},{1,11},{2,8},{3,9},{4,14},{5,15},{6,12},{7,13},{8,2},{9,3},... | collective-permute-start | bytes 294920 | tf_op jit(solution)/shard_map/ppermute | solution.py:580
  63.8 0.3 collective-permute-start.20
  64.1 2.7 %collective-permute-start.21 = (bf16[192,256]{1,0:T(8,128)(2,1)S(1)}, bf16[192,256]{1,0:T(8,128)(2,1)S(1)}, u32[]{:S(2)}, u32[]{:S(2)}) collective-permute-start(bf16[192,256]{1,0:T(8,128)(2,1)S(1)} %get-tuple-element.111), channel_id=1, source_target_pairs={{0,6},{1,7},{2,4},{3,5},{4,2},{5,3},{6,0},{7,1},{8,14},{9,15},{10,... | collective-permute-start | bytes 294920 | tf_op jit(solution)/shard_map/ppermute | solution.py:580
  66.7 0.6 collective-permute-start.22
  67.3 1.6 %shard_map.147 = (f32[128,2048]{1,0:T(8,128)S(1)}, f32[128,128]{1,0:T(8,128)S(1)}, f32[128,2048]{1,0:T(8,128)S(1)}, f32[128,2048]{1,0:T(8,128)S(1)}) custom-call(s32[1]{0:T(128)} %bitcast.me_ref, bf16[128,2048]{1,0:T(8,128)(2,1)S(1)} %copy-done.1, bf16[128,256]{1,0:T(8,128)(2,1)S(1)} %copy-done.3, bf16[128,256]{1,0:T(8,128)(2,1)S(1)} %copy-done.4, ...), custom_call_target="tpu_custom_call" | custom-call | flops 201326592 | bytes 6520836 | tf_op jit(solution)/shard_map/pallas_call | solution.py:45
  68.9 1.2 %collective-permute-done.19.rest_3_ = bf16[192,256]{1,0:T(8,128)(2,1)S(1)} collective-permute-done((bf16[192,256]{1,0:T(8,128)(2,1)S(1)}, bf16[192,256]{1,0:T(8,128)(2,1)S(1)}, u32[]{:S(2)}, u32[]{:S(2)}) %collective-permute-start.19) | collective-permute-done | bytes 98336 | tf_op jit(solution)/shard_map/ppermute | solution.py:580
  70.1 2.6 %collective-permute-done.21.rest_6_ = bf16[192,256]{1,0:T(8,128)(2,1)S(1)} collective-permute-done((bf16[192,256]{1,0:T(8,128)(2,1)S(1)}, bf16[192,256]{1,0:T(8,128)(2,1)S(1)}, u32[]{:S(2)}, u32[]{:S(2)}) %collective-permute-start.21) | collective-permute-done | bytes 98336 | tf_op jit(solution)/shard_map/ppermute | solution.py:580
  72.7 0.7 collective-permute-done.22.rest_7_
  73.5 2.8 %shard_map.148 = (f32[128,2048]{1,0:T(8,128)S(1)}, bf16[128,2048]{1,0:T(8,128)(2,1)S(1)}, bf16[1024,256]{1,0:T(8,128)(2,1)S(1)}, bf16[1040,256]{1,0:T(8,128)(2,1)S(1)}, bf16[128,2048]{1,0:T(8,128)(2,1)S(1)}) custom-call(s32[1]{0:T(128)} %bitcast.me_ref, bf16[2048,1280]{1,0:T(8,128)(2,1)S(1)} %bitcast.4, f32[128,2048]{1,0:T(8,128)S(1)} %get-tuple-element.105.gated_ref, ...), custom_call_target="tpu_custom_call" | custom-call | flops 805306368 | bytes 12484612 | tf_op jit(solution)/shard_map/pallas_call | solution.py:45
  76.4 1.9 %collective-permute-done.23.got_ref = bf16[1040,256]{1,0:T(8,128)(2,1)S(1)} collective-permute-done((bf16[1040,256]{1,0:T(8,128)(2,1)S(1)}, bf16[1040,256]{1,0:T(8,128)(2,1)S(1)}, u32[]{:S(2)}, u32[]{:S(2)}) %collective-permute-start.23) | collective-permute-done | bytes 532512 | tf_op jit(solution)/shard_map/ppermute | solution.py:580
  78.3 0.5 shard_map.150
  78.8 1.2 %collective-permute-start.24 = (bf16[272,256]{1,0:T(8,128)(2,1)S(1)}, bf16[272,256]{1,0:T(8,128)(2,1)S(1)}, u32[]{:S(2)}, u32[]{:S(2)}) collective-permute-start(bf16[272,256]{1,0:T(8,128)(2,1)S(1)} %get-tuple-element.124), channel_id=1, source_target_pairs={{0,2},{1,3},{2,0},{3,1},{4,6},{5,7},{6,4},{7,5},{8,10},{9,11},{10,... | collective-permute-start | bytes 417800 | tf_op jit(solution)/shard_map/ppermute | solution.py:580
  80.0 1.2 %collective-permute-start.25 = (bf16[272,256]{1,0:T(8,128)(2,1)S(1)}, bf16[272,256]{1,0:T(8,128)(2,1)S(1)}, u32[]{:S(2)}, u32[]{:S(2)}) collective-permute-start(bf16[272,256]{1,0:T(8,128)(2,1)S(1)} %get-tuple-element.125), channel_id=1, source_target_pairs={{0,4},{1,5},{2,6},{3,7},{4,0},{5,1},{6,2},{7,3},{8,12},{9,13},{10,... | collective-permute-start | bytes 417800 | tf_op jit(solution)/shard_map/ppermute | solution.py:580
  81.2 1.1 %collective-permute-start.26 = (bf16[272,256]{1,0:T(8,128)(2,1)S(1)}, bf16[272,256]{1,0:T(8,128)(2,1)S(1)}, u32[]{:S(2)}, u32[]{:S(2)}) collective-permute-start(bf16[272,256]{1,0:T(8,128)(2,1)S(1)} %get-tuple-element.126), channel_id=1, source_target_pairs={{0,6},{1,7},{2,4},{3,5},{4,2},{5,3},{6,0},{7,1},{8,14},{9,15},{10,... | collective-permute-start | bytes 417800 | tf_op jit(solution)/shard_map/ppermute | solution.py:580
  82.3 2.2 %collective-permute-done.24.rest_1_ = bf16[272,256]{1,0:T(8,128)(2,1)S(1)} collective-permute-done((bf16[272,256]{1,0:T(8,128)(2,1)S(1)}, bf16[272,256]{1,0:T(8,128)(2,1)S(1)}, u32[]{:S(2)}, u32[]{:S(2)}) %collective-permute-start.24) | collective-permute-done | bytes 139296 | tf_op jit(solution)/shard_map/ppermute | solution.py:580
  84.6 2.0 %collective-permute-done.25.rest_2_ = bf16[272,256]{1,0:T(8,128)(2,1)S(1)} collective-permute-done((bf16[272,256]{1,0:T(8,128)(2,1)S(1)}, bf16[272,256]{1,0:T(8,128)(2,1)S(1)}, u32[]{:S(2)}, u32[]{:S(2)}) %collective-permute-start.25) | collective-permute-done | bytes 139296 | tf_op jit(solution)/shard_map/ppermute | solution.py:580
  86.6 2.2 %collective-permute-done.26.rest_3_ = bf16[272,256]{1,0:T(8,128)(2,1)S(1)} collective-permute-done((bf16[272,256]{1,0:T(8,128)(2,1)S(1)}, bf16[272,256]{1,0:T(8,128)(2,1)S(1)}, u32[]{:S(2)}, u32[]{:S(2)}) %collective-permute-start.26) | collective-permute-done | bytes 139296 | tf_op jit(solution)/shard_map/ppermute | solution.py:580
  88.8 0.2 shard_map.151
  89.0 1.5 %collective-permute-start.27 = (bf16[256,256]{1,0:T(8,128)(2,1)S(1)}, bf16[256,256]{1,0:T(8,128)(2,1)S(1)}, u32[]{:S(2)}, u32[]{:S(2)}) collective-permute-start(bf16[256,256]{1,0:T(8,128)(2,1)S(1)} %shard_map.151), channel_id=1, source_target_pairs={{8,0},{9,1},{10,2},{11,3},{12,4},{13,5},{14,6},{15,7},{24,16},{25,... | collective-permute-start | bytes 393224 | tf_op jit(solution)/shard_map/ppermute | solution.py:628
  90.5 2.8 %shard_map.149 = (f32[128,2048]{1,0:T(8,128)S(1)}, f32[128,256]{1,0:T(8,128)S(1)}, f32[128,256]{1,0:T(8,128)}, f32[128,2048]{1,0:T(8,128)}) custom-call(s32[1]{0:T(128)} %bitcast.me_ref, bf16[128,2048]{1,0:T(8,128)(2,1)S(1)} %get-tuple-element.113.grad_ref, bf16[128,2048]{1,0:T(8,128)(2,1)S(1)} %get-tuple-element.114.grown_ref, ...), custom_call_target="tpu_custom_call" | custom-call | flops 268435456 | bytes 7241732 | tf_op jit(solution)/shard_map/pallas_call | solution.py:45
  93.4 5.7 %collective-permute-done.27.carry_ref = bf16[256,256]{1,0:T(8,128)(2,1)S(1)} collective-permute-done((bf16[256,256]{1,0:T(8,128)(2,1)S(1)}, bf16[256,256]{1,0:T(8,128)(2,1)S(1)}, u32[]{:S(2)}, u32[]{:S(2)}) %collective-permute-start.27) | collective-permute-done | bytes 131104 | tf_op jit(solution)/shard_map/ppermute | solution.py:628
  99.0 0.3 shard_map.152
  99.3 1.1 %collective-permute-start.28 = (bf16[256,256]{1,0:T(8,128)(2,1)S(1)}, bf16[256,256]{1,0:T(8,128)(2,1)S(1)}, u32[]{:S(2)}, u32[]{:S(2)}) collective-permute-start(bf16[256,256]{1,0:T(8,128)(2,1)S(1)} %get-tuple-element.129), channel_id=1, source_target_pairs={{0,2},{1,3},{2,0},{3,1},{4,6},{5,7},{6,4},{7,5},{8,10},{9,11},{10,... | collective-permute-start | bytes 393224 | tf_op jit(solution)/shard_map/ppermute | solution.py:580
  100.5 2.4 %collective-permute-start.30 = (bf16[256,256]{1,0:T(8,128)(2,1)S(1)}, bf16[256,256]{1,0:T(8,128)(2,1)S(1)}, u32[]{:S(2)}, u32[]{:S(2)}) collective-permute-start(bf16[256,256]{1,0:T(8,128)(2,1)S(1)} %get-tuple-element.131), channel_id=1, source_target_pairs={{0,6},{1,7},{2,4},{3,5},{4,2},{5,3},{6,0},{7,1},{8,14},{9,15},{10,... | collective-permute-start | bytes 393224 | tf_op jit(solution)/shard_map/ppermute | solution.py:580
  102.9 2.9 %collective-permute-done.28.rest_1_ = bf16[256,256]{1,0:T(8,128)(2,1)S(1)} collective-permute-done((bf16[256,256]{1,0:T(8,128)(2,1)S(1)}, bf16[256,256]{1,0:T(8,128)(2,1)S(1)}, u32[]{:S(2)}, u32[]{:S(2)}) %collective-permute-start.28) | collective-permute-done | bytes 131104 | tf_op jit(solution)/shard_map/ppermute | solution.py:580
  105.8 0.6 collective-permute-done.29.rest_2_
  106.4 1.2 %collective-permute-done.30.rest_3_ = bf16[256,256]{1,0:T(8,128)(2,1)S(1)} collective-permute-done((bf16[256,256]{1,0:T(8,128)(2,1)S(1)}, bf16[256,256]{1,0:T(8,128)(2,1)S(1)}, u32[]{:S(2)}, u32[]{:S(2)}) %collective-permute-start.30) | collective-permute-done | bytes 131104 | tf_op jit(solution)/shard_map/ppermute | solution.py:580
  107.6 0.6 shard_map.153
  108.3 0.4 shard_map.154
  108.7 1.5 %collective-permute-done.31.other_ref = bf16[1024,256]{1,0:T(8,128)(2,1)S(1)} collective-permute-done((bf16[1024,256]{1,0:T(8,128)(2,1)S(1)}, bf16[1024,256]{1,0:T(8,128)(2,1)S(1)}, u32[]{:S(2)}, u32[]{:S(2)}) %collective-permute-start.31) | collective-permute-done | bytes 524320 | tf_op jit(solution)/shard_map/ppermute | solution.py:580
  110.2 1.4 %shard_map.155 = (f32[128,2048]{1,0:T(8,128)}, f32[128,256]{1,0:T(8,128)}) custom-call(s32[1]{0:T(128)} %bitcast.me_ref, f32[128,2048]{1,0:T(8,128)S(1)} %get-tuple-element.117.value_ref, f32[128,256]{1,0:T(8,128)S(1)} %get-tuple-element.118.write_part_ref, f32[128,1024]{1,0:T(8,128)S(1)} %get-tuple-element.133.half_ref, ...), custom_call_target="tpu_custom_call" | custom-call | flops 134217728 | bytes 5177348 | tf_op jit(solution)/shard_map/pallas_call | solution.py:45
  (44 shorter events, 0.4 us)
Async XLA Ops:
  1.4 1.0 copy-start
  2.5 0.8 copy-start.2
  3.3 0.7 copy-start.8
  5.7 12.9 %collective-permute-start = (bf16[1040,256]{1,0:T(8,128)(2,1)S(1)}, bf16[1040,256]{1,0:T(8,128)(2,1)S(1)}, u32[]{:S(2)}, u32[]{:S(2)}) collective-permute-start(bf16[1040,256]{1,0:T(8,128)(2,1)S(1)} %get-tuple-element.77), channel_id=1, source_target_pairs={{0,1},{1,0},{2,3},{3,2},{4,5},{5,4},{6,7},{7,6},{8,9},{9,8},{10,11... | collective-permute-start | bytes 1597448 | tf_op jit(solution)/shard_map/ppermute | solution.py:580
  6.2 7.5 %collective-permute-start.7 = (bf16[128,256]{1,0:T(8,128)(2,1)S(1)}, bf16[128,256]{1,0:T(8,128)(2,1)S(1)}, u32[]{:S(2)}, u32[]{:S(2)}) collective-permute-start(bf16[128,256]{1,0:T(8,128)(2,1)S(1)} %pad_add_fusion.refs_0_), channel_id=1, source_target_pairs={{0,12},{1,13},{2,14},{3,15},{4,8},{5,9},{6,10},{7,11},{8,4},{9,5},... | collective-permute-start | bytes 196616 | tf_op jit(solution)/shard_map/ppermute | solution.py:580
  10.9 6.1 %collective-permute-start.6 = (bf16[128,256]{1,0:T(8,128)(2,1)S(1)}, bf16[128,256]{1,0:T(8,128)(2,1)S(1)}, u32[]{:S(2)}, u32[]{:S(2)}) collective-permute-start(bf16[128,256]{1,0:T(8,128)(2,1)S(1)} %pad_add_fusion.refs_0_), channel_id=1, source_target_pairs={{0,8},{1,9},{2,10},{3,11},{4,12},{5,13},{6,14},{7,15},{8,0},{9,1},... | collective-permute-start | bytes 196616 | tf_op jit(solution)/shard_map/ppermute | solution.py:580
  10.9 6.1 %collective-permute-start.5 = (bf16[128,256]{1,0:T(8,128)(2,1)S(1)}, bf16[128,256]{1,0:T(8,128)(2,1)S(1)}, u32[]{:S(2)}, u32[]{:S(2)}) collective-permute-start(bf16[128,256]{1,0:T(8,128)(2,1)S(1)} %pad_add_fusion.refs_0_), channel_id=1, source_target_pairs={{0,4},{1,5},{2,6},{3,7},{4,0},{5,1},{6,2},{7,3},{8,12},{9,13},{10,... | collective-permute-start | bytes 196616 | tf_op jit(solution)/shard_map/ppermute | solution.py:580
  17.0 12.3 %collective-permute-start.9 = (bf16[4,128,256]{2,1,0:T(8,128)(2,1)S(1)}, bf16[4,128,256]{2,1,0:T(8,128)(2,1)S(1)}, u32[]{:S(2)}, u32[]{:S(2)}) collective-permute-start(bf16[4,128,256]{2,1,0:T(8,128)(2,1)S(1)} %shard_map.142.rest_0_), channel_id=1, source_target_pairs={{0,2},{1,3},{2,0},{3,1},{4,6},{5,7},{6,4},{7,5},{8,10},{9,11},{10,... | collective-permute-start | bytes 786440 | tf_op jit(solution)/shard_map/ppermute | solution.py:580
  19.1 11.8 %collective-permute-start.1 = (bf16[272,256]{1,0:T(8,128)(2,1)S(1)}, bf16[272,256]{1,0:T(8,128)(2,1)S(1)}, u32[]{:S(2)}, u32[]{:S(2)}) collective-permute-start(bf16[272,256]{1,0:T(8,128)(2,1)S(1)} %get-tuple-element.79), channel_id=1, source_target_pairs={{0,2},{1,3},{2,0},{3,1},{4,6},{5,7},{6,4},{7,5},{8,10},{9,11},{10,... | collective-permute-start | bytes 417800 | tf_op jit(solution)/shard_map/ppermute | solution.py:580
  19.7 11.2 %collective-permute-start.2 = (bf16[272,256]{1,0:T(8,128)(2,1)S(1)}, bf16[272,256]{1,0:T(8,128)(2,1)S(1)}, u32[]{:S(2)}, u32[]{:S(2)}) collective-permute-start(bf16[272,256]{1,0:T(8,128)(2,1)S(1)} %get-tuple-element.80), channel_id=1, source_target_pairs={{0,4},{1,5},{2,6},{3,7},{4,0},{5,1},{6,2},{7,3},{8,12},{9,13},{10,... | collective-permute-start | bytes 417800 | tf_op jit(solution)/shard_map/ppermute | solution.py:580
  20.9 10.0 %collective-permute-start.3 = (bf16[272,256]{1,0:T(8,128)(2,1)S(1)}, bf16[272,256]{1,0:T(8,128)(2,1)S(1)}, u32[]{:S(2)}, u32[]{:S(2)}) collective-permute-start(bf16[272,256]{1,0:T(8,128)(2,1)S(1)} %get-tuple-element.81), channel_id=1, source_target_pairs={{0,6},{1,7},{2,4},{3,5},{4,2},{5,3},{6,0},{7,1},{8,14},{9,15},{10,... | collective-permute-start | bytes 417800 | tf_op jit(solution)/shard_map/ppermute | solution.py:580
  22.7 0.9 copy-start.6
  23.6 0.9 copy-start.7
  24.6 9.3 %collective-permute-start.8 = (bf16[4,128,256]{2,1,0:T(8,128)(2,1)S(1)}, bf16[4,128,256]{2,1,0:T(8,128)(2,1)S(1)}, u32[]{:S(2)}, u32[]{:S(2)}) collective-permute-start(bf16[4,128,256]{2,1,0:T(8,128)(2,1)S(1)} %shard_map.142.rest_0_), channel_id=1, source_target_pairs={{0,1},{1,0},{2,3},{3,2},{4,5},{5,4},{6,7},{7,6},{8,9},{9,8},{10,11... | collective-permute-start | bytes 786440 | tf_op jit(solution)/shard_map/ppermute | solution.py:580
  30.9 3.1 %collective-permute-start.10 = (bf16[4,128,256]{2,1,0:T(8,128)(2,1)S(1)}, bf16[4,128,256]{2,1,0:T(8,128)(2,1)S(1)}, u32[]{:S(2)}, u32[]{:S(2)}) collective-permute-start(bf16[4,128,256]{2,1,0:T(8,128)(2,1)S(1)} %collective-permute-done.9.rest_2_), channel_id=1, source_target_pairs={{0,1},{1,0},{2,3},{3,2},{4,5},{5,4},{6,7},{7,6},{8,9},{9,8},{10,11... | collective-permute-start | bytes 786440 | tf_op jit(solution)/shard_map/ppermute | solution.py:580
  31.1 8.0 %collective-permute-start.4 = (bf16[256,256]{1,0:T(8,128)(2,1)S(1)}, bf16[256,256]{1,0:T(8,128)(2,1)S(1)}, u32[]{:S(2)}, u32[]{:S(2)}) collective-permute-start(bf16[256,256]{1,0:T(8,128)(2,1)S(1)} %shard_map.140), channel_id=1, source_target_pairs={{0,8},{1,9},{2,10},{3,11},{4,12},{5,13},{6,14},{7,15},{16,24},{17,... | collective-permute-start | bytes 393224 | tf_op jit(solution)/shard_map/ppermute | solution.py:628
  34.0 39.5 %slice-start = ((s8[5242880]{0:T(1024)(128)(4,1)}), s8[4194304]{0:T(1024)(128)(4,1)S(1)}, s32[]{:S(2)}) async-start(s8[5242880]{0:T(1024)(128)(4,1)} %bitcast.3), calls=%async_computation | async-start | bytes 8388608
  34.0 33.3 %copy-start.1 = (bf16[128,2048]{1,0:T(8,128)(2,1)S(1)}, bf16[128,2048]{1,0:T(8,128)(2,1)}, u32[]{:S(2)}) copy-start(bf16[128,2048]{1,0:T(8,128)(2,1)} %input_ref.5) | copy-start | bytes 1572868
  34.0 33.3 %copy-start.3 = (bf16[128,256]{1,0:T(8,128)(2,1)S(1)}, bf16[128,256]{1,0:T(8,128)(2,1)}, u32[]{:S(2)}) copy-start(bf16[128,256]{1,0:T(8,128)(2,1)} %write_ref.9) | copy-start | bytes 196612
  34.0 33.3 %copy-start.4 = (bf16[128,256]{1,0:T(8,128)(2,1)S(1)}, bf16[128,256]{1,0:T(8,128)(2,1)}, u32[]{:S(2)}) copy-start(bf16[128,256]{1,0:T(8,128)(2,1)} %read_ref.5) | copy-start | bytes 196612
  34.0 33.3 %copy-start.5 = (bf16[128,2048]{1,0:T(8,128)(2,1)S(1)}, bf16[128,2048]{1,0:T(8,128)(2,1)}, u32[]{:S(2)}) copy-start(bf16[128,2048]{1,0:T(8,128)(2,1)} %gate_ref.1) | copy-start | bytes 1572868
  34.1 39.4 %slice-start.1 = ((s8[5242880]{0:T(1024)(128)(4,1)}), s8[1048576]{0:T(1024)(128)(4,1)S(1)}, s32[]{:S(2)}) async-start(s8[5242880]{0:T(1024)(128)(4,1)} %bitcast.3), calls=%async_computation.1 | async-start | bytes 2097152
  39.1 34.4 %copy-start.9 = (f32[2048]{0:T(1024)S(1)}, f32[2048]{0:T(1024)}, u32[]{:S(2)}) copy-start(f32[2048]{0:T(1024)} %param.20) | copy-start | bytes 24580
  39.1 4.5 %collective-permute-start.14 = (bf16[8,160,256]{2,1,0:T(8,128)(2,1)S(1)}, bf16[8,160,256]{2,1,0:T(8,128)(2,1)S(1)}, u32[]{:S(2)}, u32[]{:S(2)}) collective-permute-start(bf16[8,160,256]{2,1,0:T(8,128)(2,1)S(1)} %get-tuple-element.94), channel_id=1, source_target_pairs={{0,1},{1,0},{2,3},{3,2},{4,5},{5,4},{6,7},{7,6},{8,9},{9,8},{10,11... | collective-permute-start | bytes 1966088 | tf_op jit(solution)/shard_map/ppermute | solution.py:580
  39.7 8.7 %collective-permute-start.11 = (bf16[256,256]{1,0:T(8,128)(2,1)S(1)}, bf16[256,256]{1,0:T(8,128)(2,1)S(1)}, u32[]{:S(2)}, u32[]{:S(2)}) collective-permute-start(bf16[256,256]{1,0:T(8,128)(2,1)S(1)} %get-tuple-element.90), channel_id=1, source_target_pairs={{0,2},{1,3},{2,0},{3,1},{4,6},{5,7},{6,4},{7,5},{8,10},{9,11},{10,... | collective-permute-start | bytes 393224 | tf_op jit(solution)/shard_map/ppermute | solution.py:580
  41.3 10.2 %collective-permute-start.12 = (bf16[256,256]{1,0:T(8,128)(2,1)S(1)}, bf16[256,256]{1,0:T(8,128)(2,1)S(1)}, u32[]{:S(2)}, u32[]{:S(2)}) collective-permute-start(bf16[256,256]{1,0:T(8,128)(2,1)S(1)} %get-tuple-element.91), channel_id=1, source_target_pairs={{0,4},{1,5},{2,6},{3,7},{4,0},{5,1},{6,2},{7,3},{8,12},{9,13},{10,... | collective-permute-start | bytes 393224 | tf_op jit(solution)/shard_map/ppermute | solution.py:580
  43.6 7.9 %collective-permute-start.13 = (bf16[256,256]{1,0:T(8,128)(2,1)S(1)}, bf16[256,256]{1,0:T(8,128)(2,1)S(1)}, u32[]{:S(2)}, u32[]{:S(2)}) collective-permute-start(bf16[256,256]{1,0:T(8,128)(2,1)S(1)} %get-tuple-element.92), channel_id=1, source_target_pairs={{0,6},{1,7},{2,4},{3,5},{4,2},{5,3},{6,0},{7,1},{8,14},{9,15},{10,... | collective-permute-start | bytes 393224 | tf_op jit(solution)/shard_map/ppermute | solution.py:580
  43.8 11.7 %collective-permute-start.15 = (bf16[192,256]{1,0:T(8,128)(2,1)S(1)}, bf16[192,256]{1,0:T(8,128)(2,1)S(1)}, u32[]{:S(2)}, u32[]{:S(2)}) collective-permute-start(bf16[192,256]{1,0:T(8,128)(2,1)S(1)} %get-tuple-element.96), channel_id=1, source_target_pairs={{0,12},{1,13},{2,14},{3,15},{4,8},{5,9},{6,10},{7,11},{8,4},{9,5},... | collective-permute-start | bytes 294920 | tf_op jit(solution)/shard_map/ppermute | solution.py:580
  48.4 12.3 %collective-permute-start.16 = (bf16[192,256]{1,0:T(8,128)(2,1)S(1)}, bf16[192,256]{1,0:T(8,128)(2,1)S(1)}, u32[]{:S(2)}, u32[]{:S(2)}) collective-permute-start(bf16[192,256]{1,0:T(8,128)(2,1)S(1)} %get-tuple-element.97), channel_id=1, source_target_pairs={{0,8},{1,9},{2,10},{3,11},{4,12},{5,13},{6,14},{7,15},{8,0},{9,1},... | collective-permute-start | bytes 294920 | tf_op jit(solution)/shard_map/ppermute | solution.py:580
  48.4 12.3 %collective-permute-start.17 = (bf16[192,256]{1,0:T(8,128)(2,1)S(1)}, bf16[192,256]{1,0:T(8,128)(2,1)S(1)}, u32[]{:S(2)}, u32[]{:S(2)}) collective-permute-start(bf16[192,256]{1,0:T(8,128)(2,1)S(1)} %get-tuple-element.98), channel_id=1, source_target_pairs={{0,14},{1,15},{2,12},{3,13},{4,10},{5,11},{6,8},{7,9},{8,6},{9,7},... | collective-permute-start | bytes 294920 | tf_op jit(solution)/shard_map/ppermute | solution.py:580
  61.3 6.0 %collective-permute-start.18 = (bf16[1024,256]{1,0:T(8,128)(2,1)S(1)}, bf16[1024,256]{1,0:T(8,128)(2,1)S(1)}, u32[]{:S(2)}, u32[]{:S(2)}) collective-permute-start(bf16[1024,256]{1,0:T(8,128)(2,1)S(1)} %get-tuple-element.104), channel_id=1, source_target_pairs={{0,1},{1,0},{2,3},{3,2},{4,5},{5,4},{6,7},{7,6},{8,9},{9,8},{10,11... | collective-permute-start | bytes 1572872 | tf_op jit(solution)/shard_map/ppermute | solution.py:580
  61.4 8.8 %collective-permute-start.19 = (bf16[192,256]{1,0:T(8,128)(2,1)S(1)}, bf16[192,256]{1,0:T(8,128)(2,1)S(1)}, u32[]{:S(2)}, u32[]{:S(2)}) collective-permute-start(bf16[192,256]{1,0:T(8,128)(2,1)S(1)} %get-tuple-element.108), channel_id=1, source_target_pairs={{0,10},{1,11},{2,8},{3,9},{4,14},{5,15},{6,12},{7,13},{8,2},{9,3},... | collective-permute-start | bytes 294920 | tf_op jit(solution)/shard_map/ppermute | solution.py:580
  63.8 6.3 %collective-permute-start.20 = (bf16[192,256]{1,0:T(8,128)(2,1)S(1)}, bf16[192,256]{1,0:T(8,128)(2,1)S(1)}, u32[]{:S(2)}, u32[]{:S(2)}) collective-permute-start(bf16[192,256]{1,0:T(8,128)(2,1)S(1)} %get-tuple-element.109), channel_id=1, source_target_pairs={{0,4},{1,5},{2,6},{3,7},{4,0},{5,1},{6,2},{7,3},{8,12},{9,13},{10,... | collective-permute-start | bytes 294920 | tf_op jit(solution)/shard_map/ppermute | solution.py:580
  64.1 8.7 %collective-permute-start.21 = (bf16[192,256]{1,0:T(8,128)(2,1)S(1)}, bf16[192,256]{1,0:T(8,128)(2,1)S(1)}, u32[]{:S(2)}, u32[]{:S(2)}) collective-permute-start(bf16[192,256]{1,0:T(8,128)(2,1)S(1)} %get-tuple-element.111), channel_id=1, source_target_pairs={{0,6},{1,7},{2,4},{3,5},{4,2},{5,3},{6,0},{7,1},{8,14},{9,15},{10,... | collective-permute-start | bytes 294920 | tf_op jit(solution)/shard_map/ppermute | solution.py:580
  66.7 6.7 %collective-permute-start.22 = (bf16[192,256]{1,0:T(8,128)(2,1)S(1)}, bf16[192,256]{1,0:T(8,128)(2,1)S(1)}, u32[]{:S(2)}, u32[]{:S(2)}) collective-permute-start(bf16[192,256]{1,0:T(8,128)(2,1)S(1)} %get-tuple-element.112), channel_id=1, source_target_pairs={{0,2},{1,3},{2,0},{3,1},{4,6},{5,7},{6,4},{7,5},{8,10},{9,11},{10,... | collective-permute-start | bytes 294920 | tf_op jit(solution)/shard_map/ppermute | solution.py:580
  76.3 2.0 %collective-permute-start.23 = (bf16[1040,256]{1,0:T(8,128)(2,1)S(1)}, bf16[1040,256]{1,0:T(8,128)(2,1)S(1)}, u32[]{:S(2)}, u32[]{:S(2)}) collective-permute-start(bf16[1040,256]{1,0:T(8,128)(2,1)S(1)} %get-tuple-element.122), channel_id=1, source_target_pairs={{0,1},{1,0},{2,3},{3,2},{4,5},{5,4},{6,7},{7,6},{8,9},{9,8},{10,11... | collective-permute-start | bytes 1597448 | tf_op jit(solution)/shard_map/ppermute | solution.py:580
  78.8 5.8 %collective-permute-start.24 = (bf16[272,256]{1,0:T(8,128)(2,1)S(1)}, bf16[272,256]{1,0:T(8,128)(2,1)S(1)}, u32[]{:S(2)}, u32[]{:S(2)}) collective-permute-start(bf16[272,256]{1,0:T(8,128)(2,1)S(1)} %get-tuple-element.124), channel_id=1, source_target_pairs={{0,2},{1,3},{2,0},{3,1},{4,6},{5,7},{6,4},{7,5},{8,10},{9,11},{10,... | collective-permute-start | bytes 417800 | tf_op jit(solution)/shard_map/ppermute | solution.py:580
  80.0 6.6 %collective-permute-start.25 = (bf16[272,256]{1,0:T(8,128)(2,1)S(1)}, bf16[272,256]{1,0:T(8,128)(2,1)S(1)}, u32[]{:S(2)}, u32[]{:S(2)}) collective-permute-start(bf16[272,256]{1,0:T(8,128)(2,1)S(1)} %get-tuple-element.125), channel_id=1, source_target_pairs={{0,4},{1,5},{2,6},{3,7},{4,0},{5,1},{6,2},{7,3},{8,12},{9,13},{10,... | collective-permute-start | bytes 417800 | tf_op jit(solution)/shard_map/ppermute | solution.py:580
  81.2 7.6 %collective-permute-start.26 = (bf16[272,256]{1,0:T(8,128)(2,1)S(1)}, bf16[272,256]{1,0:T(8,128)(2,1)S(1)}, u32[]{:S(2)}, u32[]{:S(2)}) collective-permute-start(bf16[272,256]{1,0:T(8,128)(2,1)S(1)} %get-tuple-element.126), channel_id=1, source_target_pairs={{0,6},{1,7},{2,4},{3,5},{4,2},{5,3},{6,0},{7,1},{8,14},{9,15},{10,... | collective-permute-start | bytes 417800 | tf_op jit(solution)/shard_map/ppermute | solution.py:580
  89.0 10.0 %collective-permute-start.27 = (bf16[256,256]{1,0:T(8,128)(2,1)S(1)}, bf16[256,256]{1,0:T(8,128)(2,1)S(1)}, u32[]{:S(2)}, u32[]{:S(2)}) collective-permute-start(bf16[256,256]{1,0:T(8,128)(2,1)S(1)} %shard_map.151), channel_id=1, source_target_pairs={{8,0},{9,1},{10,2},{11,3},{12,4},{13,5},{14,6},{15,7},{24,16},{25,... | collective-permute-start | bytes 393224 | tf_op jit(solution)/shard_map/ppermute | solution.py:628
  99.3 6.4 %collective-permute-start.28 = (bf16[256,256]{1,0:T(8,128)(2,1)S(1)}, bf16[256,256]{1,0:T(8,128)(2,1)S(1)}, u32[]{:S(2)}, u32[]{:S(2)}) collective-permute-start(bf16[256,256]{1,0:T(8,128)(2,1)S(1)} %get-tuple-element.129), channel_id=1, source_target_pairs={{0,2},{1,3},{2,0},{3,1},{4,6},{5,7},{6,4},{7,5},{8,10},{9,11},{10,... | collective-permute-start | bytes 393224 | tf_op jit(solution)/shard_map/ppermute | solution.py:580
  100.5 5.9 %collective-permute-start.29 = (bf16[256,256]{1,0:T(8,128)(2,1)S(1)}, bf16[256,256]{1,0:T(8,128)(2,1)S(1)}, u32[]{:S(2)}, u32[]{:S(2)}) collective-permute-start(bf16[256,256]{1,0:T(8,128)(2,1)S(1)} %get-tuple-element.130), channel_id=1, source_target_pairs={{0,4},{1,5},{2,6},{3,7},{4,0},{5,1},{6,2},{7,3},{8,12},{9,13},{10,... | collective-permute-start | bytes 393224 | tf_op jit(solution)/shard_map/ppermute | solution.py:580
  100.5 7.1 %collective-permute-start.30 = (bf16[256,256]{1,0:T(8,128)(2,1)S(1)}, bf16[256,256]{1,0:T(8,128)(2,1)S(1)}, u32[]{:S(2)}, u32[]{:S(2)}) collective-permute-start(bf16[256,256]{1,0:T(8,128)(2,1)S(1)} %get-tuple-element.131), channel_id=1, source_target_pairs={{0,6},{1,7},{2,4},{3,5},{4,2},{5,3},{6,0},{7,1},{8,14},{9,15},{10,... | collective-permute-start | bytes 393224 | tf_op jit(solution)/shard_map/ppermute | solution.py:580
  108.2 2.0 %collective-permute-start.31 = (bf16[1024,256]{1,0:T(8,128)(2,1)S(1)}, bf16[1024,256]{1,0:T(8,128)(2,1)S(1)}, u32[]{:S(2)}, u32[]{:S(2)}) collective-permute-start(bf16[1024,256]{1,0:T(8,128)(2,1)S(1)} %get-tuple-element.135), channel_id=1, source_target_pairs={{0,1},{1,0},{2,3},{3,2},{4,5},{5,4},{6,7},{7,6},{8,9},{9,8},{10,11... | collective-permute-start | bytes 1572872 | tf_op jit(solution)/shard_map/ppermute | solution.py:580

commit v3 on v2

--- a/solution.py
+++ b/solution.py
@@ -714,7 +714,7 @@
     query_tiles, grad_tiles = call(
         stack_kernel, [stacked, stacked], [queries, d_out], rows * wide
     )
-    slices, got = scan_slices(me, cumulated, keep, give, False)
+    slices, got = scan_slices(me, cumulated, keep, tied(give, plane), False)
     parts = scan_parts(slices)
     across = crossed(plane, 2)
     across_other = crossed(tied(across, (tuple(parts[1:]), query_tiles)), 1)

time: 112 us -> 109 us (0.973)
  waiting for transfers between devices: 45.6 us -> 41.6 us
    ppermute x30, waiting for transfers between devices: 39.9 us -> 35.9 us  [crossed(): return lax.ppermute(array, 'ctx', pairs)]
  transfers between devices with their start and end apart: 32 -> 32, of which waited for: 18 -> 18; matrix products, arithmetic and copies ran while one was open for 0% -> 0% of each run, Pallas kernels for 10% -> 12%
where the time goes in v3:
time: 109 us
  waiting for transfers between devices  41.6 us (38%)
  starting transfers between devices  41.5 us (38%)
  Pallas kernels  19.2 us (18%)
  local copies, waits for them, and re-layouts  4.54 us (4%)
    ppermute x30, starting transfers between devices, crossed(): return lax.ppermute(array, 'ctx', pairs)  36.2 us
    ppermute x30, waiting for transfers between devices, crossed(): return lax.ppermute(array, 'ctx', pairs)  35.9 us
    pallas_call x18, Pallas kernels, call(): pl.pallas_call(kernel, out_shape=tuple(outs), in_specs=specs, out_specs=t...  19.2 us
    ppermute x2, waiting for transfers between devices, scan_carry(): return lax.ppermute(total, 'ctx', pairs)  5.67 us
    ppermute x2, starting transfers between devices, scan_carry(): return lax.ppermute(total, 'ctx', pairs)  5.25 us
    unnamed x24, local copies, waits for them, and re-layouts  4.54 us
  transfers between devices with their start and end apart: 32, of which 18 were waited for; matrix products, arithmetic and copies ran while one was open for 0% of the time, Pallas kernels for 12%

profile of v3, /device:TPU:0, one launch (start us, length us, event | category | flops | bytes accessed | tf_op | source)
XLA Modules:
  0.0 108.5 jit_solution(11146038700707321897)
XLA Ops:
  0.6 0.8 pad_add_fusion.refs_0_
  1.4 5.1 %collective-permute-start.2 = (bf16[128,256]{1,0:T(8,128)(2,1)S(1)}, bf16[128,256]{1,0:T(8,128)(2,1)S(1)}, u32[]{:S(2)}, u32[]{:S(2)}) collective-permute-start(bf16[128,256]{1,0:T(8,128)(2,1)S(1)} %pad_add_fusion.refs_0_), channel_id=1, source_target_pairs={{0,12},{1,13},{2,14},{3,15},{4,8},{5,9},{6,10},{7,11},{8,4},{9,5},... | collective-permute-start | bytes 196616 | tf_op jit(solution)/shard_map/ppermute | solution.py:580
  6.5 0.6 collective-permute-start
  7.2 1.0 copy-done
  8.2 0.8 copy-done.2
  9.1 0.7 copy-done.8
  9.8 1.7 %shard_map.138 = (bf16[1024,256]{1,0:T(8,128)(2,1)S(1)}, bf16[1040,256]{1,0:T(8,128)(2,1)S(1)}, bf16[128,2048]{1,0:T(8,128)(2,1)S(1)}, f32[128,2048]{1,0:T(8,128...) custom-call(s32[1]{0:T(128)} %bitcast.me_ref, bf16[128,2048]{1,0:T(8,128)(2,1)S(1)} %copy-done, ...), custom_call_target="tpu_custom_call" | custom-call | flops 134217728 | bytes 4317188 | tf_op jit(solution)/shard_map/pallas_call | solution.py:45
  11.5 0.7 collective-permute-done.1.refs_2_
  12.2 0.1 collective-permute-start.3
  12.2 1.6 %collective-permute-start.9 = (bf16[4,128,256]{2,1,0:T(8,128)(2,1)S(1)}, bf16[4,128,256]{2,1,0:T(8,128)(2,1)S(1)}, u32[]{:S(2)}, u32[]{:S(2)}) collective-permute-start(bf16[4,128,256]{2,1,0:T(8,128)(2,1)S(1)} %shard_map.139.rest_0_), channel_id=1, source_target_pairs={{0,2},{1,3},{2,0},{3,1},{4,6},{5,7},{6,4},{7,5},{8,10},{9,11},{10,... | collective-permute-start | bytes 786440 | tf_op jit(solution)/shard_map/ppermute | solution.py:580
  13.8 0.3 collective-permute-done.3.got_ref
  14.1 0.5 shard_map.140
  14.7 1.6 %collective-permute-start.4 = (bf16[272,256]{1,0:T(8,128)(2,1)S(1)}, bf16[272,256]{1,0:T(8,128)(2,1)S(1)}, u32[]{:S(2)}, u32[]{:S(2)}) collective-permute-start(bf16[272,256]{1,0:T(8,128)(2,1)S(1)} %get-tuple-element.81), channel_id=1, source_target_pairs={{0,2},{1,3},{2,0},{3,1},{4,6},{5,7},{6,4},{7,5},{8,10},{9,11},{10,... | collective-permute-start | bytes 417800 | tf_op jit(solution)/shard_map/ppermute | solution.py:580
  16.2 1.1 collective-permute-start.5
  17.3 0.9 collective-permute-start.6
  18.2 0.9 copy-done.6
  19.2 0.9 copy-done.7
  20.1 0.1 shard_map.142
  20.3 2.0 %collective-permute-done.9.rest_2_ = bf16[4,128,256]{2,1,0:T(8,128)(2,1)S(1)} collective-permute-done((bf16[4,128,256]{2,1,0:T(8,128)(2,1)S(1)}, bf16[4,128,256]{2,1,0:T(8,128)(2,1)S(1)}, u32[]{:S(2)}, u32[]{:S(2)}) %collective-permute-start.9) | collective-permute-done | bytes 262176 | tf_op jit(solution)/shard_map/ppermute | solution.py:580
  22.3 4.6 %collective-permute-done.4.rest_1_ = bf16[272,256]{1,0:T(8,128)(2,1)S(1)} collective-permute-done((bf16[272,256]{1,0:T(8,128)(2,1)S(1)}, bf16[272,256]{1,0:T(8,128)(2,1)S(1)}, u32[]{:S(2)}, u32[]{:S(2)}) %collective-permute-start.4) | collective-permute-done | bytes 139296 | tf_op jit(solution)/shard_map/ppermute | solution.py:580
  26.9 0.2 shard_map.141
  27.2 3.7 %collective-permute-start.7 = (bf16[256,256]{1,0:T(8,128)(2,1)S(1)}, bf16[256,256]{1,0:T(8,128)(2,1)S(1)}, u32[]{:S(2)}, u32[]{:S(2)}) collective-permute-start(bf16[256,256]{1,0:T(8,128)(2,1)S(1)} %shard_map.141), channel_id=1, source_target_pairs={{0,8},{1,9},{2,10},{3,11},{4,12},{5,13},{6,14},{7,15},{16,24},{17,... | collective-permute-start | bytes 393224 | tf_op jit(solution)/shard_map/ppermute | solution.py:628
  31.0 5.0 %shard_map.143 = (bf16[8,160,256]{2,1,0:T(8,128)(2,1)S(1)}, bf16[8,160,256]{2,1,0:T(8,128)(2,1)S(1)}) custom-call(s32[1]{0:T(128)} %bitcast.me_ref, bf16[4,256,128]{2,1,0:T(8,128)(2,1)S(1)} %get-tuple-element.85.query_ref, bf16[4,256,128]{2,1,0:T(8,128)(2,1)S(1)} %get-tuple-element.86.grad_ref, bf16[4,128,256]{2,1,0:T(8,128)(2,1)S(1)} %shard_map.139.rest_0_, ...), custom_call_target="tpu_custom_call" | custom-call | flops 2684354560 | bytes 2883588 | tf_op jit(solution)/shard_map/pallas_call | solution.py:45
  36.1 0.3 collective-permute-start.14
  36.4 0.3 shard_map.144
  36.6 1.6 %collective-permute-start.11 = (bf16[256,256]{1,0:T(8,128)(2,1)S(1)}, bf16[256,256]{1,0:T(8,128)(2,1)S(1)}, u32[]{:S(2)}, u32[]{:S(2)}) collective-permute-start(bf16[256,256]{1,0:T(8,128)(2,1)S(1)} %get-tuple-element.92), channel_id=1, source_target_pairs={{0,2},{1,3},{2,0},{3,1},{4,6},{5,7},{6,4},{7,5},{8,10},{9,11},{10,... | collective-permute-start | bytes 393224 | tf_op jit(solution)/shard_map/ppermute | solution.py:580
  38.2 2.1 %collective-permute-start.12 = (bf16[256,256]{1,0:T(8,128)(2,1)S(1)}, bf16[256,256]{1,0:T(8,128)(2,1)S(1)}, u32[]{:S(2)}, u32[]{:S(2)}) collective-permute-start(bf16[256,256]{1,0:T(8,128)(2,1)S(1)} %get-tuple-element.93), channel_id=1, source_target_pairs={{0,4},{1,5},{2,6},{3,7},{4,0},{5,1},{6,2},{7,3},{8,12},{9,13},{10,... | collective-permute-start | bytes 393224 | tf_op jit(solution)/shard_map/ppermute | solution.py:580
  40.4 0.1 shard_map.145
  40.5 4.8 %collective-permute-start.15 = (bf16[192,256]{1,0:T(8,128)(2,1)S(1)}, bf16[192,256]{1,0:T(8,128)(2,1)S(1)}, u32[]{:S(2)}, u32[]{:S(2)}) collective-permute-start(bf16[192,256]{1,0:T(8,128)(2,1)S(1)} %get-tuple-element.98), channel_id=1, source_target_pairs={{0,12},{1,13},{2,14},{3,15},{4,8},{5,9},{6,10},{7,11},{8,4},{9,5},... | collective-permute-start | bytes 294920 | tf_op jit(solution)/shard_map/ppermute | solution.py:580
  45.3 3.1 %collective-permute-start.17 = (bf16[192,256]{1,0:T(8,128)(2,1)S(1)}, bf16[192,256]{1,0:T(8,128)(2,1)S(1)}, u32[]{:S(2)}, u32[]{:S(2)}) collective-permute-start(bf16[192,256]{1,0:T(8,128)(2,1)S(1)} %get-tuple-element.100), channel_id=1, source_target_pairs={{0,14},{1,15},{2,12},{3,13},{4,10},{5,11},{6,8},{7,9},{8,6},{9,7},... | collective-permute-start | bytes 294920 | tf_op jit(solution)/shard_map/ppermute | solution.py:580
  48.5 4.0 %collective-permute-done.15.rest_0_ = bf16[192,256]{1,0:T(8,128)(2,1)S(1)} collective-permute-done((bf16[192,256]{1,0:T(8,128)(2,1)S(1)}, bf16[192,256]{1,0:T(8,128)(2,1)S(1)}, u32[]{:S(2)}, u32[]{:S(2)}) %collective-permute-start.15) | collective-permute-done | bytes 98336 | tf_op jit(solution)/shard_map/ppermute | solution.py:580
  52.5 5.2 %collective-permute-done.16.rest_1_ = bf16[192,256]{1,0:T(8,128)(2,1)S(1)} collective-permute-done((bf16[192,256]{1,0:T(8,128)(2,1)S(1)}, bf16[192,256]{1,0:T(8,128)(2,1)S(1)}, u32[]{:S(2)}, u32[]{:S(2)}) %collective-permute-start.16) | collective-permute-done | bytes 98336 | tf_op jit(solution)/shard_map/ppermute | solution.py:580
  57.6 0.6 shard_map.146
  58.3 2.4 %collective-permute-start.19 = (bf16[192,256]{1,0:T(8,128)(2,1)S(1)}, bf16[192,256]{1,0:T(8,128)(2,1)S(1)}, u32[]{:S(2)}, u32[]{:S(2)}) collective-permute-start(bf16[192,256]{1,0:T(8,128)(2,1)S(1)} %get-tuple-element.110), channel_id=1, source_target_pairs={{0,10},{1,11},{2,8},{3,9},{4,14},{5,15},{6,12},{7,13},{8,2},{9,3},... | collective-permute-start | bytes 294920 | tf_op jit(solution)/shard_map/ppermute | solution.py:580
  60.7 0.3 collective-permute-start.20
  61.0 2.7 %collective-permute-start.21 = (bf16[192,256]{1,0:T(8,128)(2,1)S(1)}, bf16[192,256]{1,0:T(8,128)(2,1)S(1)}, u32[]{:S(2)}, u32[]{:S(2)}) collective-permute-start(bf16[192,256]{1,0:T(8,128)(2,1)S(1)} %get-tuple-element.113), channel_id=1, source_target_pairs={{0,6},{1,7},{2,4},{3,5},{4,2},{5,3},{6,0},{7,1},{8,14},{9,15},{10,... | collective-permute-start | bytes 294920 | tf_op jit(solution)/shard_map/ppermute | solution.py:580
  63.7 0.6 collective-permute-start.22
  64.3 1.6 %shard_map.147 = (f32[128,2048]{1,0:T(8,128)S(1)}, f32[128,128]{1,0:T(8,128)S(1)}, f32[128,2048]{1,0:T(8,128)S(1)}, f32[128,2048]{1,0:T(8,128)S(1)}) custom-call(s32[1]{0:T(128)} %bitcast.me_ref, bf16[128,2048]{1,0:T(8,128)(2,1)S(1)} %copy-done.1, bf16[128,256]{1,0:T(8,128)(2,1)S(1)} %copy-done.3, bf16[128,256]{1,0:T(8,128)(2,1)S(1)} %copy-done.4, ...), custom_call_target="tpu_custom_call" | custom-call | flops 201326592 | bytes 6520836 | tf_op jit(solution)/shard_map/pallas_call | solution.py:45
  65.9 1.2 %collective-permute-done.19.rest_3_ = bf16[192,256]{1,0:T(8,128)(2,1)S(1)} collective-permute-done((bf16[192,256]{1,0:T(8,128)(2,1)S(1)}, bf16[192,256]{1,0:T(8,128)(2,1)S(1)}, u32[]{:S(2)}, u32[]{:S(2)}) %collective-permute-start.19) | collective-permute-done | bytes 98336 | tf_op jit(solution)/shard_map/ppermute | solution.py:580
  67.1 2.6 %collective-permute-done.21.rest_6_ = bf16[192,256]{1,0:T(8,128)(2,1)S(1)} collective-permute-done((bf16[192,256]{1,0:T(8,128)(2,1)S(1)}, bf16[192,256]{1,0:T(8,128)(2,1)S(1)}, u32[]{:S(2)}, u32[]{:S(2)}) %collective-permute-start.21) | collective-permute-done | bytes 98336 | tf_op jit(solution)/shard_map/ppermute | solution.py:580
  69.7 0.7 collective-permute-done.22.rest_7_
  70.4 2.8 %shard_map.148 = (f32[128,2048]{1,0:T(8,128)S(1)}, bf16[128,2048]{1,0:T(8,128)(2,1)S(1)}, bf16[1024,256]{1,0:T(8,128)(2,1)S(1)}, bf16[1040,256]{1,0:T(8,128)(2,1)S(1)}, bf16[128,2048]{1,0:T(8,128)(2,1)S(1)}) custom-call(s32[1]{0:T(128)} %bitcast.me_ref, bf16[2048,1280]{1,0:T(8,128)(2,1)S(1)} %bitcast.4, f32[128,2048]{1,0:T(8,128)S(1)} %get-tuple-element.107.gated_ref, ...), custom_call_target="tpu_custom_call" | custom-call | flops 805306368 | bytes 12484612 | tf_op jit(solution)/shard_map/pallas_call | solution.py:45
  73.3 1.9 %collective-permute-done.23.got_ref = bf16[1040,256]{1,0:T(8,128)(2,1)S(1)} collective-permute-done((bf16[1040,256]{1,0:T(8,128)(2,1)S(1)}, bf16[1040,256]{1,0:T(8,128)(2,1)S(1)}, u32[]{:S(2)}, u32[]{:S(2)}) %collective-permute-start.23) | collective-permute-done | bytes 532512 | tf_op jit(solution)/shard_map/ppermute | solution.py:580
  75.2 0.5 shard_map.150
  75.7 1.2 %collective-permute-start.24 = (bf16[272,256]{1,0:T(8,128)(2,1)S(1)}, bf16[272,256]{1,0:T(8,128)(2,1)S(1)}, u32[]{:S(2)}, u32[]{:S(2)}) collective-permute-start(bf16[272,256]{1,0:T(8,128)(2,1)S(1)} %get-tuple-element.126), channel_id=1, source_target_pairs={{0,2},{1,3},{2,0},{3,1},{4,6},{5,7},{6,4},{7,5},{8,10},{9,11},{10,... | collective-permute-start | bytes 417800 | tf_op jit(solution)/shard_map/ppermute | solution.py:580
  77.0 1.2 %collective-permute-start.25 = (bf16[272,256]{1,0:T(8,128)(2,1)S(1)}, bf16[272,256]{1,0:T(8,128)(2,1)S(1)}, u32[]{:S(2)}, u32[]{:S(2)}) collective-permute-start(bf16[272,256]{1,0:T(8,128)(2,1)S(1)} %get-tuple-element.127), channel_id=1, source_target_pairs={{0,4},{1,5},{2,6},{3,7},{4,0},{5,1},{6,2},{7,3},{8,12},{9,13},{10,... | collective-permute-start | bytes 417800 | tf_op jit(solution)/shard_map/ppermute | solution.py:580
  78.1 1.1 %collective-permute-start.26 = (bf16[272,256]{1,0:T(8,128)(2,1)S(1)}, bf16[272,256]{1,0:T(8,128)(2,1)S(1)}, u32[]{:S(2)}, u32[]{:S(2)}) collective-permute-start(bf16[272,256]{1,0:T(8,128)(2,1)S(1)} %get-tuple-element.128), channel_id=1, source_target_pairs={{0,6},{1,7},{2,4},{3,5},{4,2},{5,3},{6,0},{7,1},{8,14},{9,15},{10,... | collective-permute-start | bytes 417800 | tf_op jit(solution)/shard_map/ppermute | solution.py:580
  79.3 2.2 %collective-permute-done.24.rest_1_ = bf16[272,256]{1,0:T(8,128)(2,1)S(1)} collective-permute-done((bf16[272,256]{1,0:T(8,128)(2,1)S(1)}, bf16[272,256]{1,0:T(8,128)(2,1)S(1)}, u32[]{:S(2)}, u32[]{:S(2)}) %collective-permute-start.24) | collective-permute-done | bytes 139296 | tf_op jit(solution)/shard_map/ppermute | solution.py:580
  81.5 2.0 %collective-permute-done.25.rest_2_ = bf16[272,256]{1,0:T(8,128)(2,1)S(1)} collective-permute-done((bf16[272,256]{1,0:T(8,128)(2,1)S(1)}, bf16[272,256]{1,0:T(8,128)(2,1)S(1)}, u32[]{:S(2)}, u32[]{:S(2)}) %collective-permute-start.25) | collective-permute-done | bytes 139296 | tf_op jit(solution)/shard_map/ppermute | solution.py:580
  83.5 2.2 %collective-permute-done.26.rest_3_ = bf16[272,256]{1,0:T(8,128)(2,1)S(1)} collective-permute-done((bf16[272,256]{1,0:T(8,128)(2,1)S(1)}, bf16[272,256]{1,0:T(8,128)(2,1)S(1)}, u32[]{:S(2)}, u32[]{:S(2)}) %collective-permute-start.26) | collective-permute-done | bytes 139296 | tf_op jit(solution)/shard_map/ppermute | solution.py:580
  85.7 0.2 shard_map.151
  85.9 1.5 %collective-permute-start.27 = (bf16[256,256]{1,0:T(8,128)(2,1)S(1)}, bf16[256,256]{1,0:T(8,128)(2,1)S(1)}, u32[]{:S(2)}, u32[]{:S(2)}) collective-permute-start(bf16[256,256]{1,0:T(8,128)(2,1)S(1)} %shard_map.151), channel_id=1, source_target_pairs={{8,0},{9,1},{10,2},{11,3},{12,4},{13,5},{14,6},{15,7},{24,16},{25,... | collective-permute-start | bytes 393224 | tf_op jit(solution)/shard_map/ppermute | solution.py:628
  87.4 2.8 %shard_map.149 = (f32[128,2048]{1,0:T(8,128)S(1)}, f32[128,256]{1,0:T(8,128)S(1)}, f32[128,256]{1,0:T(8,128)}, f32[128,2048]{1,0:T(8,128)}) custom-call(s32[1]{0:T(128)} %bitcast.me_ref, bf16[128,2048]{1,0:T(8,128)(2,1)S(1)} %get-tuple-element.115.grad_ref, bf16[128,2048]{1,0:T(8,128)(2,1)S(1)} %get-tuple-element.116.grown_ref, ...), custom_call_target="tpu_custom_call" | custom-call | flops 268435456 | bytes 7241732 | tf_op jit(solution)/shard_map/pallas_call | solution.py:45
  90.3 5.7 %collective-permute-done.27.carry_ref = bf16[256,256]{1,0:T(8,128)(2,1)S(1)} collective-permute-done((bf16[256,256]{1,0:T(8,128)(2,1)S(1)}, bf16[256,256]{1,0:T(8,128)(2,1)S(1)}, u32[]{:S(2)}, u32[]{:S(2)}) %collective-permute-start.27) | collective-permute-done | bytes 131104 | tf_op jit(solution)/shard_map/ppermute | solution.py:628
  95.9 0.3 shard_map.152
  96.2 1.2 %collective-permute-start.28 = (bf16[256,256]{1,0:T(8,128)(2,1)S(1)}, bf16[256,256]{1,0:T(8,128)(2,1)S(1)}, u32[]{:S(2)}, u32[]{:S(2)}) collective-permute-start(bf16[256,256]{1,0:T(8,128)(2,1)S(1)} %get-tuple-element.131), channel_id=1, source_target_pairs={{0,2},{1,3},{2,0},{3,1},{4,6},{5,7},{6,4},{7,5},{8,10},{9,11},{10,... | collective-permute-start | bytes 393224 | tf_op jit(solution)/shard_map/ppermute | solution.py:580
  97.4 2.4 %collective-permute-start.30 = (bf16[256,256]{1,0:T(8,128)(2,1)S(1)}, bf16[256,256]{1,0:T(8,128)(2,1)S(1)}, u32[]{:S(2)}, u32[]{:S(2)}) collective-permute-start(bf16[256,256]{1,0:T(8,128)(2,1)S(1)} %get-tuple-element.133), channel_id=1, source_target_pairs={{0,6},{1,7},{2,4},{3,5},{4,2},{5,3},{6,0},{7,1},{8,14},{9,15},{10,... | collective-permute-start | bytes 393224 | tf_op jit(solution)/shard_map/ppermute | solution.py:580
  99.8 2.9 %collective-permute-done.28.rest_1_ = bf16[256,256]{1,0:T(8,128)(2,1)S(1)} collective-permute-done((bf16[256,256]{1,0:T(8,128)(2,1)S(1)}, bf16[256,256]{1,0:T(8,128)(2,1)S(1)}, u32[]{:S(2)}, u32[]{:S(2)}) %collective-permute-start.28) | collective-permute-done | bytes 131104 | tf_op jit(solution)/shard_map/ppermute | solution.py:580
  102.7 0.6 collective-permute-done.29.rest_2_
  103.3 1.2 %collective-permute-done.30.rest_3_ = bf16[256,256]{1,0:T(8,128)(2,1)S(1)} collective-permute-done((bf16[256,256]{1,0:T(8,128)(2,1)S(1)}, bf16[256,256]{1,0:T(8,128)(2,1)S(1)}, u32[]{:S(2)}, u32[]{:S(2)}) %collective-permute-start.30) | collective-permute-done | bytes 131104 | tf_op jit(solution)/shard_map/ppermute | solution.py:580
  104.6 0.6 shard_map.153
  105.3 0.4 shard_map.154
  105.6 1.5 %collective-permute-done.31.other_ref = bf16[1024,256]{1,0:T(8,128)(2,1)S(1)} collective-permute-done((bf16[1024,256]{1,0:T(8,128)(2,1)S(1)}, bf16[1024,256]{1,0:T(8,128)(2,1)S(1)}, u32[]{:S(2)}, u32[]{:S(2)}) %collective-permute-start.31) | collective-permute-done | bytes 524320 | tf_op jit(solution)/shard_map/ppermute | solution.py:580
  107.2 1.4 %shard_map.155 = (f32[128,2048]{1,0:T(8,128)}, f32[128,256]{1,0:T(8,128)}) custom-call(s32[1]{0:T(128)} %bitcast.me_ref, f32[128,2048]{1,0:T(8,128)S(1)} %get-tuple-element.119.value_ref, f32[128,256]{1,0:T(8,128)S(1)} %get-tuple-element.120.write_part_ref, f32[128,1024]{1,0:T(8,128)S(1)} %get-tuple-element.135.half_ref, ...), custom_call_target="tpu_custom_call" | custom-call | flops 134217728 | bytes 5177348 | tf_op jit(solution)/shard_map/pallas_call | solution.py:45
  (44 shorter events, 0.4 us)
Async XLA Ops:
  1.4 10.0 %collective-permute-start.2 = (bf16[128,256]{1,0:T(8,128)(2,1)S(1)}, bf16[128,256]{1,0:T(8,128)(2,1)S(1)}, u32[]{:S(2)}, u32[]{:S(2)}) collective-permute-start(bf16[128,256]{1,0:T(8,128)(2,1)S(1)} %pad_add_fusion.refs_0_), channel_id=1, source_target_pairs={{0,12},{1,13},{2,14},{3,15},{4,8},{5,9},{6,10},{7,11},{8,4},{9,5},... | collective-permute-start | bytes 196616 | tf_op jit(solution)/shard_map/ppermute | solution.py:580
  6.5 5.6 %collective-permute-start.1 = (bf16[128,256]{1,0:T(8,128)(2,1)S(1)}, bf16[128,256]{1,0:T(8,128)(2,1)S(1)}, u32[]{:S(2)}, u32[]{:S(2)}) collective-permute-start(bf16[128,256]{1,0:T(8,128)(2,1)S(1)} %pad_add_fusion.refs_0_), channel_id=1, source_target_pairs={{0,8},{1,9},{2,10},{3,11},{4,12},{5,13},{6,14},{7,15},{8,0},{9,1},... | collective-permute-start | bytes 196616 | tf_op jit(solution)/shard_map/ppermute | solution.py:580
  6.5 5.6 %collective-permute-start = (bf16[128,256]{1,0:T(8,128)(2,1)S(1)}, bf16[128,256]{1,0:T(8,128)(2,1)S(1)}, u32[]{:S(2)}, u32[]{:S(2)}) collective-permute-start(bf16[128,256]{1,0:T(8,128)(2,1)S(1)} %pad_add_fusion.refs_0_), channel_id=1, source_target_pairs={{0,4},{1,5},{2,6},{3,7},{4,0},{5,1},{6,2},{7,3},{8,12},{9,13},{10,... | collective-permute-start | bytes 196616 | tf_op jit(solution)/shard_map/ppermute | solution.py:580
  7.2 1.0 copy-start
  8.2 0.8 copy-start.2
  9.1 0.7 copy-start.8
  12.2 2.0 %collective-permute-start.3 = (bf16[1040,256]{1,0:T(8,128)(2,1)S(1)}, bf16[1040,256]{1,0:T(8,128)(2,1)S(1)}, u32[]{:S(2)}, u32[]{:S(2)}) collective-permute-start(bf16[1040,256]{1,0:T(8,128)(2,1)S(1)} %get-tuple-element.79), channel_id=1, source_target_pairs={{0,1},{1,0},{2,3},{3,2},{4,5},{5,4},{6,7},{7,6},{8,9},{9,8},{10,11... | collective-permute-start | bytes 1597448 | tf_op jit(solution)/shard_map/ppermute | solution.py:580
  12.2 10.1 %collective-permute-start.9 = (bf16[4,128,256]{2,1,0:T(8,128)(2,1)S(1)}, bf16[4,128,256]{2,1,0:T(8,128)(2,1)S(1)}, u32[]{:S(2)}, u32[]{:S(2)}) collective-permute-start(bf16[4,128,256]{2,1,0:T(8,128)(2,1)S(1)} %shard_map.139.rest_0_), channel_id=1, source_target_pairs={{0,2},{1,3},{2,0},{3,1},{4,6},{5,7},{6,4},{7,5},{8,10},{9,11},{10,... | collective-permute-start | bytes 786440 | tf_op jit(solution)/shard_map/ppermute | solution.py:580
  14.7 12.3 %collective-permute-start.4 = (bf16[272,256]{1,0:T(8,128)(2,1)S(1)}, bf16[272,256]{1,0:T(8,128)(2,1)S(1)}, u32[]{:S(2)}, u32[]{:S(2)}) collective-permute-start(bf16[272,256]{1,0:T(8,128)(2,1)S(1)} %get-tuple-element.81), channel_id=1, source_target_pairs={{0,2},{1,3},{2,0},{3,1},{4,6},{5,7},{6,4},{7,5},{8,10},{9,11},{10,... | collective-permute-start | bytes 417800 | tf_op jit(solution)/shard_map/ppermute | solution.py:580
  16.2 10.7 %collective-permute-start.5 = (bf16[272,256]{1,0:T(8,128)(2,1)S(1)}, bf16[272,256]{1,0:T(8,128)(2,1)S(1)}, u32[]{:S(2)}, u32[]{:S(2)}) collective-permute-start(bf16[272,256]{1,0:T(8,128)(2,1)S(1)} %get-tuple-element.82), channel_id=1, source_target_pairs={{0,4},{1,5},{2,6},{3,7},{4,0},{5,1},{6,2},{7,3},{8,12},{9,13},{10,... | collective-permute-start | bytes 417800 | tf_op jit(solution)/shard_map/ppermute | solution.py:580
  17.3 9.6 %collective-permute-start.6 = (bf16[272,256]{1,0:T(8,128)(2,1)S(1)}, bf16[272,256]{1,0:T(8,128)(2,1)S(1)}, u32[]{:S(2)}, u32[]{:S(2)}) collective-permute-start(bf16[272,256]{1,0:T(8,128)(2,1)S(1)} %get-tuple-element.83), channel_id=1, source_target_pairs={{0,6},{1,7},{2,4},{3,5},{4,2},{5,3},{6,0},{7,1},{8,14},{9,15},{10,... | collective-permute-start | bytes 417800 | tf_op jit(solution)/shard_map/ppermute | solution.py:580
  18.2 0.9 copy-start.6
  19.2 0.9 copy-start.7
  20.2 10.7 %collective-permute-start.8 = (bf16[4,128,256]{2,1,0:T(8,128)(2,1)S(1)}, bf16[4,128,256]{2,1,0:T(8,128)(2,1)S(1)}, u32[]{:S(2)}, u32[]{:S(2)}) collective-permute-start(bf16[4,128,256]{2,1,0:T(8,128)(2,1)S(1)} %shard_map.139.rest_0_), channel_id=1, source_target_pairs={{0,1},{1,0},{2,3},{3,2},{4,5},{5,4},{6,7},{7,6},{8,9},{9,8},{10,11... | collective-permute-start | bytes 786440 | tf_op jit(solution)/shard_map/ppermute | solution.py:580
  26.9 4.0 %collective-permute-start.10 = (bf16[4,128,256]{2,1,0:T(8,128)(2,1)S(1)}, bf16[4,128,256]{2,1,0:T(8,128)(2,1)S(1)}, u32[]{:S(2)}, u32[]{:S(2)}) collective-permute-start(bf16[4,128,256]{2,1,0:T(8,128)(2,1)S(1)} %collective-permute-done.9.rest_2_), channel_id=1, source_target_pairs={{0,1},{1,0},{2,3},{3,2},{4,5},{5,4},{6,7},{7,6},{8,9},{9,8},{10,11... | collective-permute-start | bytes 786440 | tf_op jit(solution)/shard_map/ppermute | solution.py:580
  27.2 8.9 %collective-permute-start.7 = (bf16[256,256]{1,0:T(8,128)(2,1)S(1)}, bf16[256,256]{1,0:T(8,128)(2,1)S(1)}, u32[]{:S(2)}, u32[]{:S(2)}) collective-permute-start(bf16[256,256]{1,0:T(8,128)(2,1)S(1)} %shard_map.141), channel_id=1, source_target_pairs={{0,8},{1,9},{2,10},{3,11},{4,12},{5,13},{6,14},{7,15},{16,24},{17,... | collective-permute-start | bytes 393224 | tf_op jit(solution)/shard_map/ppermute | solution.py:628
  30.9 39.5 %slice-start = ((s8[5242880]{0:T(1024)(128)(4,1)}), s8[4194304]{0:T(1024)(128)(4,1)S(1)}, s32[]{:S(2)}) async-start(s8[5242880]{0:T(1024)(128)(4,1)} %bitcast.3), calls=%async_computation | async-start | bytes 8388608
  30.9 33.3 %copy-start.1 = (bf16[128,2048]{1,0:T(8,128)(2,1)S(1)}, bf16[128,2048]{1,0:T(8,128)(2,1)}, u32[]{:S(2)}) copy-start(bf16[128,2048]{1,0:T(8,128)(2,1)} %input_ref.5) | copy-start | bytes 1572868
  31.0 33.3 %copy-start.3 = (bf16[128,256]{1,0:T(8,128)(2,1)S(1)}, bf16[128,256]{1,0:T(8,128)(2,1)}, u32[]{:S(2)}) copy-start(bf16[128,256]{1,0:T(8,128)(2,1)} %write_ref.9) | copy-start | bytes 196612
  31.0 33.3 %copy-start.4 = (bf16[128,256]{1,0:T(8,128)(2,1)S(1)}, bf16[128,256]{1,0:T(8,128)(2,1)}, u32[]{:S(2)}) copy-start(bf16[128,256]{1,0:T(8,128)(2,1)} %read_ref.5) | copy-start | bytes 196612
  31.0 33.3 %copy-start.5 = (bf16[128,2048]{1,0:T(8,128)(2,1)S(1)}, bf16[128,2048]{1,0:T(8,128)(2,1)}, u32[]{:S(2)}) copy-start(bf16[128,2048]{1,0:T(8,128)(2,1)} %gate_ref.1) | copy-start | bytes 1572868
  31.0 39.4 %slice-start.1 = ((s8[5242880]{0:T(1024)(128)(4,1)}), s8[1048576]{0:T(1024)(128)(4,1)S(1)}, s32[]{:S(2)}) async-start(s8[5242880]{0:T(1024)(128)(4,1)} %bitcast.3), calls=%async_computation.1 | async-start | bytes 2097152
  36.0 34.4 %copy-start.9 = (f32[2048]{0:T(1024)S(1)}, f32[2048]{0:T(1024)}, u32[]{:S(2)}) copy-start(f32[2048]{0:T(1024)} %param.20) | copy-start | bytes 24580
  36.1 4.3 %collective-permute-start.14 = (bf16[8,160,256]{2,1,0:T(8,128)(2,1)S(1)}, bf16[8,160,256]{2,1,0:T(8,128)(2,1)S(1)}, u32[]{:S(2)}, u32[]{:S(2)}) collective-permute-start(bf16[8,160,256]{2,1,0:T(8,128)(2,1)S(1)} %get-tuple-element.96), channel_id=1, source_target_pairs={{0,1},{1,0},{2,3},{3,2},{4,5},{5,4},{6,7},{7,6},{8,9},{9,8},{10,11... | collective-permute-start | bytes 1966088 | tf_op jit(solution)/shard_map/ppermute | solution.py:580
  36.6 8.7 %collective-permute-start.11 = (bf16[256,256]{1,0:T(8,128)(2,1)S(1)}, bf16[256,256]{1,0:T(8,128)(2,1)S(1)}, u32[]{:S(2)}, u32[]{:S(2)}) collective-permute-start(bf16[256,256]{1,0:T(8,128)(2,1)S(1)} %get-tuple-element.92), channel_id=1, source_target_pairs={{0,2},{1,3},{2,0},{3,1},{4,6},{5,7},{6,4},{7,5},{8,10},{9,11},{10,... | collective-permute-start | bytes 393224 | tf_op jit(solution)/shard_map/ppermute | solution.py:580
  38.2 10.2 %collective-permute-start.12 = (bf16[256,256]{1,0:T(8,128)(2,1)S(1)}, bf16[256,256]{1,0:T(8,128)(2,1)S(1)}, u32[]{:S(2)}, u32[]{:S(2)}) collective-permute-start(bf16[256,256]{1,0:T(8,128)(2,1)S(1)} %get-tuple-element.93), channel_id=1, source_target_pairs={{0,4},{1,5},{2,6},{3,7},{4,0},{5,1},{6,2},{7,3},{8,12},{9,13},{10,... | collective-permute-start | bytes 393224 | tf_op jit(solution)/shard_map/ppermute | solution.py:580
  40.4 8.1 %collective-permute-start.13 = (bf16[256,256]{1,0:T(8,128)(2,1)S(1)}, bf16[256,256]{1,0:T(8,128)(2,1)S(1)}, u32[]{:S(2)}, u32[]{:S(2)}) collective-permute-start(bf16[256,256]{1,0:T(8,128)(2,1)S(1)} %get-tuple-element.94), channel_id=1, source_target_pairs={{0,6},{1,7},{2,4},{3,5},{4,2},{5,3},{6,0},{7,1},{8,14},{9,15},{10,... | collective-permute-start | bytes 393224 | tf_op jit(solution)/shard_map/ppermute | solution.py:580
  40.5 12.0 %collective-permute-start.15 = (bf16[192,256]{1,0:T(8,128)(2,1)S(1)}, bf16[192,256]{1,0:T(8,128)(2,1)S(1)}, u32[]{:S(2)}, u32[]{:S(2)}) collective-permute-start(bf16[192,256]{1,0:T(8,128)(2,1)S(1)} %get-tuple-element.98), channel_id=1, source_target_pairs={{0,12},{1,13},{2,14},{3,15},{4,8},{5,9},{6,10},{7,11},{8,4},{9,5},... | collective-permute-start | bytes 294920 | tf_op jit(solution)/shard_map/ppermute | solution.py:580
  45.3 12.3 %collective-permute-start.16 = (bf16[192,256]{1,0:T(8,128)(2,1)S(1)}, bf16[192,256]{1,0:T(8,128)(2,1)S(1)}, u32[]{:S(2)}, u32[]{:S(2)}) collective-permute-start(bf16[192,256]{1,0:T(8,128)(2,1)S(1)} %get-tuple-element.99), channel_id=1, source_target_pairs={{0,8},{1,9},{2,10},{3,11},{4,12},{5,13},{6,14},{7,15},{8,0},{9,1},... | collective-permute-start | bytes 294920 | tf_op jit(solution)/shard_map/ppermute | solution.py:580
  45.3 12.3 %collective-permute-start.17 = (bf16[192,256]{1,0:T(8,128)(2,1)S(1)}, bf16[192,256]{1,0:T(8,128)(2,1)S(1)}, u32[]{:S(2)}, u32[]{:S(2)}) collective-permute-start(bf16[192,256]{1,0:T(8,128)(2,1)S(1)} %get-tuple-element.100), channel_id=1, source_target_pairs={{0,14},{1,15},{2,12},{3,13},{4,10},{5,11},{6,8},{7,9},{8,6},{9,7},... | collective-permute-start | bytes 294920 | tf_op jit(solution)/shard_map/ppermute | solution.py:580
  58.2 6.0 %collective-permute-start.18 = (bf16[1024,256]{1,0:T(8,128)(2,1)S(1)}, bf16[1024,256]{1,0:T(8,128)(2,1)S(1)}, u32[]{:S(2)}, u32[]{:S(2)}) collective-permute-start(bf16[1024,256]{1,0:T(8,128)(2,1)S(1)} %get-tuple-element.106), channel_id=1, source_target_pairs={{0,1},{1,0},{2,3},{3,2},{4,5},{5,4},{6,7},{7,6},{8,9},{9,8},{10,11... | collective-permute-start | bytes 1572872 | tf_op jit(solution)/shard_map/ppermute | solution.py:580
  58.3 8.8 %collective-permute-start.19 = (bf16[192,256]{1,0:T(8,128)(2,1)S(1)}, bf16[192,256]{1,0:T(8,128)(2,1)S(1)}, u32[]{:S(2)}, u32[]{:S(2)}) collective-permute-start(bf16[192,256]{1,0:T(8,128)(2,1)S(1)} %get-tuple-element.110), channel_id=1, source_target_pairs={{0,10},{1,11},{2,8},{3,9},{4,14},{5,15},{6,12},{7,13},{8,2},{9,3},... | collective-permute-start | bytes 294920 | tf_op jit(solution)/shard_map/ppermute | solution.py:580
  60.7 6.3 %collective-permute-start.20 = (bf16[192,256]{1,0:T(8,128)(2,1)S(1)}, bf16[192,256]{1,0:T(8,128)(2,1)S(1)}, u32[]{:S(2)}, u32[]{:S(2)}) collective-permute-start(bf16[192,256]{1,0:T(8,128)(2,1)S(1)} %get-tuple-element.111), channel_id=1, source_target_pairs={{0,4},{1,5},{2,6},{3,7},{4,0},{5,1},{6,2},{7,3},{8,12},{9,13},{10,... | collective-permute-start | bytes 294920 | tf_op jit(solution)/shard_map/ppermute | solution.py:580
  61.0 8.7 %collective-permute-start.21 = (bf16[192,256]{1,0:T(8,128)(2,1)S(1)}, bf16[192,256]{1,0:T(8,128)(2,1)S(1)}, u32[]{:S(2)}, u32[]{:S(2)}) collective-permute-start(bf16[192,256]{1,0:T(8,128)(2,1)S(1)} %get-tuple-element.113), channel_id=1, source_target_pairs={{0,6},{1,7},{2,4},{3,5},{4,2},{5,3},{6,0},{7,1},{8,14},{9,15},{10,... | collective-permute-start | bytes 294920 | tf_op jit(solution)/shard_map/ppermute | solution.py:580
  63.7 6.7 %collective-permute-start.22 = (bf16[192,256]{1,0:T(8,128)(2,1)S(1)}, bf16[192,256]{1,0:T(8,128)(2,1)S(1)}, u32[]{:S(2)}, u32[]{:S(2)}) collective-permute-start(bf16[192,256]{1,0:T(8,128)(2,1)S(1)} %get-tuple-element.114), channel_id=1, source_target_pairs={{0,2},{1,3},{2,0},{3,1},{4,6},{5,7},{6,4},{7,5},{8,10},{9,11},{10,... | collective-permute-start | bytes 294920 | tf_op jit(solution)/shard_map/ppermute | solution.py:580
  73.2 2.0 %collective-permute-start.23 = (bf16[1040,256]{1,0:T(8,128)(2,1)S(1)}, bf16[1040,256]{1,0:T(8,128)(2,1)S(1)}, u32[]{:S(2)}, u32[]{:S(2)}) collective-permute-start(bf16[1040,256]{1,0:T(8,128)(2,1)S(1)} %get-tuple-element.124), channel_id=1, source_target_pairs={{0,1},{1,0},{2,3},{3,2},{4,5},{5,4},{6,7},{7,6},{8,9},{9,8},{10,11... | collective-permute-start | bytes 1597448 | tf_op jit(solution)/shard_map/ppermute | solution.py:580
  75.7 5.8 %collective-permute-start.24 = (bf16[272,256]{1,0:T(8,128)(2,1)S(1)}, bf16[272,256]{1,0:T(8,128)(2,1)S(1)}, u32[]{:S(2)}, u32[]{:S(2)}) collective-permute-start(bf16[272,256]{1,0:T(8,128)(2,1)S(1)} %get-tuple-element.126), channel_id=1, source_target_pairs={{0,2},{1,3},{2,0},{3,1},{4,6},{5,7},{6,4},{7,5},{8,10},{9,11},{10,... | collective-permute-start | bytes 417800 | tf_op jit(solution)/shard_map/ppermute | solution.py:580
  77.0 6.6 %collective-permute-start.25 = (bf16[272,256]{1,0:T(8,128)(2,1)S(1)}, bf16[272,256]{1,0:T(8,128)(2,1)S(1)}, u32[]{:S(2)}, u32[]{:S(2)}) collective-permute-start(bf16[272,256]{1,0:T(8,128)(2,1)S(1)} %get-tuple-element.127), channel_id=1, source_target_pairs={{0,4},{1,5},{2,6},{3,7},{4,0},{5,1},{6,2},{7,3},{8,12},{9,13},{10,... | collective-permute-start | bytes 417800 | tf_op jit(solution)/shard_map/ppermute | solution.py:580
  78.1 7.6 %collective-permute-start.26 = (bf16[272,256]{1,0:T(8,128)(2,1)S(1)}, bf16[272,256]{1,0:T(8,128)(2,1)S(1)}, u32[]{:S(2)}, u32[]{:S(2)}) collective-permute-start(bf16[272,256]{1,0:T(8,128)(2,1)S(1)} %get-tuple-element.128), channel_id=1, source_target_pairs={{0,6},{1,7},{2,4},{3,5},{4,2},{5,3},{6,0},{7,1},{8,14},{9,15},{10,... | collective-permute-start | bytes 417800 | tf_op jit(solution)/shard_map/ppermute | solution.py:580
  85.9 10.0 %collective-permute-start.27 = (bf16[256,256]{1,0:T(8,128)(2,1)S(1)}, bf16[256,256]{1,0:T(8,128)(2,1)S(1)}, u32[]{:S(2)}, u32[]{:S(2)}) collective-permute-start(bf16[256,256]{1,0:T(8,128)(2,1)S(1)} %shard_map.151), channel_id=1, source_target_pairs={{8,0},{9,1},{10,2},{11,3},{12,4},{13,5},{14,6},{15,7},{24,16},{25,... | collective-permute-start | bytes 393224 | tf_op jit(solution)/shard_map/ppermute | solution.py:628
  96.2 6.4 %collective-permute-start.28 = (bf16[256,256]{1,0:T(8,128)(2,1)S(1)}, bf16[256,256]{1,0:T(8,128)(2,1)S(1)}, u32[]{:S(2)}, u32[]{:S(2)}) collective-permute-start(bf16[256,256]{1,0:T(8,128)(2,1)S(1)} %get-tuple-element.131), channel_id=1, source_target_pairs={{0,2},{1,3},{2,0},{3,1},{4,6},{5,7},{6,4},{7,5},{8,10},{9,11},{10,... | collective-permute-start | bytes 393224 | tf_op jit(solution)/shard_map/ppermute | solution.py:580
  97.4 5.9 %collective-permute-start.29 = (bf16[256,256]{1,0:T(8,128)(2,1)S(1)}, bf16[256,256]{1,0:T(8,128)(2,1)S(1)}, u32[]{:S(2)}, u32[]{:S(2)}) collective-permute-start(bf16[256,256]{1,0:T(8,128)(2,1)S(1)} %get-tuple-element.132), channel_id=1, source_target_pairs={{0,4},{1,5},{2,6},{3,7},{4,0},{5,1},{6,2},{7,3},{8,12},{9,13},{10,... | collective-permute-start | bytes 393224 | tf_op jit(solution)/shard_map/ppermute | solution.py:580
  97.4 7.1 %collective-permute-start.30 = (bf16[256,256]{1,0:T(8,128)(2,1)S(1)}, bf16[256,256]{1,0:T(8,128)(2,1)S(1)}, u32[]{:S(2)}, u32[]{:S(2)}) collective-permute-start(bf16[256,256]{1,0:T(8,128)(2,1)S(1)} %get-tuple-element.133), channel_id=1, source_target_pairs={{0,6},{1,7},{2,4},{3,5},{4,2},{5,3},{6,0},{7,1},{8,14},{9,15},{10,... | collective-permute-start | bytes 393224 | tf_op jit(solution)/shard_map/ppermute | solution.py:580
  105.2 2.0 %collective-permute-start.31 = (bf16[1024,256]{1,0:T(8,128)(2,1)S(1)}, bf16[1024,256]{1,0:T(8,128)(2,1)S(1)}, u32[]{:S(2)}, u32[]{:S(2)}) collective-permute-start(bf16[1024,256]{1,0:T(8,128)(2,1)S(1)} %get-tuple-element.137), channel_id=1, source_target_pairs={{0,1},{1,0},{2,3},{3,2},{4,5},{5,4},{6,7},{7,6},{8,9},{9,8},{10,11... | collective-permute-start | bytes 1572872 | tf_op jit(solution)/shard_map/ppermute | solution.py:580

commit v4 on v3

--- a/solution.py
+++ b/solution.py
@@ -777,7 +777,7 @@
     )
     order = sorted(range(chips), key=lambda k: (-(k // 4), k % 2, -k))
     received = [crossed(sent[k], 2 * k) if k else sent[k] for k in order]
-    returned = tied(tuple(scan_parts(backs)), tuple(received[:3]))
+    returned = tied(tuple(scan_parts(backs)), tuple(received[:2]))
     incoming, incoming_other = scan_out(me, cumulated, returned, keep, got, False)
 
     both_states = pltpu.VMEM((2, channels // 2, nstate), BF16)

time: 109 us -> 109 us (level)
  waiting for transfers between devices: 41.6 us -> 43.9 us
  starting transfers between devices: 41.5 us -> 39.3 us
    ppermute x30, waiting for transfers between devices: 35.9 us -> 38.5 us  [crossed(): return lax.ppermute(array, 'ctx', pairs)]
    ppermute x30, starting transfers between devices: 36.2 us -> 34 us  [crossed(): return lax.ppermute(array, 'ctx', pairs)]
  transfers between devices with their start and end apart: 32 -> 32, of which waited for: 18 -> 19; matrix products, arithmetic and copies ran while one was open for 0% -> 0% of each run, Pallas kernels for 12% -> 12%
where the time goes in v4:
time: 109 us
  waiting for transfers between devices  43.9 us (40%)
  starting transfers between devices  39.3 us (36%)
  Pallas kernels  19.2 us (18%)
  local copies, waits for them, and re-layouts  4.54 us (4%)
    ppermute x30, waiting for transfers between devices, crossed(): return lax.ppermute(array, 'ctx', pairs)  38.5 us
    ppermute x30, starting transfers between devices, crossed(): return lax.ppermute(array, 'ctx', pairs)  34 us
    pallas_call x18, Pallas kernels, call(): pl.pallas_call(kernel, out_shape=tuple(outs), in_specs=specs, out_specs=t...  19.2 us
    ppermute x2, waiting for transfers between devices, scan_carry(): return lax.ppermute(total, 'ctx', pairs)  5.39 us
    ppermute x2, starting transfers between devices, scan_carry(): return lax.ppermute(total, 'ctx', pairs)  5.25 us
    unnamed x24, local copies, waits for them, and re-layouts  4.54 us
  transfers between devices with their start and end apart: 32, of which 19 were waited for; matrix products, arithmetic and copies ran while one was open for 0% of the time, Pallas kernels for 12%

profile of v4, /device:TPU:0, one launch (start us, length us, event | category | flops | bytes accessed | tf_op | source)
XLA Modules:
  0.0 108.7 jit_solution(725090248214363891)
XLA Ops:
  0.6 0.8 pad_add_fusion.refs_0_
  1.4 5.1 %collective-permute-start.2 = (bf16[128,256]{1,0:T(8,128)(2,1)S(1)}, bf16[128,256]{1,0:T(8,128)(2,1)S(1)}, u32[]{:S(2)}, u32[]{:S(2)}) collective-permute-start(bf16[128,256]{1,0:T(8,128)(2,1)S(1)} %pad_add_fusion.refs_0_), channel_id=1, source_target_pairs={{0,12},{1,13},{2,14},{3,15},{4,8},{5,9},{6,10},{7,11},{8,4},{9,5},... | collective-permute-start | bytes 196616 | tf_op jit(solution)/shard_map/ppermute | solution.py:580
  6.5 0.6 collective-permute-start
  7.2 1.0 copy-done
  8.2 0.8 copy-done.2
  9.1 0.7 copy-done.8
  9.8 1.7 %shard_map.138 = (bf16[1024,256]{1,0:T(8,128)(2,1)S(1)}, bf16[1040,256]{1,0:T(8,128)(2,1)S(1)}, bf16[128,2048]{1,0:T(8,128)(2,1)S(1)}, f32[128,2048]{1,0:T(8,128...) custom-call(s32[1]{0:T(128)} %bitcast.me_ref, bf16[128,2048]{1,0:T(8,128)(2,1)S(1)} %copy-done, ...), custom_call_target="tpu_custom_call" | custom-call | flops 134217728 | bytes 4317188 | tf_op jit(solution)/shard_map/pallas_call | solution.py:45
  11.5 0.7 collective-permute-done.1.refs_2_
  12.2 1.6 %collective-permute-start.9 = (bf16[4,128,256]{2,1,0:T(8,128)(2,1)S(1)}, bf16[4,128,256]{2,1,0:T(8,128)(2,1)S(1)}, u32[]{:S(2)}, u32[]{:S(2)}) collective-permute-start(bf16[4,128,256]{2,1,0:T(8,128)(2,1)S(1)} %shard_map.139.rest_0_), channel_id=1, source_target_pairs={{0,2},{1,3},{2,0},{3,1},{4,6},{5,7},{6,4},{7,5},{8,10},{9,11},{10,... | collective-permute-start | bytes 786440 | tf_op jit(solution)/shard_map/ppermute | solution.py:580
  13.8 0.3 collective-permute-done.3.got_ref
  14.1 0.5 shard_map.140
  14.7 1.6 %collective-permute-start.4 = (bf16[272,256]{1,0:T(8,128)(2,1)S(1)}, bf16[272,256]{1,0:T(8,128)(2,1)S(1)}, u32[]{:S(2)}, u32[]{:S(2)}) collective-permute-start(bf16[272,256]{1,0:T(8,128)(2,1)S(1)} %get-tuple-element.81), channel_id=1, source_target_pairs={{0,2},{1,3},{2,0},{3,1},{4,6},{5,7},{6,4},{7,5},{8,10},{9,11},{10,... | collective-permute-start | bytes 417800 | tf_op jit(solution)/shard_map/ppermute | solution.py:580
  16.2 1.1 collective-permute-start.5
  17.3 0.9 collective-permute-start.6
  18.2 0.9 copy-done.6
  19.2 0.9 copy-done.7
  20.1 0.1 shard_map.142
  20.3 2.0 %collective-permute-done.9.rest_2_ = bf16[4,128,256]{2,1,0:T(8,128)(2,1)S(1)} collective-permute-done((bf16[4,128,256]{2,1,0:T(8,128)(2,1)S(1)}, bf16[4,128,256]{2,1,0:T(8,128)(2,1)S(1)}, u32[]{:S(2)}, u32[]{:S(2)}) %collective-permute-start.9) | collective-permute-done | bytes 262176 | tf_op jit(solution)/shard_map/ppermute | solution.py:580
  22.3 4.6 %collective-permute-done.4.rest_1_ = bf16[272,256]{1,0:T(8,128)(2,1)S(1)} collective-permute-done((bf16[272,256]{1,0:T(8,128)(2,1)S(1)}, bf16[272,256]{1,0:T(8,128)(2,1)S(1)}, u32[]{:S(2)}, u32[]{:S(2)}) %collective-permute-start.4) | collective-permute-done | bytes 139296 | tf_op jit(solution)/shard_map/ppermute | solution.py:580
  26.9 0.2 shard_map.141
  27.2 3.7 %collective-permute-start.7 = (bf16[256,256]{1,0:T(8,128)(2,1)S(1)}, bf16[256,256]{1,0:T(8,128)(2,1)S(1)}, u32[]{:S(2)}, u32[]{:S(2)}) collective-permute-start(bf16[256,256]{1,0:T(8,128)(2,1)S(1)} %shard_map.141), channel_id=1, source_target_pairs={{0,8},{1,9},{2,10},{3,11},{4,12},{5,13},{6,14},{7,15},{16,24},{17,... | collective-permute-start | bytes 393224 | tf_op jit(solution)/shard_map/ppermute | solution.py:628
  31.0 5.0 %shard_map.143 = (bf16[8,160,256]{2,1,0:T(8,128)(2,1)S(1)}, bf16[8,160,256]{2,1,0:T(8,128)(2,1)S(1)}) custom-call(s32[1]{0:T(128)} %bitcast.me_ref, bf16[4,256,128]{2,1,0:T(8,128)(2,1)S(1)} %get-tuple-element.85.query_ref, bf16[4,256,128]{2,1,0:T(8,128)(2,1)S(1)} %get-tuple-element.86.grad_ref, bf16[4,128,256]{2,1,0:T(8,128)(2,1)S(1)} %shard_map.139.rest_0_, ...), custom_call_target="tpu_custom_call" | custom-call | flops 2684354560 | bytes 2883588 | tf_op jit(solution)/shard_map/pallas_call | solution.py:45
  36.1 0.3 collective-permute-start.14
  36.4 0.3 shard_map.144
  36.6 1.6 %collective-permute-start.11 = (bf16[256,256]{1,0:T(8,128)(2,1)S(1)}, bf16[256,256]{1,0:T(8,128)(2,1)S(1)}, u32[]{:S(2)}, u32[]{:S(2)}) collective-permute-start(bf16[256,256]{1,0:T(8,128)(2,1)S(1)} %get-tuple-element.92), channel_id=1, source_target_pairs={{0,2},{1,3},{2,0},{3,1},{4,6},{5,7},{6,4},{7,5},{8,10},{9,11},{10,... | collective-permute-start | bytes 393224 | tf_op jit(solution)/shard_map/ppermute | solution.py:580
  38.2 2.1 %collective-permute-start.12 = (bf16[256,256]{1,0:T(8,128)(2,1)S(1)}, bf16[256,256]{1,0:T(8,128)(2,1)S(1)}, u32[]{:S(2)}, u32[]{:S(2)}) collective-permute-start(bf16[256,256]{1,0:T(8,128)(2,1)S(1)} %get-tuple-element.93), channel_id=1, source_target_pairs={{0,4},{1,5},{2,6},{3,7},{4,0},{5,1},{6,2},{7,3},{8,12},{9,13},{10,... | collective-permute-start | bytes 393224 | tf_op jit(solution)/shard_map/ppermute | solution.py:580
  40.4 0.1 shard_map.145
  40.5 4.8 %collective-permute-start.15 = (bf16[192,256]{1,0:T(8,128)(2,1)S(1)}, bf16[192,256]{1,0:T(8,128)(2,1)S(1)}, u32[]{:S(2)}, u32[]{:S(2)}) collective-permute-start(bf16[192,256]{1,0:T(8,128)(2,1)S(1)} %get-tuple-element.98), channel_id=1, source_target_pairs={{0,12},{1,13},{2,14},{3,15},{4,8},{5,9},{6,10},{7,11},{8,4},{9,5},... | collective-permute-start | bytes 294920 | tf_op jit(solution)/shard_map/ppermute | solution.py:580
  45.3 1.7 %collective-permute-done.13.rest_3_ = bf16[256,256]{1,0:T(8,128)(2,1)S(1)} collective-permute-done((bf16[256,256]{1,0:T(8,128)(2,1)S(1)}, bf16[256,256]{1,0:T(8,128)(2,1)S(1)}, u32[]{:S(2)}, u32[]{:S(2)}) %collective-permute-start.13) | collective-permute-done | bytes 131104 | tf_op jit(solution)/shard_map/ppermute | solution.py:580
  47.0 5.4 %collective-permute-done.15.rest_0_ = bf16[192,256]{1,0:T(8,128)(2,1)S(1)} collective-permute-done((bf16[192,256]{1,0:T(8,128)(2,1)S(1)}, bf16[192,256]{1,0:T(8,128)(2,1)S(1)}, u32[]{:S(2)}, u32[]{:S(2)}) %collective-permute-start.15) | collective-permute-done | bytes 98336 | tf_op jit(solution)/shard_map/ppermute | solution.py:580
  52.5 2.4 %collective-permute-done.16.rest_1_ = bf16[192,256]{1,0:T(8,128)(2,1)S(1)} collective-permute-done((bf16[192,256]{1,0:T(8,128)(2,1)S(1)}, bf16[192,256]{1,0:T(8,128)(2,1)S(1)}, u32[]{:S(2)}, u32[]{:S(2)}) %collective-permute-start.16) | collective-permute-done | bytes 98336 | tf_op jit(solution)/shard_map/ppermute | solution.py:580
  54.8 0.6 shard_map.146
  55.5 1.9 %collective-permute-start.18 = (bf16[192,256]{1,0:T(8,128)(2,1)S(1)}, bf16[192,256]{1,0:T(8,128)(2,1)S(1)}, u32[]{:S(2)}, u32[]{:S(2)}) collective-permute-start(bf16[192,256]{1,0:T(8,128)(2,1)S(1)} %get-tuple-element.109), channel_id=1, source_target_pairs={{0,14},{1,15},{2,12},{3,13},{4,10},{5,11},{6,8},{7,9},{8,6},{9,7},... | collective-permute-start | bytes 294920 | tf_op jit(solution)/shard_map/ppermute | solution.py:580
  57.4 0.4 collective-permute-start.19
  57.8 3.1 %collective-permute-start.20 = (bf16[192,256]{1,0:T(8,128)(2,1)S(1)}, bf16[192,256]{1,0:T(8,128)(2,1)S(1)}, u32[]{:S(2)}, u32[]{:S(2)}) collective-permute-start(bf16[192,256]{1,0:T(8,128)(2,1)S(1)} %get-tuple-element.111), channel_id=1, source_target_pairs={{0,4},{1,5},{2,6},{3,7},{4,0},{5,1},{6,2},{7,3},{8,12},{9,13},{10,... | collective-permute-start | bytes 294920 | tf_op jit(solution)/shard_map/ppermute | solution.py:580
  60.9 0.6 collective-permute-start.21
  61.4 0.9 collective-permute-start.22
  62.4 1.6 %shard_map.147 = (f32[128,2048]{1,0:T(8,128)S(1)}, f32[128,128]{1,0:T(8,128)S(1)}, f32[128,2048]{1,0:T(8,128)S(1)}, f32[128,2048]{1,0:T(8,128)S(1)}) custom-call(s32[1]{0:T(128)} %bitcast.me_ref, bf16[128,2048]{1,0:T(8,128)(2,1)S(1)} %copy-done.1, bf16[128,256]{1,0:T(8,128)(2,1)S(1)} %copy-done.3, bf16[128,256]{1,0:T(8,128)(2,1)S(1)} %copy-done.4, ...), custom_call_target="tpu_custom_call" | custom-call | flops 201326592 | bytes 6520836 | tf_op jit(solution)/shard_map/pallas_call | solution.py:45
  64.0 3.8 %collective-permute-done.19.rest_3_ = bf16[192,256]{1,0:T(8,128)(2,1)S(1)} collective-permute-done((bf16[192,256]{1,0:T(8,128)(2,1)S(1)}, bf16[192,256]{1,0:T(8,128)(2,1)S(1)}, u32[]{:S(2)}, u32[]{:S(2)}) %collective-permute-start.19) | collective-permute-done | bytes 98336 | tf_op jit(solution)/shard_map/ppermute | solution.py:580
  67.8 2.0 %collective-permute-done.21.rest_6_ = bf16[192,256]{1,0:T(8,128)(2,1)S(1)} collective-permute-done((bf16[192,256]{1,0:T(8,128)(2,1)S(1)}, bf16[192,256]{1,0:T(8,128)(2,1)S(1)}, u32[]{:S(2)}, u32[]{:S(2)}) %collective-permute-start.21) | collective-permute-done | bytes 98336 | tf_op jit(solution)/shard_map/ppermute | solution.py:580
  69.8 0.4 collective-permute-done.22.rest_7_
  70.2 2.8 %shard_map.148 = (f32[128,2048]{1,0:T(8,128)S(1)}, bf16[128,2048]{1,0:T(8,128)(2,1)S(1)}, bf16[1024,256]{1,0:T(8,128)(2,1)S(1)}, bf16[1040,256]{1,0:T(8,128)(2,1)S(1)}, bf16[128,2048]{1,0:T(8,128)(2,1)S(1)}) custom-call(s32[1]{0:T(128)} %bitcast.me_ref, bf16[2048,1280]{1,0:T(8,128)(2,1)S(1)} %bitcast.4, f32[128,2048]{1,0:T(8,128)S(1)} %get-tuple-element.106.gated_ref, ...), custom_call_target="tpu_custom_call" | custom-call | flops 805306368 | bytes 12484612 | tf_op jit(solution)/shard_map/pallas_call | solution.py:45
  73.1 1.9 %collective-permute-done.23.got_ref = bf16[1040,256]{1,0:T(8,128)(2,1)S(1)} collective-permute-done((bf16[1040,256]{1,0:T(8,128)(2,1)S(1)}, bf16[1040,256]{1,0:T(8,128)(2,1)S(1)}, u32[]{:S(2)}, u32[]{:S(2)}) %collective-permute-start.23) | collective-permute-done | bytes 532512 | tf_op jit(solution)/shard_map/ppermute | solution.py:580
  75.0 0.5 shard_map.150
  75.5 1.0 collective-permute-start.24
  76.5 0.4 collective-permute-start.25
  76.9 2.2 %collective-permute-start.26 = (bf16[272,256]{1,0:T(8,128)(2,1)S(1)}, bf16[272,256]{1,0:T(8,128)(2,1)S(1)}, u32[]{:S(2)}, u32[]{:S(2)}) collective-permute-start(bf16[272,256]{1,0:T(8,128)(2,1)S(1)} %get-tuple-element.128), channel_id=1, source_target_pairs={{0,6},{1,7},{2,4},{3,5},{4,2},{5,3},{6,0},{7,1},{8,14},{9,15},{10,... | collective-permute-start | bytes 417800 | tf_op jit(solution)/shard_map/ppermute | solution.py:580
  79.1 2.2 %collective-permute-done.24.rest_1_ = bf16[272,256]{1,0:T(8,128)(2,1)S(1)} collective-permute-done((bf16[272,256]{1,0:T(8,128)(2,1)S(1)}, bf16[272,256]{1,0:T(8,128)(2,1)S(1)}, u32[]{:S(2)}, u32[]{:S(2)}) %collective-permute-start.24) | collective-permute-done | bytes 139296 | tf_op jit(solution)/shard_map/ppermute | solution.py:580
  81.3 1.7 %collective-permute-done.25.rest_2_ = bf16[272,256]{1,0:T(8,128)(2,1)S(1)} collective-permute-done((bf16[272,256]{1,0:T(8,128)(2,1)S(1)}, bf16[272,256]{1,0:T(8,128)(2,1)S(1)}, u32[]{:S(2)}, u32[]{:S(2)}) %collective-permute-start.25) | collective-permute-done | bytes 139296 | tf_op jit(solution)/shard_map/ppermute | solution.py:580
  83.0 2.4 %collective-permute-done.26.rest_3_ = bf16[272,256]{1,0:T(8,128)(2,1)S(1)} collective-permute-done((bf16[272,256]{1,0:T(8,128)(2,1)S(1)}, bf16[272,256]{1,0:T(8,128)(2,1)S(1)}, u32[]{:S(2)}, u32[]{:S(2)}) %collective-permute-start.26) | collective-permute-done | bytes 139296 | tf_op jit(solution)/shard_map/ppermute | solution.py:580
  85.5 0.2 shard_map.151
  85.7 1.5 %collective-permute-start.27 = (bf16[256,256]{1,0:T(8,128)(2,1)S(1)}, bf16[256,256]{1,0:T(8,128)(2,1)S(1)}, u32[]{:S(2)}, u32[]{:S(2)}) collective-permute-start(bf16[256,256]{1,0:T(8,128)(2,1)S(1)} %shard_map.151), channel_id=1, source_target_pairs={{8,0},{9,1},{10,2},{11,3},{12,4},{13,5},{14,6},{15,7},{24,16},{25,... | collective-permute-start | bytes 393224 | tf_op jit(solution)/shard_map/ppermute | solution.py:628
  87.2 2.8 %shard_map.149 = (f32[128,2048]{1,0:T(8,128)S(1)}, f32[128,256]{1,0:T(8,128)S(1)}, f32[128,256]{1,0:T(8,128)}, f32[128,2048]{1,0:T(8,128)}) custom-call(s32[1]{0:T(128)} %bitcast.me_ref, bf16[128,2048]{1,0:T(8,128)(2,1)S(1)} %get-tuple-element.115.grad_ref, bf16[128,2048]{1,0:T(8,128)(2,1)S(1)} %get-tuple-element.116.grown_ref, ...), custom_call_target="tpu_custom_call" | custom-call | flops 268435456 | bytes 7241732 | tf_op jit(solution)/shard_map/pallas_call | solution.py:45
  90.0 5.4 %collective-permute-done.27.carry_ref = bf16[256,256]{1,0:T(8,128)(2,1)S(1)} collective-permute-done((bf16[256,256]{1,0:T(8,128)(2,1)S(1)}, bf16[256,256]{1,0:T(8,128)(2,1)S(1)}, u32[]{:S(2)}, u32[]{:S(2)}) %collective-permute-start.27) | collective-permute-done | bytes 131104 | tf_op jit(solution)/shard_map/ppermute | solution.py:628
  95.4 0.3 shard_map.152
  95.7 1.1 collective-permute-start.28
  96.8 2.5 %collective-permute-start.30 = (bf16[256,256]{1,0:T(8,128)(2,1)S(1)}, bf16[256,256]{1,0:T(8,128)(2,1)S(1)}, u32[]{:S(2)}, u32[]{:S(2)}) collective-permute-start(bf16[256,256]{1,0:T(8,128)(2,1)S(1)} %get-tuple-element.133), channel_id=1, source_target_pairs={{0,6},{1,7},{2,4},{3,5},{4,2},{5,3},{6,0},{7,1},{8,14},{9,15},{10,... | collective-permute-start | bytes 393224 | tf_op jit(solution)/shard_map/ppermute | solution.py:580
  99.3 2.2 %collective-permute-done.28.rest_1_ = bf16[256,256]{1,0:T(8,128)(2,1)S(1)} collective-permute-done((bf16[256,256]{1,0:T(8,128)(2,1)S(1)}, bf16[256,256]{1,0:T(8,128)(2,1)S(1)}, u32[]{:S(2)}, u32[]{:S(2)}) %collective-permute-start.28) | collective-permute-done | bytes 131104 | tf_op jit(solution)/shard_map/ppermute | solution.py:580
  101.4 1.2 %collective-permute-done.29.rest_2_ = bf16[256,256]{1,0:T(8,128)(2,1)S(1)} collective-permute-done((bf16[256,256]{1,0:T(8,128)(2,1)S(1)}, bf16[256,256]{1,0:T(8,128)(2,1)S(1)}, u32[]{:S(2)}, u32[]{:S(2)}) %collective-permute-start.29) | collective-permute-done | bytes 131104 | tf_op jit(solution)/shard_map/ppermute | solution.py:580
  102.7 2.0 %collective-permute-done.30.rest_3_ = bf16[256,256]{1,0:T(8,128)(2,1)S(1)} collective-permute-done((bf16[256,256]{1,0:T(8,128)(2,1)S(1)}, bf16[256,256]{1,0:T(8,128)(2,1)S(1)}, u32[]{:S(2)}, u32[]{:S(2)}) %collective-permute-start.30) | collective-permute-done | bytes 131104 | tf_op jit(solution)/shard_map/ppermute | solution.py:580
  104.7 0.6 shard_map.153
  105.4 0.4 shard_map.154
  105.8 1.5 %collective-permute-done.31.other_ref = bf16[1024,256]{1,0:T(8,128)(2,1)S(1)} collective-permute-done((bf16[1024,256]{1,0:T(8,128)(2,1)S(1)}, bf16[1024,256]{1,0:T(8,128)(2,1)S(1)}, u32[]{:S(2)}, u32[]{:S(2)}) %collective-permute-start.31) | collective-permute-done | bytes 524320 | tf_op jit(solution)/shard_map/ppermute | solution.py:580
  107.3 1.4 %shard_map.155 = (f32[128,2048]{1,0:T(8,128)}, f32[128,256]{1,0:T(8,128)}) custom-call(s32[1]{0:T(128)} %bitcast.me_ref, f32[128,2048]{1,0:T(8,128)S(1)} %get-tuple-element.119.value_ref, f32[128,256]{1,0:T(8,128)S(1)} %get-tuple-element.120.write_part_ref, f32[128,1024]{1,0:T(8,128)S(1)} %get-tuple-element.135.half_ref, ...), custom_call_target="tpu_custom_call" | custom-call | flops 134217728 | bytes 5177348 | tf_op jit(solution)/shard_map/pallas_call | solution.py:45
  (44 shorter events, 0.5 us)
Async XLA Ops:
  1.4 10.0 %collective-permute-start.2 = (bf16[128,256]{1,0:T(8,128)(2,1)S(1)}, bf16[128,256]{1,0:T(8,128)(2,1)S(1)}, u32[]{:S(2)}, u32[]{:S(2)}) collective-permute-start(bf16[128,256]{1,0:T(8,128)(2,1)S(1)} %pad_add_fusion.refs_0_), channel_id=1, source_target_pairs={{0,12},{1,13},{2,14},{3,15},{4,8},{5,9},{6,10},{7,11},{8,4},{9,5},... | collective-permute-start | bytes 196616 | tf_op jit(solution)/shard_map/ppermute | solution.py:580
  6.5 5.6 %collective-permute-start.1 = (bf16[128,256]{1,0:T(8,128)(2,1)S(1)}, bf16[128,256]{1,0:T(8,128)(2,1)S(1)}, u32[]{:S(2)}, u32[]{:S(2)}) collective-permute-start(bf16[128,256]{1,0:T(8,128)(2,1)S(1)} %pad_add_fusion.refs_0_), channel_id=1, source_target_pairs={{0,8},{1,9},{2,10},{3,11},{4,12},{5,13},{6,14},{7,15},{8,0},{9,1},... | collective-permute-start | bytes 196616 | tf_op jit(solution)/shard_map/ppermute | solution.py:580
  6.5 5.6 %collective-permute-start = (bf16[128,256]{1,0:T(8,128)(2,1)S(1)}, bf16[128,256]{1,0:T(8,128)(2,1)S(1)}, u32[]{:S(2)}, u32[]{:S(2)}) collective-permute-start(bf16[128,256]{1,0:T(8,128)(2,1)S(1)} %pad_add_fusion.refs_0_), channel_id=1, source_target_pairs={{0,4},{1,5},{2,6},{3,7},{4,0},{5,1},{6,2},{7,3},{8,12},{9,13},{10,... | collective-permute-start | bytes 196616 | tf_op jit(solution)/shard_map/ppermute | solution.py:580
  7.2 1.0 copy-start
  8.2 0.8 copy-start.2
  9.1 0.7 copy-start.8
  12.2 2.0 %collective-permute-start.3 = (bf16[1040,256]{1,0:T(8,128)(2,1)S(1)}, bf16[1040,256]{1,0:T(8,128)(2,1)S(1)}, u32[]{:S(2)}, u32[]{:S(2)}) collective-permute-start(bf16[1040,256]{1,0:T(8,128)(2,1)S(1)} %get-tuple-element.79), channel_id=1, source_target_pairs={{0,1},{1,0},{2,3},{3,2},{4,5},{5,4},{6,7},{7,6},{8,9},{9,8},{10,11... | collective-permute-start | bytes 1597448 | tf_op jit(solution)/shard_map/ppermute | solution.py:580
  12.2 10.1 %collective-permute-start.9 = (bf16[4,128,256]{2,1,0:T(8,128)(2,1)S(1)}, bf16[4,128,256]{2,1,0:T(8,128)(2,1)S(1)}, u32[]{:S(2)}, u32[]{:S(2)}) collective-permute-start(bf16[4,128,256]{2,1,0:T(8,128)(2,1)S(1)} %shard_map.139.rest_0_), channel_id=1, source_target_pairs={{0,2},{1,3},{2,0},{3,1},{4,6},{5,7},{6,4},{7,5},{8,10},{9,11},{10,... | collective-permute-start | bytes 786440 | tf_op jit(solution)/shard_map/ppermute | solution.py:580
  14.7 12.3 %collective-permute-start.4 = (bf16[272,256]{1,0:T(8,128)(2,1)S(1)}, bf16[272,256]{1,0:T(8,128)(2,1)S(1)}, u32[]{:S(2)}, u32[]{:S(2)}) collective-permute-start(bf16[272,256]{1,0:T(8,128)(2,1)S(1)} %get-tuple-element.81), channel_id=1, source_target_pairs={{0,2},{1,3},{2,0},{3,1},{4,6},{5,7},{6,4},{7,5},{8,10},{9,11},{10,... | collective-permute-start | bytes 417800 | tf_op jit(solution)/shard_map/ppermute | solution.py:580
  16.2 10.7 %collective-permute-start.5 = (bf16[272,256]{1,0:T(8,128)(2,1)S(1)}, bf16[272,256]{1,0:T(8,128)(2,1)S(1)}, u32[]{:S(2)}, u32[]{:S(2)}) collective-permute-start(bf16[272,256]{1,0:T(8,128)(2,1)S(1)} %get-tuple-element.82), channel_id=1, source_target_pairs={{0,4},{1,5},{2,6},{3,7},{4,0},{5,1},{6,2},{7,3},{8,12},{9,13},{10,... | collective-permute-start | bytes 417800 | tf_op jit(solution)/shard_map/ppermute | solution.py:580
  17.3 9.6 %collective-permute-start.6 = (bf16[272,256]{1,0:T(8,128)(2,1)S(1)}, bf16[272,256]{1,0:T(8,128)(2,1)S(1)}, u32[]{:S(2)}, u32[]{:S(2)}) collective-permute-start(bf16[272,256]{1,0:T(8,128)(2,1)S(1)} %get-tuple-element.83), channel_id=1, source_target_pairs={{0,6},{1,7},{2,4},{3,5},{4,2},{5,3},{6,0},{7,1},{8,14},{9,15},{10,... | collective-permute-start | bytes 417800 | tf_op jit(solution)/shard_map/ppermute | solution.py:580
  18.2 0.9 copy-start.6
  19.2 0.9 copy-start.7
  20.2 10.7 %collective-permute-start.8 = (bf16[4,128,256]{2,1,0:T(8,128)(2,1)S(1)}, bf16[4,128,256]{2,1,0:T(8,128)(2,1)S(1)}, u32[]{:S(2)}, u32[]{:S(2)}) collective-permute-start(bf16[4,128,256]{2,1,0:T(8,128)(2,1)S(1)} %shard_map.139.rest_0_), channel_id=1, source_target_pairs={{0,1},{1,0},{2,3},{3,2},{4,5},{5,4},{6,7},{7,6},{8,9},{9,8},{10,11... | collective-permute-start | bytes 786440 | tf_op jit(solution)/shard_map/ppermute | solution.py:580
  26.9 4.0 %collective-permute-start.10 = (bf16[4,128,256]{2,1,0:T(8,128)(2,1)S(1)}, bf16[4,128,256]{2,1,0:T(8,128)(2,1)S(1)}, u32[]{:S(2)}, u32[]{:S(2)}) collective-permute-start(bf16[4,128,256]{2,1,0:T(8,128)(2,1)S(1)} %collective-permute-done.9.rest_2_), channel_id=1, source_target_pairs={{0,1},{1,0},{2,3},{3,2},{4,5},{5,4},{6,7},{7,6},{8,9},{9,8},{10,11... | collective-permute-start | bytes 786440 | tf_op jit(solution)/shard_map/ppermute | solution.py:580
  27.2 8.9 %collective-permute-start.7 = (bf16[256,256]{1,0:T(8,128)(2,1)S(1)}, bf16[256,256]{1,0:T(8,128)(2,1)S(1)}, u32[]{:S(2)}, u32[]{:S(2)}) collective-permute-start(bf16[256,256]{1,0:T(8,128)(2,1)S(1)} %shard_map.141), channel_id=1, source_target_pairs={{0,8},{1,9},{2,10},{3,11},{4,12},{5,13},{6,14},{7,15},{16,24},{17,... | collective-permute-start | bytes 393224 | tf_op jit(solution)/shard_map/ppermute | solution.py:628
  30.9 39.2 %slice-start = ((s8[5242880]{0:T(1024)(128)(4,1)}), s8[4194304]{0:T(1024)(128)(4,1)S(1)}, s32[]{:S(2)}) async-start(s8[5242880]{0:T(1024)(128)(4,1)} %bitcast.3), calls=%async_computation | async-start | bytes 8388608
  30.9 31.4 %copy-start.1 = (bf16[128,2048]{1,0:T(8,128)(2,1)S(1)}, bf16[128,2048]{1,0:T(8,128)(2,1)}, u32[]{:S(2)}) copy-start(bf16[128,2048]{1,0:T(8,128)(2,1)} %input_ref.5) | copy-start | bytes 1572868
  31.0 31.4 %copy-start.3 = (bf16[128,256]{1,0:T(8,128)(2,1)S(1)}, bf16[128,256]{1,0:T(8,128)(2,1)}, u32[]{:S(2)}) copy-start(bf16[128,256]{1,0:T(8,128)(2,1)} %write_ref.9) | copy-start | bytes 196612
  31.0 31.4 %copy-start.4 = (bf16[128,256]{1,0:T(8,128)(2,1)S(1)}, bf16[128,256]{1,0:T(8,128)(2,1)}, u32[]{:S(2)}) copy-start(bf16[128,256]{1,0:T(8,128)(2,1)} %read_ref.5) | copy-start | bytes 196612
  31.0 31.4 %copy-start.5 = (bf16[128,2048]{1,0:T(8,128)(2,1)S(1)}, bf16[128,2048]{1,0:T(8,128)(2,1)}, u32[]{:S(2)}) copy-start(bf16[128,2048]{1,0:T(8,128)(2,1)} %gate_ref.1) | copy-start | bytes 1572868
  31.0 39.2 %slice-start.1 = ((s8[5242880]{0:T(1024)(128)(4,1)}), s8[1048576]{0:T(1024)(128)(4,1)S(1)}, s32[]{:S(2)}) async-start(s8[5242880]{0:T(1024)(128)(4,1)} %bitcast.3), calls=%async_computation.1 | async-start | bytes 2097152
  36.0 34.1 %copy-start.9 = (f32[2048]{0:T(1024)S(1)}, f32[2048]{0:T(1024)}, u32[]{:S(2)}) copy-start(f32[2048]{0:T(1024)} %param.20) | copy-start | bytes 24580
  36.1 4.3 %collective-permute-start.14 = (bf16[8,160,256]{2,1,0:T(8,128)(2,1)S(1)}, bf16[8,160,256]{2,1,0:T(8,128)(2,1)S(1)}, u32[]{:S(2)}, u32[]{:S(2)}) collective-permute-start(bf16[8,160,256]{2,1,0:T(8,128)(2,1)S(1)} %get-tuple-element.96), channel_id=1, source_target_pairs={{0,1},{1,0},{2,3},{3,2},{4,5},{5,4},{6,7},{7,6},{8,9},{9,8},{10,11... | collective-permute-start | bytes 1966088 | tf_op jit(solution)/shard_map/ppermute | solution.py:580
  36.6 8.7 %collective-permute-start.11 = (bf16[256,256]{1,0:T(8,128)(2,1)S(1)}, bf16[256,256]{1,0:T(8,128)(2,1)S(1)}, u32[]{:S(2)}, u32[]{:S(2)}) collective-permute-start(bf16[256,256]{1,0:T(8,128)(2,1)S(1)} %get-tuple-element.92), channel_id=1, source_target_pairs={{0,2},{1,3},{2,0},{3,1},{4,6},{5,7},{6,4},{7,5},{8,10},{9,11},{10,... | collective-permute-start | bytes 393224 | tf_op jit(solution)/shard_map/ppermute | solution.py:580
  38.2 7.1 %collective-permute-start.12 = (bf16[256,256]{1,0:T(8,128)(2,1)S(1)}, bf16[256,256]{1,0:T(8,128)(2,1)S(1)}, u32[]{:S(2)}, u32[]{:S(2)}) collective-permute-start(bf16[256,256]{1,0:T(8,128)(2,1)S(1)} %get-tuple-element.93), channel_id=1, source_target_pairs={{0,4},{1,5},{2,6},{3,7},{4,0},{5,1},{6,2},{7,3},{8,12},{9,13},{10,... | collective-permute-start | bytes 393224 | tf_op jit(solution)/shard_map/ppermute | solution.py:580
  40.4 6.7 %collective-permute-start.13 = (bf16[256,256]{1,0:T(8,128)(2,1)S(1)}, bf16[256,256]{1,0:T(8,128)(2,1)S(1)}, u32[]{:S(2)}, u32[]{:S(2)}) collective-permute-start(bf16[256,256]{1,0:T(8,128)(2,1)S(1)} %get-tuple-element.94), channel_id=1, source_target_pairs={{0,6},{1,7},{2,4},{3,5},{4,2},{5,3},{6,0},{7,1},{8,14},{9,15},{10,... | collective-permute-start | bytes 393224 | tf_op jit(solution)/shard_map/ppermute | solution.py:580
  40.5 12.0 %collective-permute-start.15 = (bf16[192,256]{1,0:T(8,128)(2,1)S(1)}, bf16[192,256]{1,0:T(8,128)(2,1)S(1)}, u32[]{:S(2)}, u32[]{:S(2)}) collective-permute-start(bf16[192,256]{1,0:T(8,128)(2,1)S(1)} %get-tuple-element.98), channel_id=1, source_target_pairs={{0,12},{1,13},{2,14},{3,15},{4,8},{5,9},{6,10},{7,11},{8,4},{9,5},... | collective-permute-start | bytes 294920 | tf_op jit(solution)/shard_map/ppermute | solution.py:580
  45.3 9.5 %collective-permute-start.16 = (bf16[192,256]{1,0:T(8,128)(2,1)S(1)}, bf16[192,256]{1,0:T(8,128)(2,1)S(1)}, u32[]{:S(2)}, u32[]{:S(2)}) collective-permute-start(bf16[192,256]{1,0:T(8,128)(2,1)S(1)} %get-tuple-element.99), channel_id=1, source_target_pairs={{0,8},{1,9},{2,10},{3,11},{4,12},{5,13},{6,14},{7,15},{8,0},{9,1},... | collective-permute-start | bytes 294920 | tf_op jit(solution)/shard_map/ppermute | solution.py:580
  55.4 6.0 %collective-permute-start.17 = (bf16[1024,256]{1,0:T(8,128)(2,1)S(1)}, bf16[1024,256]{1,0:T(8,128)(2,1)S(1)}, u32[]{:S(2)}, u32[]{:S(2)}) collective-permute-start(bf16[1024,256]{1,0:T(8,128)(2,1)S(1)} %get-tuple-element.105), channel_id=1, source_target_pairs={{0,1},{1,0},{2,3},{3,2},{4,5},{5,4},{6,7},{7,6},{8,9},{9,8},{10,11... | collective-permute-start | bytes 1572872 | tf_op jit(solution)/shard_map/ppermute | solution.py:580
  55.5 8.5 %collective-permute-start.18 = (bf16[192,256]{1,0:T(8,128)(2,1)S(1)}, bf16[192,256]{1,0:T(8,128)(2,1)S(1)}, u32[]{:S(2)}, u32[]{:S(2)}) collective-permute-start(bf16[192,256]{1,0:T(8,128)(2,1)S(1)} %get-tuple-element.109), channel_id=1, source_target_pairs={{0,14},{1,15},{2,12},{3,13},{4,10},{5,11},{6,8},{7,9},{8,6},{9,7},... | collective-permute-start | bytes 294920 | tf_op jit(solution)/shard_map/ppermute | solution.py:580
  57.4 10.4 %collective-permute-start.19 = (bf16[192,256]{1,0:T(8,128)(2,1)S(1)}, bf16[192,256]{1,0:T(8,128)(2,1)S(1)}, u32[]{:S(2)}, u32[]{:S(2)}) collective-permute-start(bf16[192,256]{1,0:T(8,128)(2,1)S(1)} %get-tuple-element.110), channel_id=1, source_target_pairs={{0,10},{1,11},{2,8},{3,9},{4,14},{5,15},{6,12},{7,13},{8,2},{9,3},... | collective-permute-start | bytes 294920 | tf_op jit(solution)/shard_map/ppermute | solution.py:580
  57.8 10.0 %collective-permute-start.20 = (bf16[192,256]{1,0:T(8,128)(2,1)S(1)}, bf16[192,256]{1,0:T(8,128)(2,1)S(1)}, u32[]{:S(2)}, u32[]{:S(2)}) collective-permute-start(bf16[192,256]{1,0:T(8,128)(2,1)S(1)} %get-tuple-element.111), channel_id=1, source_target_pairs={{0,4},{1,5},{2,6},{3,7},{4,0},{5,1},{6,2},{7,3},{8,12},{9,13},{10,... | collective-permute-start | bytes 294920 | tf_op jit(solution)/shard_map/ppermute | solution.py:580
  60.9 8.9 %collective-permute-start.21 = (bf16[192,256]{1,0:T(8,128)(2,1)S(1)}, bf16[192,256]{1,0:T(8,128)(2,1)S(1)}, u32[]{:S(2)}, u32[]{:S(2)}) collective-permute-start(bf16[192,256]{1,0:T(8,128)(2,1)S(1)} %get-tuple-element.113), channel_id=1, source_target_pairs={{0,6},{1,7},{2,4},{3,5},{4,2},{5,3},{6,0},{7,1},{8,14},{9,15},{10,... | collective-permute-start | bytes 294920 | tf_op jit(solution)/shard_map/ppermute | solution.py:580
  61.4 8.7 %collective-permute-start.22 = (bf16[192,256]{1,0:T(8,128)(2,1)S(1)}, bf16[192,256]{1,0:T(8,128)(2,1)S(1)}, u32[]{:S(2)}, u32[]{:S(2)}) collective-permute-start(bf16[192,256]{1,0:T(8,128)(2,1)S(1)} %get-tuple-element.114), channel_id=1, source_target_pairs={{0,2},{1,3},{2,0},{3,1},{4,6},{5,7},{6,4},{7,5},{8,10},{9,11},{10,... | collective-permute-start | bytes 294920 | tf_op jit(solution)/shard_map/ppermute | solution.py:580
  73.0 2.0 %collective-permute-start.23 = (bf16[1040,256]{1,0:T(8,128)(2,1)S(1)}, bf16[1040,256]{1,0:T(8,128)(2,1)S(1)}, u32[]{:S(2)}, u32[]{:S(2)}) collective-permute-start(bf16[1040,256]{1,0:T(8,128)(2,1)S(1)} %get-tuple-element.124), channel_id=1, source_target_pairs={{0,1},{1,0},{2,3},{3,2},{4,5},{5,4},{6,7},{7,6},{8,9},{9,8},{10,11... | collective-permute-start | bytes 1597448 | tf_op jit(solution)/shard_map/ppermute | solution.py:580
  75.5 5.8 %collective-permute-start.24 = (bf16[272,256]{1,0:T(8,128)(2,1)S(1)}, bf16[272,256]{1,0:T(8,128)(2,1)S(1)}, u32[]{:S(2)}, u32[]{:S(2)}) collective-permute-start(bf16[272,256]{1,0:T(8,128)(2,1)S(1)} %get-tuple-element.126), channel_id=1, source_target_pairs={{0,2},{1,3},{2,0},{3,1},{4,6},{5,7},{6,4},{7,5},{8,10},{9,11},{10,... | collective-permute-start | bytes 417800 | tf_op jit(solution)/shard_map/ppermute | solution.py:580
  76.5 6.6 %collective-permute-start.25 = (bf16[272,256]{1,0:T(8,128)(2,1)S(1)}, bf16[272,256]{1,0:T(8,128)(2,1)S(1)}, u32[]{:S(2)}, u32[]{:S(2)}) collective-permute-start(bf16[272,256]{1,0:T(8,128)(2,1)S(1)} %get-tuple-element.127), channel_id=1, source_target_pairs={{0,4},{1,5},{2,6},{3,7},{4,0},{5,1},{6,2},{7,3},{8,12},{9,13},{10,... | collective-permute-start | bytes 417800 | tf_op jit(solution)/shard_map/ppermute | solution.py:580
  76.9 8.5 %collective-permute-start.26 = (bf16[272,256]{1,0:T(8,128)(2,1)S(1)}, bf16[272,256]{1,0:T(8,128)(2,1)S(1)}, u32[]{:S(2)}, u32[]{:S(2)}) collective-permute-start(bf16[272,256]{1,0:T(8,128)(2,1)S(1)} %get-tuple-element.128), channel_id=1, source_target_pairs={{0,6},{1,7},{2,4},{3,5},{4,2},{5,3},{6,0},{7,1},{8,14},{9,15},{10,... | collective-permute-start | bytes 417800 | tf_op jit(solution)/shard_map/ppermute | solution.py:580
  85.7 9.7 %collective-permute-start.27 = (bf16[256,256]{1,0:T(8,128)(2,1)S(1)}, bf16[256,256]{1,0:T(8,128)(2,1)S(1)}, u32[]{:S(2)}, u32[]{:S(2)}) collective-permute-start(bf16[256,256]{1,0:T(8,128)(2,1)S(1)} %shard_map.151), channel_id=1, source_target_pairs={{8,0},{9,1},{10,2},{11,3},{12,4},{13,5},{14,6},{15,7},{24,16},{25,... | collective-permute-start | bytes 393224 | tf_op jit(solution)/shard_map/ppermute | solution.py:628
  95.7 5.7 %collective-permute-start.28 = (bf16[256,256]{1,0:T(8,128)(2,1)S(1)}, bf16[256,256]{1,0:T(8,128)(2,1)S(1)}, u32[]{:S(2)}, u32[]{:S(2)}) collective-permute-start(bf16[256,256]{1,0:T(8,128)(2,1)S(1)} %get-tuple-element.131), channel_id=1, source_target_pairs={{0,2},{1,3},{2,0},{3,1},{4,6},{5,7},{6,4},{7,5},{8,10},{9,11},{10,... | collective-permute-start | bytes 393224 | tf_op jit(solution)/shard_map/ppermute | solution.py:580
  96.8 5.9 %collective-permute-start.29 = (bf16[256,256]{1,0:T(8,128)(2,1)S(1)}, bf16[256,256]{1,0:T(8,128)(2,1)S(1)}, u32[]{:S(2)}, u32[]{:S(2)}) collective-permute-start(bf16[256,256]{1,0:T(8,128)(2,1)S(1)} %get-tuple-element.132), channel_id=1, source_target_pairs={{0,4},{1,5},{2,6},{3,7},{4,0},{5,1},{6,2},{7,3},{8,12},{9,13},{10,... | collective-permute-start | bytes 393224 | tf_op jit(solution)/shard_map/ppermute | solution.py:580
  96.8 7.9 %collective-permute-start.30 = (bf16[256,256]{1,0:T(8,128)(2,1)S(1)}, bf16[256,256]{1,0:T(8,128)(2,1)S(1)}, u32[]{:S(2)}, u32[]{:S(2)}) collective-permute-start(bf16[256,256]{1,0:T(8,128)(2,1)S(1)} %get-tuple-element.133), channel_id=1, source_target_pairs={{0,6},{1,7},{2,4},{3,5},{4,2},{5,3},{6,0},{7,1},{8,14},{9,15},{10,... | collective-permute-start | bytes 393224 | tf_op jit(solution)/shard_map/ppermute | solution.py:580
  105.3 2.0 %collective-permute-start.31 = (bf16[1024,256]{1,0:T(8,128)(2,1)S(1)}, bf16[1024,256]{1,0:T(8,128)(2,1)S(1)}, u32[]{:S(2)}, u32[]{:S(2)}) collective-permute-start(bf16[1024,256]{1,0:T(8,128)(2,1)S(1)} %get-tuple-element.137), channel_id=1, source_target_pairs={{0,1},{1,0},{2,3},{3,2},{4,5},{5,4},{6,7},{7,6},{8,9},{9,8},{10,11... | collective-permute-start | bytes 1572872 | tf_op jit(solution)/shard_map/ppermute | solution.py:580
